TPU v7x, 32 devices: a whole 2x2x4 slice. The times are simulated.
32 devices in a mesh: pipe: 2 (over y), ctx: 4 (over x, core), tp: 4 (over z).
Axes of the slice: x: 2, y: 2, z: 4, core: 2. Of those that a mesh axis runs over, the one named last changes fastest.
Arguments:
- block_input: bfloat16 [3, 1024, 2048], P(None, ('ctx', 'tp')), may hold values from -6 to 6
- out_grad: bfloat16 [3, 1024, 2048], P(None, ('ctx', 'tp')), may hold values from -6 to 6
- triple_weight: bfloat16 [2, 2048, 8, 3, 256], P('pipe', 'ctx', 'tp'), may hold values from -0.125 to 0.125
- output_weight: bfloat16 [2, 8, 256, 2048], P('pipe', 'tp', None, 'ctx'), may hold values from -0.75 to 0.75
- expand_weight: bfloat16 [2, 2048, 8192], P('pipe', 'ctx', 'tp'), may hold values from -0.125 to 0.125
- contract_weight: bfloat16 [2, 8192, 2048], P('pipe', 'tp', 'ctx'), may hold values from -0.0625 to 0.0625
- norm_gains: bfloat16 [2, 2, 2048], P('pipe', None, 'ctx'), may hold values from 0.5 to 1.5
- norm_biases: bfloat16 [2, 2, 2048], P('pipe', None, 'ctx'), may hold values from -3 to 3
Outputs:
- layer_outputs: bfloat16 [2, 3, 1024, 2048], P('pipe', None, ('ctx', 'tp'))
- entry_grads: bfloat16 [2, 3, 1024, 2048], P('pipe', None, ('ctx', 'tp'))
- triple_grads: float32 [2, 2048, 8, 3, 256], P('pipe', 'ctx', 'tp')
- output_grads: float32 [2, 8, 256, 2048], P('pipe', 'tp', None, 'ctx')
- expand_grads: float32 [2, 2048, 8192], P('pipe', 'ctx', 'tp')
- contract_grads: float32 [2, 8192, 2048], P('pipe', 'tp', 'ctx')
- gain_grads: float32 [2, 2, 2048], P('pipe', None, 'ctx')
- bias_grads: float32 [2, 2, 2048], P('pipe', None, 'ctx')
All inputs are finite; a program needn't handle non-finite values.
Results may differ from a plain program's by a relative error of at most 0.029.
Values may be sent and summed in bfloat16 or wider, within the bound.
No kernel may reach another device: no remote copies, remote signals or barrier semaphores. Data moves between devices by JAX's collectives and lax.ppermute only.
A program may use at most 320 MiB of HBM per device.

v0:
```python
import functools
import math
from types import SimpleNamespace

import jax
import jax.numpy as jnp
from jax import lax
from jax.experimental import pallas as pl
from jax.experimental.pallas import tpu as pltpu
from jax.sharding import PartitionSpec as P

ROT = 64
LANES = 128
epsilon = 1e-05
masked_score = -1e30
f32 = jnp.float32
bf16 = jnp.bfloat16
mebibyte = 1024 * 1024
half_root = 0.7071067811865476
bell = 0.3989422804014327


def dot(a, b, dims):
    return lax.dot_general(a, b, (dims, ((), ())), preferred_element_type=f32)


def plain(a, b):
    return dot(a, b, ((1,), (0,)))


def turned(a, b):
    return dot(a, b, ((1,), (1,)))


def doubling(count):
    order, step = [0], count // 2
    while step:
        order += [k ^ step for k in order]
        step //= 2
    return order


def xor_blocks(values, index, count, inverse=False):
    width = values.shape[-1] // count
    order = doubling(count)

    def taken(places):
        return jnp.concatenate(
            [values[..., k * width : (k + 1) * width] for k in places], axis=-1
        )

    if inverse:
        values = taken([order.index(k) for k in range(count)])
    step = 1
    while step < count:
        swapped = taken([k ^ step for k in range(count)])
        values = jnp.where((index & step) != 0, swapped, values)
        step *= 2
    return values if inverse else taken(order)


def rope_tables(positions):
    half = ROT // 2
    frequency = 10000.0 ** (-jnp.arange(0, ROT, 2, dtype=f32) / ROT)
    angles = positions.astype(f32)[:, None] * frequency[None, :]
    cosine, sine = jnp.cos(angles), jnp.sin(angles)
    count = positions.shape[0]
    rest = jnp.zeros((count, LANES - ROT), f32)
    none = jnp.zeros((count, half), f32)
    return jnp.stack(
        [
            jnp.concatenate([cosine, cosine, rest + 1.0], axis=1),
            jnp.concatenate([-sine, none, rest], axis=1),
            jnp.concatenate([none, sine, rest], axis=1),
        ]
    )


def turn(values, tables, sign):
    half = ROT // 2
    part = values[:, :LANES]
    moved = (
        pltpu.roll(part, LANES - half, 1) * tables[1] + pltpu.roll(part, half, 1) * tables[2]
    )
    part = part * tables[0] + (moved if sign > 0 else -moved)
    return jnp.concatenate([part, values[:, LANES:]], axis=1)


def normalize(values):
    center = values - jnp.mean(values, axis=-1, keepdims=True)
    inverse = lax.rsqrt(jnp.mean(center * center, axis=-1, keepdims=True) + epsilon)
    return (center * inverse, inverse)


def whole(array):
    zeros = (0,) * array.ndim
    return pl.BlockSpec(array.shape, lambda *_: zeros)


def at(block, place):
    return pl.BlockSpec(block, lambda *_: place)


kept_out = pl.BlockSpec(memory_space=pl.ANY)


def shape(dims, dtype=bf16):
    return jax.ShapeDtypeStruct(dims, dtype)


class Order:
    def __init__(self):
        self.last = []

    def follow(self, results):
        self.last = [min(results, key=lambda array: array.size * array.dtype.itemsize)]

    def also(self, array):
        self.last = self.last + [array]


took = dict(
    project=7,
    expand=8,
    attend=5,
    branch=8,
    hidden_both=14,
    attend_both=11,
    attend_back=8,
    hidden_back=13,
    project_back=8,
    weight_sums=16,
    fold=7,
)
peak = 1.15e9


def run(order, flags, kernel, ins, outs, scratch, name, grid=(1,), work=0):
    taken = len(ins)
    ins = [(flags, pl.BlockSpec(memory_space=pltpu.SMEM))] + list(ins)
    ins += [(array, kept_out) for array in order.last]
    arrays = [array for array, _ in ins]
    once = grid == (1,)

    def sized(spec, dtype):
        if spec.block_shape is None:
            return spec, 0
        size = math.prod(spec.block_shape) * jnp.dtype(dtype).itemsize
        if not once:
            return spec, 2 * size
        single = pl.BlockSpec(
            spec.block_shape, spec.index_map, pipeline_mode=pl.Buffered(1)
        )
        return single, size

    in_specs = [sized(spec, array.dtype) for array, spec in ins]
    out_specs = [sized(spec, struct.dtype) for struct, spec in outs]
    held = sum(size for _, size in in_specs + out_specs)
    for buffer in scratch:
        if buffer.memory_space == pltpu.VMEM:
            held += math.prod(buffer.shape) * jnp.dtype(buffer.dtype).itemsize

    def body(flag_ref, *refs):
        @pl.when(flag_ref[0] == 1)
        def _():
            kernel(flag_ref, *refs[:taken], *refs[len(ins) - 1 :])

    results = pl.pallas_call(
        body,
        grid=grid,
        in_specs=[spec for spec, _ in in_specs],
        out_specs=[spec for spec, _ in out_specs],
        out_shape=[struct for struct, _ in outs],
        scratch_shapes=scratch,
        compiler_params=pltpu.CompilerParams(
            vmem_limit_bytes=int(held + (work + 4) * mebibyte)
        ),
        cost_estimate=pl.CostEstimate(
            flops=int(took[name] * peak), bytes_accessed=0, transcendentals=0
        ),
        name=name,
    )(*arrays)
    order.follow(results)
    return results


def fence(through, waits):
    count = len(through)

    def kernel(*refs):
        pass

    return pl.pallas_call(
        kernel,
        in_specs=[kept_out] * (count + len(waits)),
        out_specs=[kept_out] * count,
        out_shape=[shape(array.shape, array.dtype) for array in through],
        input_output_aliases={j: j for j in range(count)},
        compiler_params=pltpu.CompilerParams(vmem_limit_bytes=mebibyte),
        cost_estimate=pl.CostEstimate(flops=1, bytes_accessed=1, transcendentals=0),
        name="fence",
    )(*through, *waits)


def full_out(dims, dtype=bf16):
    zeros = (0,) * len(dims)
    return (shape(dims, dtype), pl.BlockSpec(dims, lambda *_: zeros))


def copies(sources, targets, sems):
    started = []
    for source, target, sem in zip(sources, targets, sems):
        copy = pltpu.make_async_copy(source, target, sem)
        copy.start()
        started.append(copy)
    return started


def project(order, flags, pieces, at_piece, gains, biases, tables, weights, heads, head_dim):
    count, width = 1, pieces[0].shape[2]
    span_rows = sum(piece.shape[1] for piece in pieces)
    rows = count * span_rows
    chunk = pieces[0].shape[1]
    spans = len(weights)
    depth = width // spans
    wide = 3 * head_dim
    columns = heads * wide

    def kernel(flag_ref, *refs):
        piece_refs = refs[: len(pieces)]
        gain_ref, bias_ref, table_ref = refs[len(pieces) : len(pieces) + 3]
        weight_refs = refs[len(pieces) + 3 : len(pieces) + 3 + spans]
        first, second, normal, queries, pair, held, sems = refs[len(pieces) + 3 + spans :]
        started = []
        for h in range(heads):
            started.append(
                copies(
                    [w.at[:depth, h * wide : (h + 1) * wide] for w in weight_refs],
                    [held.at[h, k * depth : (k + 1) * depth] for k in range(spans)],
                    [sems.at[h, k] for k in range(spans)],
                )
            )
        start = 0
        for piece_ref in piece_refs:
            chunks = piece_ref.shape[1] // chunk

            def one(i, _, piece_ref=piece_ref, start=start, chunks=chunks):
                m, c = i // chunks, i % chunks
                values = piece_ref[m, pl.ds(pl.multiple_of(c * chunk, chunk), chunk), :]
                normed, _ = normalize(values.astype(f32))
                to = pl.ds(
                    pl.multiple_of(m * span_rows + start + c * chunk, chunk), chunk
                )
                normal[to, :] = normed.astype(bf16)
                first[to, :] = (normed * gain_ref[0:1] + bias_ref[0:1]).astype(bf16)
                second[to, :] = (normed * gain_ref[1:2] + bias_ref[1:2]).astype(bf16)
                return 0

            lax.fori_loop(0, count * chunks, one, 0)
            start += piece_ref.shape[1]
        for h in range(heads):
            for copy in started[h]:
                copy.wait()

            def two(m, _, h=h):
                to = pl.ds(pl.multiple_of(m * span_rows, span_rows), span_rows)
                made = plain(first[to, :], held[h])
                queries[h, to, :] = turn(made[:, :head_dim], table_ref, 1).astype(bf16)
                pair[0, h, to, :] = turn(
                    made[:, head_dim : 2 * head_dim], table_ref, 1
                ).astype(bf16)
                pair[1, h, to, :] = made[:, 2 * head_dim :].astype(bf16)
                return 0

            lax.fori_loop(0, count, two, 0)

    ins = [(piece, at((1,) + piece.shape[1:], (at_piece, 0, 0))) for piece in pieces]
    ins += [(array, whole(array)) for array in (gains, biases, tables)]
    ins += [(w, kept_out) for w in weights]
    outs = [full_out((rows, width))] * 3 + [
        full_out((heads, rows, head_dim)),
        full_out((2, heads, rows, head_dim)),
    ]
    scratch = [
        pltpu.VMEM((heads, width, wide), bf16),
        pltpu.SemaphoreType.DMA((heads, spans)),
    ]
    return run(order, flags, kernel, ins, outs, scratch, "project")


def expand_up(order, flags, second, weights, span_rows):
    rows, width = second.shape
    depth, hidden = weights[0].shape
    spans = len(weights)
    tile = min(512, hidden)
    tiles = hidden // tile

    def kernel(flag_ref, *refs):
        second_ref, weight_refs = refs[0], refs[1 : 1 + spans]
        active, slope, held, sems = refs[1 + spans :]
        started = []
        for t in range(tiles):
            started.append(
                copies(
                    [w.at[:, t * tile : (t + 1) * tile] for w in weight_refs],
                    [held.at[t, k * depth : (k + 1) * depth] for k in range(spans)],
                    [sems.at[t, k] for k in range(spans)],
                )
            )
        for t in range(tiles):
            for copy in started[t]:
                copy.wait()

            def one(m, _, t=t):
                to = pl.ds(pl.multiple_of(m * span_rows, span_rows), span_rows)
                pre = plain(second_ref[to, :], held[t])
                risen = 0.5 * (1.0 + lax.erf(pre * half_root))
                columns = slice(t * tile, (t + 1) * tile)
                active[to, columns] = (pre * risen).astype(bf16)
                slope[to, columns] = (
                    risen + pre * jnp.exp(-0.5 * pre * pre) * bell
                ).astype(bf16)
                return 0

            lax.fori_loop(0, rows // span_rows, one, 0)

    ins = [(second, whole(second))] + [(w, kept_out) for w in weights]
    outs = [full_out((rows, hidden))] * 2
    scratch = [
        pltpu.VMEM((tiles, width, tile), bf16),
        pltpu.SemaphoreType.DMA((tiles, spans)),
    ]
    return run(order, flags, kernel, ins, outs, scratch, "expand")


def spread(refs):
    return [ref.at[j] for ref in refs for j in range(ref.shape[0])]


def attention(here, pairs, head, row_ref, key_ref, scale):
    scores = []
    for k, pair in enumerate(pairs):
        raw = turned(here, pair[0, head]) * scale
        scores.append(jnp.where(key_ref[k] <= row_ref[...], raw, masked_score))
    top = functools.reduce(
        jnp.maximum, [jnp.max(part, axis=1, keepdims=True) for part in scores]
    )
    scores = [jnp.exp(part - top) for part in scores]
    inverse = 1.0 / sum(jnp.sum(part, axis=1, keepdims=True) for part in scores)
    return [part * inverse for part in scores]


def attend(order, flags, queries, pairs, positions, key_positions, scale):
    heads, rows, head_dim = queries.shape
    spans = sum(pair.shape[0] for pair in pairs)

    def kernel(flag_ref, query_ref, *refs):
        views, refs = spread(refs[: len(pairs)]), refs[len(pairs) :]
        row_ref, key_ref, attended, probs = refs
        for h in range(heads):
            parts = attention(query_ref[h], views, h, row_ref, key_ref, scale)
            summed = None
            for k in range(spans):
                part = parts[k].astype(bf16)
                probs[k, h] = part
                term = plain(part, views[k][1, h])
                summed = term if summed is None else summed + term
            attended[:, h * head_dim : (h + 1) * head_dim] = summed.astype(bf16)

    ins = [
        (array, whole(array)) for array in (queries, *pairs, positions, key_positions)
    ]
    outs = [full_out((rows, heads * head_dim)), full_out((spans, heads, rows, rows))]
    work = spans * rows * rows * 4 * heads * 4 / mebibyte
    return run(order, flags, kernel, ins, outs, [], "attend", work=work)


def attention_grads(grad, here, parts, views, head, keep, send, scale):
    half = keep.shape[0]
    grad_probs = [turned(grad, view[1, head]) for view in views]
    delta = sum(
        jnp.sum(part.astype(f32) * slope, axis=1, keepdims=True)
        for part, slope in zip(parts, grad_probs)
    )
    query_grad = None
    for k, view in enumerate(views):
        slopes = (parts[k].astype(f32) * (grad_probs[k] - delta)).astype(bf16)
        term = plain(slopes, view[0, head])
        query_grad = term if query_grad is None else query_grad + term
        side = keep if k < half else send
        side[k % half, 0, head] = (dot(slopes, here, ((0,), (0,))) * scale).astype(bf16)
        side[k % half, 1, head] = dot(parts[k].astype(bf16), grad, ((0,), (0,))).astype(bf16)
    return query_grad * scale


def attend_both(
    order, flags, rows_in, packed, queries, pairs, positions, key_positions, tables, scale
):
    heads, rows, head_dim = queries.shape
    width = rows_in.shape[1]
    spans = len(packed)
    across, depth = heads * head_dim, width // spans
    half = spans // 2

    def kernel(flag_ref, rows_ref, *refs):
        packed_refs, refs = refs[:spans], refs[spans:]
        query_ref, refs = refs[0], refs[1:]
        views, refs = spread(refs[: len(pairs)]), refs[len(pairs) :]
        row_ref, key_ref, table_ref, attended, turned_back, keep, send, held, sems = refs
        started = copies(
            [w.at[:across, 3 * across : 3 * across + depth] for w in packed_refs],
            [held.at[:, k * depth : (k + 1) * depth] for k in range(spans)],
            [sems.at[k] for k in range(spans)],
        )
        all_parts = []
        for h in range(heads):
            parts = attention(query_ref[h], views, h, row_ref, key_ref, scale)
            summed = None
            for k in range(spans):
                term = plain(parts[k].astype(bf16), views[k][1, h])
                summed = term if summed is None else summed + term
            attended[:, h * head_dim : (h + 1) * head_dim] = summed.astype(bf16)
            all_parts.append(parts)
        for copy in started:
            copy.wait()
        grads = turned(rows_ref[...], held[...]).astype(bf16)
        for h in range(heads):
            made = attention_grads(
                grads[:, h * head_dim : (h + 1) * head_dim],
                query_ref[h],
                all_parts[h],
                views,
                h,
                keep,
                send,
                scale,
            )
            turned_back[h] = turn(made, table_ref, -1).astype(bf16)

    ins = [(rows_in, whole(rows_in))] + [(w, kept_out) for w in packed]
    ins += [
        (array, whole(array)) for array in (queries, *pairs, positions, key_positions, tables)
    ]
    outs = [full_out((rows, across)), full_out((heads, rows, head_dim))]
    outs += [full_out((half, 2, heads, rows, head_dim))] * 2
    scratch = [pltpu.VMEM((across, width), bf16), pltpu.SemaphoreType.DMA((spans,))]
    work = spans * rows * rows * 4 * (heads + 4) / mebibyte
    return run(order, flags, kernel, ins, outs, scratch, "attend_both", work=work)


def hidden_both(order, flags, second, pieces, at_piece, expand, contract, normal, gains):
    rows, width = second.shape
    hidden, depth = contract[0].shape
    spans = len(contract)
    tile = min(512, hidden)
    tiles = hidden // tile

    def kernel(flag_ref, second_ref, *refs):
        piece_refs, refs = refs[: len(pieces)], refs[len(pieces) :]
        expand_refs, refs = refs[:spans], refs[spans:]
        contract_refs, refs = refs[:spans], refs[spans:]
        normal_ref, gain_ref, rows_out, active, grads, part, side, *refs = refs
        held_up, held_down, sems_up, sems_down = refs
        started = []
        for t in range(tiles):
            block = slice(t * tile, (t + 1) * tile)
            places = [slice(k * depth, (k + 1) * depth) for k in range(spans)]
            up = copies(
                [w.at[:, block] for w in expand_refs],
                [held_up.at[place, block] for place in places],
                [sems_up.at[t, k] for k in range(spans)],
            )
            down = copies(
                [w.at[block, :] for w in contract_refs],
                [held_down.at[block, place] for place in places],
                [sems_down.at[t, k] for k in range(spans)],
            )
            started.append((up, down))
        start = 0
        for piece_ref in piece_refs:
            size = piece_ref.shape[1]
            rows_out[start : start + size, :] = piece_ref[0]
            start += size
        for t in range(tiles):
            block = slice(t * tile, (t + 1) * tile)
            for copy in started[t][0] + started[t][1]:
                copy.wait()
            pre = plain(second_ref[...], held_up[:, block])
            risen = 0.5 * (1.0 + lax.erf(pre * half_root))
            active[:, block] = (pre * risen).astype(bf16)
            slope = risen + pre * jnp.exp(-0.5 * pre * pre) * bell
            grads[:, block] = (turned(rows_out[...], held_down[block, :]) * slope).astype(bf16)
        for k in range(spans):
            place = slice(k * depth, (k + 1) * depth)
            made = turned(grads[...], held_up[place, :])
            side[0:1, place] = jnp.sum(
                made * normal_ref[:, place].astype(f32), axis=0, keepdims=True
            )
            side[1:2, place] = jnp.sum(made, axis=0, keepdims=True)
            part[:, place] = made * gain_ref[1:2, place]

    ins = [(second, whole(second))]
    ins += [(piece, at((1,) + piece.shape[1:], (at_piece, 0, 0))) for piece in pieces]
    ins += [(w, kept_out) for w in expand] + [(w, kept_out) for w in contract]
    ins += [(normal, whole(normal)), (gains, whole(gains))]
    outs = [
        full_out((rows, width)),
        full_out((rows, hidden)),
        full_out((rows, hidden)),
        full_out((rows, width), f32),
        full_out((2, width), f32),
    ]
    scratch = [
        pltpu.VMEM((width, hidden), bf16),
        pltpu.VMEM((hidden, width), bf16),
        pltpu.SemaphoreType.DMA((tiles, spans)),
        pltpu.SemaphoreType.DMA((tiles, spans)),
    ]
    return run(order, flags, kernel, ins, outs, scratch, "hidden_both")


def branch_out(order, flags, groups, contract, packed):
    hidden, depth = contract[0].shape
    across = groups[0][1].shape[1]
    spans = len(contract)
    width = depth * spans
    span_rows = groups[0][0].shape[0]
    block = span_rows // 2
    count = len(groups)

    def kernel(flag_ref, *refs):
        group_refs, refs = refs[: 2 * count], refs[2 * count :]
        contract_refs, packed_refs = refs[:spans], refs[spans : 2 * spans]
        blocks, refs = refs[2 * spans : 2 * (spans + count)], refs[2 * (spans + count) :]
        held, held_out, sems = refs
        outputs = [w.at[:across, 3 * across : 3 * across + depth] for w in packed_refs]
        started = copies(
            [ref for k in range(spans) for ref in (outputs[k], contract_refs[k])],
            [ref for k in range(spans) for ref in (held_out.at[k], held.at[k])],
            [sems.at[j] for j in range(2 * spans)],
        )
        for k in range(spans):
            started[2 * k].wait()
            started[2 * k + 1].wait()
            columns = slice(k * depth, (k + 1) * depth)
            for c in range(count):
                made = plain(group_refs[2 * c + 1][...], held_out[k])
                made = made + plain(group_refs[2 * c][...], held[k])
                blocks[2 * c][:, columns] = made[:block].astype(bf16)
                blocks[2 * c + 1][:, columns] = made[block:].astype(bf16)

    ins = []
    for active, attended in groups:
        ins += [(active, whole(active)), (attended, whole(attended))]
    ins += [(w, kept_out) for w in contract] + [(w, kept_out) for w in packed]
    outs = [full_out((block, width))] * (2 * count)
    scratch = [
        pltpu.VMEM((spans, hidden, depth), bf16),
        pltpu.VMEM((spans, across, depth), bf16),
        pltpu.SemaphoreType.DMA((2 * spans,)),
    ]
    return run(order, flags, kernel, ins, outs, scratch, "branch")


def attend_back(order, flags, pieces, packed, queries, pairs, probs, tables, scale):
    rows = sum(piece.shape[1] for piece in pieces)
    width = pieces[0].shape[2]
    heads, _, head_dim = queries.shape
    spans = len(packed)
    across, depth = heads * head_dim, width // spans
    half = spans // 2

    def kernel(flag_ref, *refs):
        piece_refs, refs = refs[: len(pieces)], refs[len(pieces) :]
        packed_refs, refs = refs[:spans], refs[spans:]
        query_ref, refs = refs[0], refs[1:]
        views, refs = spread(refs[: len(pairs)]), refs[len(pairs) :]
        prob_ref, table_ref, rows_out, turned_back, keep, send, held, sems = refs
        started = copies(
            [w.at[:across, 3 * across : 3 * across + depth] for w in packed_refs],
            [held.at[:, k * depth : (k + 1) * depth] for k in range(spans)],
            [sems.at[k] for k in range(spans)],
        )
        start = 0
        for piece_ref in piece_refs:
            size = piece_ref.shape[1]
            rows_out[start : start + size, :] = piece_ref[0]
            start += size
        for copy in started:
            copy.wait()
        grads = turned(rows_out[...], held[...]).astype(bf16)
        for h in range(heads):
            made = attention_grads(
                grads[:, h * head_dim : (h + 1) * head_dim],
                query_ref[h],
                [prob_ref[k, h] for k in range(spans)],
                views,
                h,
                keep,
                send,
                scale,
            )
            turned_back[h] = turn(made, table_ref, -1).astype(bf16)

    ins = [(piece, whole(piece)) for piece in pieces] + [(w, kept_out) for w in packed]
    ins += [(array, whole(array)) for array in (queries, *pairs, probs, tables)]
    outs = [full_out((rows, width)), full_out((heads, rows, head_dim))]
    outs += [full_out((half, 2, heads, rows, head_dim))] * 2
    scratch = [pltpu.VMEM((across, width), bf16), pltpu.SemaphoreType.DMA((spans,))]
    work = spans * rows * rows * 4 * 4 / mebibyte
    return run(order, flags, kernel, ins, outs, scratch, "attend_back", work=work)


def hidden_back(order, flags, upstream, contract, expand, slope, normal, gains):
    span_rows, width = upstream.shape
    hidden, depth = contract[0].shape
    spans = len(contract)
    tile = min(512, hidden)
    tiles = hidden // tile

    def kernel(flag_ref, *refs):
        upstream_ref, refs = refs[0], refs[1:]
        contract_refs, refs = refs[:spans], refs[spans:]
        expand_refs, refs = refs[:spans], refs[spans:]
        slope_ref, normal_ref, gain_ref, grads, part, side, held, held_up, sems, sems_up = refs
        started = [
            copies(
                [w.at[t * tile : (t + 1) * tile, :] for w in contract_refs],
                [held.at[t, :, k * depth : (k + 1) * depth] for k in range(spans)],
                [sems.at[t, k] for k in range(spans)],
            )
            for t in range(tiles)
        ]
        started_up = copies(
            expand_refs, [held_up.at[k] for k in range(spans)], [sems_up.at[k] for k in range(spans)]
        )
        for t in range(tiles):
            for copy in started[t]:
                copy.wait()
            columns = slice(t * tile, (t + 1) * tile)
            grads[:, columns] = (
                turned(upstream_ref[...], held[t]) * slope_ref[:, columns].astype(f32)
            ).astype(bf16)
        for k in range(spans):
            started_up[k].wait()
            made = turned(grads[...], held_up[k])
            columns = slice(k * depth, (k + 1) * depth)
            side[0:1, columns] = jnp.sum(
                made * normal_ref[:, columns].astype(f32), axis=0, keepdims=True
            )
            side[1:2, columns] = jnp.sum(made, axis=0, keepdims=True)
            part[:, columns] = made * gain_ref[1:2, columns]

    ins = [(upstream, whole(upstream))]
    ins += [(w, kept_out) for w in contract] + [(w, kept_out) for w in expand]
    ins += [
        (slope, whole(slope)),
        (normal, whole(normal)),
        (gains, whole(gains)),
    ]
    outs = [
        full_out((span_rows, hidden)),
        full_out((span_rows, width), f32),
        full_out((2, width), f32),
    ]
    scratch = [
        pltpu.VMEM((tiles, tile, width), bf16),
        pltpu.VMEM((spans, depth, hidden), bf16),
        pltpu.SemaphoreType.DMA((tiles, spans)),
        pltpu.SemaphoreType.DMA((spans,)),
    ]
    return run(order, flags, kernel, ins, outs, scratch, "hidden_back")


def project_back(
    order, flags, turned_back, own, came, weights, part, normal, gains, tables
):
    heads, span_rows, head_dim = turned_back.shape
    spans = len(weights)
    width = part.shape[1]
    depth, columns = width // spans, 3 * heads * head_dim
    block = span_rows // 2

    def kernel(flag_ref, *refs):
        query_ref, own_ref, came_ref, refs = refs[0], refs[1], refs[2], refs[3:]
        weight_refs, refs = refs[:spans], refs[spans:]
        part_ref, normal_ref, gain_ref, table_ref, grads, side, *refs = refs
        low, high, held, sems = refs
        started = copies(
            [w.at[:depth, :columns] for w in weight_refs],
            [held.at[k] for k in range(spans)],
            [sems.at[k] for k in range(spans)],
        )
        for h in range(heads):
            at_column = h * 3 * head_dim
            keys = own_ref[0, h].astype(f32) + came_ref[0, h].astype(f32)
            values = own_ref[1, h].astype(f32) + came_ref[1, h].astype(f32)
            grads[:, at_column : at_column + head_dim] = query_ref[h]
            grads[:, at_column + head_dim : at_column + 2 * head_dim] = turn(
                keys, table_ref, -1
            ).astype(bf16)
            grads[:, at_column + 2 * head_dim : at_column + 3 * head_dim] = values.astype(bf16)
        for k in range(spans):
            started[k].wait()
            made = turned(grads[...], held[k])
            span_columns = slice(k * depth, (k + 1) * depth)
            side[0:1, span_columns] = jnp.sum(
                made * normal_ref[:, span_columns].astype(f32), axis=0, keepdims=True
            )
            side[1:2, span_columns] = jnp.sum(made, axis=0, keepdims=True)
            both = (made * gain_ref[0:1, span_columns] + part_ref[:, span_columns]).astype(bf16)
            low[:, span_columns] = both[:block]
            high[:, span_columns] = both[block:]

    ins = [(array, whole(array)) for array in (turned_back, own, came)]
    ins += [(w, kept_out) for w in weights]
    ins += [(part, whole(part)), (normal, whole(normal))]
    ins += [(gains, whole(gains)), (tables, whole(tables))]
    outs = [full_out((span_rows, columns)), full_out((2, width), f32)]
    outs += [full_out((block, width))] * 2
    scratch = [pltpu.VMEM((spans, depth, columns), bf16), pltpu.SemaphoreType.DMA((spans,))]
    return run(order, flags, kernel, ins, outs, scratch, "project_back")


def weight_sums(order, flags, lefts, rights, by_rows, spans):
    rows = sum(piece.shape[0] for piece in lefts[0][0])
    left_width = sum(group[0].shape[1] for group in lefts[0])
    right_width = sum(group[0].shape[1] for group in rights[0])
    if by_rows:
        tile = left_width // spans
        steps, block = spans // 2, (tile, right_width)
    else:
        tile = min(512, left_width)
        while left_width % tile:
            tile //= 2
        steps, block = left_width // tile, (tile, right_width // 2)
    chunk = min(1024, block[1])
    while right_width % chunk:
        chunk //= 2
    pieces = [
        [piece for groups in (lefts[s], rights[s]) for group in groups for piece in group]
        for s in (0, 1)
    ]
    most = max(len(p) for p in pieces)

    def kernel(flag_ref, *refs):
        piece_refs = (refs[: len(pieces[0])], refs[len(pieces[0]) : len(pieces[0]) + len(pieces[1])])
        keep, send, left, right, flipped, sems = refs[len(pieces[0]) + len(pieces[1]) :]
        g = pl.program_id(0)
        for s in (0, 1):

            @pl.when((g == 0) & (flag_ref[2] == s))
            def _(s=s):
                targets = []
                for held, groups in ((left, lefts[s]), (right, rights[s])):
                    column = 0
                    for group in groups:
                        row, wide = 0, group[0].shape[1]
                        for piece in group:
                            targets.append(
                                held.at[row : row + piece.shape[0], column : column + wide]
                            )
                            row += piece.shape[0]
                        column += wide
                started = copies(
                    piece_refs[s], targets, [sems.at[j] for j in range(len(targets))]
                )
                for copy in started:
                    copy.wait()

        def product(column, store):
            flipped[...] = left[:, pl.ds(pl.multiple_of(column, LANES), tile)].T

            def one(c, _):
                columns = pl.ds(pl.multiple_of(c * chunk, chunk), chunk)
                store(c, plain(flipped[...], right[:, columns]).astype(bf16))
                return 0

            lax.fori_loop(0, right_width // chunk, one, 0)

        if by_rows:

            def to(target):
                def store(c, made):
                    target[:, pl.ds(pl.multiple_of(c * chunk, chunk), chunk)] = made

                return store

            product(g * tile, to(keep))
            product((g + steps) * tile, to(send))
        else:
            half = right_width // 2 // chunk

            def store(c, made):
                @pl.when(c < half)
                def _():
                    keep[:, pl.ds(pl.multiple_of(c * chunk, chunk), chunk)] = made

                @pl.when(c >= half)
                def _():
                    send[:, pl.ds(pl.multiple_of((c - half) * chunk, chunk), chunk)] = made

            product(g * tile, store)

    ins = [(piece, kept_out) for s in (0, 1) for piece in pieces[s]]
    dims = (steps * tile, block[1])
    outs = [(shape(dims), pl.BlockSpec(block, lambda g: (g, 0)))] * 2
    scratch = [
        pltpu.VMEM((rows, left_width), bf16),
        pltpu.VMEM((rows, right_width), bf16),
        pltpu.VMEM((tile, rows), bf16),
        pltpu.SemaphoreType.DMA((most,)),
    ]
    return run(
        order, flags, kernel, ins, outs, scratch, "weight_sums", grid=(steps,)
    )


def fold(order, flags, keep, came, dim):
    rows, columns = keep.shape
    if dim == 0:
        tile = rows // 4
        steps, block = rows // 2 // tile, (tile, columns)
        places = [lambda g: (g, 0), lambda g: (g + steps, 0)]
        half = (rows // 2, columns)
    else:
        tile = rows // 4
        steps, block = rows // tile, (tile, columns // 2)
        places = [lambda g: (g, 0), lambda g: (g, 1)]
        half = (rows, columns // 2)

    def kernel(flag_ref, keep_low, keep_high, came_low, came_high, low, high):
        low[...] = (keep_low[...].astype(f32) + came_low[...].astype(f32)).astype(bf16)
        high[...] = (keep_high[...].astype(f32) + came_high[...].astype(f32)).astype(bf16)

    ins = [(array, pl.BlockSpec(block, place)) for array in (keep, came) for place in places]
    outs = [(shape(half), pl.BlockSpec(block, lambda g: (g, 0)))] * 2
    return run(order, flags, kernel, ins, outs, [], "fold", grid=(steps,))


def shards(
    block_input,
    out_grad,
    triple_weight,
    output_weight,
    expand_weight,
    contract_weight,
    norm_gains,
    norm_biases,
):
    section = lax.axis_index("pipe")
    span = lax.axis_index("ctx")
    lane = lax.axis_index("tp")
    spans = lax.axis_size("ctx")
    lanes = lax.axis_size("tp")
    micros, rows, width = block_input.shape
    span_rows = rows * lanes
    heads = triple_weight.shape[2]
    head_dim = triple_weight.shape[4]
    across_units = heads * head_dim
    scale = head_dim ** (-0.5)
    first_section = section == 0
    both = (0, 1)

    def hop(array, axis, step, sections):
        size = lax.axis_size(axis)
        pairs = [(s * size + a, s * size + (a ^ step)) for s in sections for a in range(size)]
        return lax.ppermute(array, ("pipe", axis), pairs)

    order = Order()

    def flags_for(wanted):
        return jnp.stack([jnp.asarray(wanted), span, section]).astype(jnp.int32)

    flags = [flags_for(section == s) for s in both]
    always = flags_for(1)

    kept = [[SimpleNamespace() for _ in range(micros)] for _ in both]
    due = {}
    slot_index = [0]

    def slot(hops, kernels=()):
        now = slot_index[0]
        slot_index[0] += 1
        ready = due.pop(now, [])
        hops = [h if len(h) == 3 else h + (1,) for h in hops]
        if hops:
            gated = fence([operand for operand, _, _ in hops], order.last + ready)
            order.last = [min(gated, key=lambda array: array.size)]
            for passed, (_, go, slots) in zip(gated, hops):
                results = go(passed)
                results = results if isinstance(results, list) else [results]
                due.setdefault(now + slots, []).extend(results)
        else:
            order.last = order.last + ready
        for kernel in kernels:
            kernel()

    def halved(keep, came, dim):
        middle = keep.shape[dim] // 2
        total = keep.astype(f32) + came.astype(f32)
        return (
            lax.slice_in_dim(total, 0, middle, axis=dim).astype(bf16),
            lax.slice_in_dim(total, middle, 2 * middle, axis=dim).astype(bf16),
        )

    def spread_hops(pieces, axis, axis_name, sections, first):
        step = lax.axis_size(axis_name) // 4
        going = first
        while step:
            pieces.append(hop(going, axis_name, step, sections))
            going = jnp.concatenate(pieces, axis=axis)
            step //= 2
        return pieces[-1]

    def fold_hops(k, first, axis_name, dim, sections):
        step, size = 1, lax.axis_size(axis_name)
        while 2 * step < size:
            came = hop(first, axis_name, step, sections)
            k.keep, k.send = halved(k.keep, came, dim)
            first = k.send
            step *= 2
        return came

    depth = width // spans
    far = spans // 2
    assert depth == across_units
    small = jnp.concatenate([norm_gains[0], norm_biases[0]], axis=0)
    packed = jnp.concatenate(
        [triple_weight[0].reshape(depth, -1), output_weight[0].reshape(-1, depth)],
        axis=1,
    )
    packed = jnp.pad(packed, ((0, 16), (0, 0)))
    packed = lax.dynamic_update_slice(packed, small, (depth, 0))
    own_expand, own_contract = expand_weight[0], contract_weight[0]
    hidden = own_expand.shape[1]
    inputs = xor_blocks(block_input, span, spans)
    cotangent = xor_blocks(out_grad, span, spans)
    early = jnp.where(first_section, inputs, cotangent)

    in_row = jnp.arange(rows, dtype=jnp.int32)
    in_span = jnp.concatenate([(lane ^ j) * rows + in_row for j in doubling(lanes)])
    positions = span * span_rows + in_span
    key_positions = jnp.stack([(span ^ k) * span_rows + in_span for k in doubling(spans)])
    tables = rope_tables(positions)
    position_column = positions[:, None]
    key_positions = key_positions[:, None, :]

    def blocks_of(own, came):
        held, step = {0: own, far: came}, far // 2
        while step:
            for k in list(held):
                held[k ^ step] = hop(held[k], "ctx", step, both)
            step //= 2
        return [held[k] for k in doubling(spans)]

    lane_offsets = doubling(lanes)

    def across(array, j, source):
        pairs = [(source * lanes + a, (1 - source) * lanes + (a ^ j)) for a in range(lanes)]
        return lax.ppermute(array, ("pipe", "tp"), pairs)

    def rows_far(s, m):
        k = kept[s][m]

        def go(passed):
            k.rows = passed
            k.pieces = [passed, hop(passed, "tp", lanes // 2, (s,))]
            return k.pieces[1]

        return k.rows, go

    def rows_near(s, m):
        k = kept[s][m]

        def go(passed):
            last_piece = spread_hops(k.pieces, 0, "tp", (s,), passed)
            k.row_pieces = [piece[None] for piece in k.pieces]
            return last_piece

        return jnp.concatenate(k.pieces, axis=0), go

    def one_way(array, direction, s):
        pairs = [
            (s * spans + a, s * spans + (a ^ far))
            for a in range(spans)
            if direction * ((a ^ far) - a) > 0
        ]
        return lax.ppermute(array, ("pipe", "ctx"), pairs)

    def pair_far(s, m):
        k = kept[s][m]

        def go(passed):
            k.pairs = [passed, one_way(passed, 1, s)]
            return k.pairs[1]

        return k.pair, go

    def pair_near(s, m):
        k = kept[s][m]

        def go(passed):
            return spread_hops(k.pairs, 0, "ctx", (s,), passed)

        return jnp.concatenate(k.pairs, axis=0), go

    def pair_grad_near(s, m):
        k = kept[s][m].pair_grad
        return k.send, lambda passed: fold_hops(k, passed, "ctx", 0, (s,))

    def pair_grad_both(s, m):
        k = kept[s][m].pair_grad

        def go(passed):
            fold_hops(k, passed, "ctx", 0, (s,))
            k.came = one_way(k.send, -1, s)
            return k.came

        return k.send, go

    def pair_grad_far(s, m):
        k = kept[s][m].pair_grad

        def go(passed):
            k.came = one_way(passed, -1, s)
            return k.came

        return k.send, go

    def sum_near(s, k):
        k.keep, going = k.blocks
        return going, lambda passed: fold_hops(k, passed, "tp", 0, (s,))

    def sum_far(s, k):
        def go(passed):
            k.blocks, k.arrived = [k.keep], [hop(passed, "tp", lanes // 2, (s,))]
            return k.arrived[0]

        return k.send, go

    def total_of(k):
        return sum(array.astype(f32) for array in [k.blocks[0], *k.arrived])

    def norm_back(upstream, combined, entering):
        normalized, inverse = normalize(entering.astype(f32))
        return (
            upstream.astype(f32)
            + inverse
            * (
                combined
                - jnp.mean(combined, axis=-1, keepdims=True)
                - normalized * jnp.mean(combined * normalized, axis=-1, keepdims=True)
            )
        ).astype(bf16)

    def middle_of(m):
        return (inputs[m].astype(f32) + total_of(kept[0][m])).astype(bf16)

    def entry_of(m):
        k = kept[1][m]
        return norm_back(cotangent[m], total_of(k), k.rows)

    def hand_one(s, m):
        k, other = kept[s][m], kept[1 - s][m]
        k.given = middle_of(m) if s == 0 else entry_of(m)

        def go(passed):
            k.given = passed
            other.rows = across(passed, 0, s)
            return other.rows

        return k.given, go

    def run_project(s, m):
        k = kept[s][m]
        pieces, place = (early_pieces, m) if s == 0 else (k.row_pieces, 0)
        k.first, k.second, k.normal, k.queries, pair = project(
            order, flags[s], pieces, place, gains, biases, tables, packed, heads, head_dim
        )
        k.pair = pair[None]

    def run_expand(m):
        k = kept[0][m]
        k.active, k.slope = expand_up(order, flags[0], k.second, weights.expand, span_rows)

    def run_attend(m):
        k = kept[0][m]
        k.attended, k.probs = attend(
            order, flags[0], k.queries, k.pairs, position_column, key_positions, scale
        )

    def run_branch(m):
        k = kept[0][m]
        k.blocks = branch_out(
            order, flags[0], [(k.active, k.attended)], contract, packed
        )

    def run_hidden_both(m):
        k = kept[1][m]
        k.upstream, k.active, k.hidden, k.part, k.side_second = hidden_both(
            order,
            flags[1],
            k.second,
            early_pieces,
            m,
            weights.expand,
            contract,
            k.normal,
            gains,
        )

    def run_attend_both(m):
        k = kept[1][m]
        k.attended, k.turned_back, keep, send = attend_both(
            order,
            flags[1],
            k.upstream,
            packed,
            k.queries,
            k.pairs,
            position_column,
            key_positions,
            tables,
            scale,
        )
        k.pair_grad = SimpleNamespace(keep=keep, send=send)

    def run_attend_back(m):
        k = kept[0][m]
        k.upstream, k.turned_back, keep, send = attend_back(
            order,
            flags[0],
            k.row_pieces,
            packed,
            k.queries,
            k.pairs,
            k.probs,
            tables,
            scale,
        )
        k.pair_grad = SimpleNamespace(keep=keep, send=send)

    def run_hidden_back(m):
        k = kept[0][m]
        k.hidden, k.part, k.side_second = hidden_back(
            order,
            flags[0],
            k.upstream,
            contract,
            weights.expand,
            k.slope,
            k.normal,
            gains,
        )

    def run_project_back(s, m):
        k = kept[s][m]
        own, arrived = k.pair_grad.keep, k.pair_grad.came
        k.stacked, k.side_first, *k.blocks = project_back(
            order,
            flags[s],
            k.turned_back,
            own.reshape(own.shape[1:]),
            arrived.reshape(arrived.shape[1:]),
            packed,
            k.part,
            k.normal,
            gains,
            tables,
        )

    def of(name, s, count=micros):
        return [getattr(kept[s][m], name) for m in range(count)]

    branch_sums, expand_sums, triple_sums = (SimpleNamespace(parts=[]) for _ in range(3))

    def run_sums(w, lefts, rights, by_rows):
        w.dim = 0 if by_rows else 1
        w.keep, w.send = weight_sums(order, always, lefts, rights, by_rows, spans)

    def wide_near(w):
        def go(passed):
            w.came = hop(passed, "ctx", 1, both)
            return w.came

        return w.send, go

    def run_fold(w):
        step = 2
        w.keep, w.send = fold(order, always, w.keep, w.came, w.dim)
        while 2 * step < spans:
            w.came = hop(w.send, "ctx", step, both)
            w.keep, w.send = fold(order, always, w.keep, w.came, w.dim)
            step *= 2

    def wide_far(w, start, stop):
        def go(passed):
            w.parts.append(hop(passed, "ctx", far, both))
            return w.parts[-1]

        return w.send[start:stop], go

    weights = SimpleNamespace(expand_came=[], contract_came=[])
    half_depth = depth // 2

    def expand_far(start, stop):
        def go(passed):
            weights.expand_came.append(hop(passed, "ctx", far, both))
            return weights.expand_came[-1]

        return own_expand[start:stop], go

    def packed_far(passed):
        weights.packed_came = hop(passed, "ctx", far, both)
        return weights.packed_came

    def packed_near(passed):
        weights.packed = blocks_of(packed, passed)
        return weights.packed[1:]

    def expand_near(passed):
        weights.expand = blocks_of(own_expand, passed)
        return weights.expand[1:]

    def contract_far(start, stop):
        def go(passed):
            weights.contract_came.append(hop(passed, "ctx", far, both))
            return weights.contract_came[-1]

        return own_contract[start:stop], go

    def contract_near(passed):
        weights.contract = blocks_of(own_contract, passed)
        return weights.contract[1:]

    def early_hops(passed):
        weights.early = [passed] + [hop(passed, "tp", j, both) for j in lane_offsets[1:]]
        return weights.early[1:]

    due[0] = [expand_far(0, half_depth)[1](own_expand[:half_depth])]
    slot([(packed, packed_far), expand_far(half_depth, depth), (early, early_hops)])
    early_pieces = weights.early
    cuts = [0, hidden // 4, 11 * hidden // 16, hidden]
    expand_came = jnp.concatenate(weights.expand_came, axis=0)
    slot(
        [
            (weights.packed_came, packed_near),
            (expand_came, expand_near),
            contract_far(cuts[0], cuts[1]),
        ]
    )
    packed = weights.packed
    small_full = jnp.concatenate(
        [piece[depth : depth + 4, :depth] for piece in packed], axis=1
    ).astype(f32)
    gains, biases = small_full[:2], small_full[2:]
    slot(
        [contract_far(cuts[1], cuts[2])],
        [lambda m=m: run_project(0, m) for m in range(micros)],
    )
    a, b = kept
    slot(
        [pair_far(0, 0), contract_far(cuts[2], cuts[3])],
        [lambda m=m: run_expand(m) for m in range(micros)],
    )
    contract_came = jnp.concatenate(weights.contract_came, axis=0)
    slot([(contract_came, contract_near), pair_near(0, 0)])
    contract = weights.contract
    slot([pair_far(0, 1)], [lambda: run_attend(0), lambda: run_branch(0)])
    slot([sum_near(0, a[0]), pair_near(0, 1)])
    slot([sum_far(0, a[0]), pair_far(0, 2)], [lambda: run_attend(1), lambda: run_branch(1)])
    slot([hand_one(0, 0), sum_near(0, a[1]), pair_near(0, 2)])
    slot(
        [rows_far(1, 0), sum_far(0, a[1])], [lambda: run_attend(2), lambda: run_branch(2)]
    )
    slot([rows_near(1, 0), hand_one(0, 1), sum_near(0, a[2])])
    slot([rows_far(1, 1), sum_far(0, a[2])], [lambda: run_project(1, 0)])
    slot(
        [pair_far(1, 0), rows_near(1, 1), hand_one(0, 2)], [lambda: run_hidden_both(0)]
    )
    slot([pair_near(1, 0), rows_far(1, 2)], [lambda: run_project(1, 1)])
    slot(
        [pair_far(1, 1), rows_near(1, 2)],
        [lambda: run_attend_both(0), lambda: run_hidden_both(1)],
    )
    slot([pair_grad_near(1, 0), pair_near(1, 1)], [lambda: run_project(1, 2)])
    slot(
        [pair_grad_far(1, 0), pair_far(1, 2)],
        [lambda: run_attend_both(1), lambda: run_hidden_both(2)],
    )
    slot([pair_grad_near(1, 1), pair_near(1, 2)], [lambda: run_project_back(1, 0)])
    slot([sum_near(1, b[0]), pair_grad_far(1, 1)], [lambda: run_attend_both(2)])
    slot([sum_far(1, b[0]), pair_grad_near(1, 2)], [lambda: run_project_back(1, 1)])
    slot([hand_one(1, 0), sum_near(1, b[1]), pair_grad_far(1, 2)])
    slot([sum_far(1, b[1]), rows_far(0, 0)], [lambda: run_project_back(1, 2)])
    slot([sum_near(1, b[2]), hand_one(1, 1), rows_near(0, 0)])
    slot([sum_far(1, b[2]), rows_far(0, 1)], [lambda: run_attend_back(0)])
    slot(
        [hand_one(1, 2), rows_near(0, 1), pair_grad_near(0, 0)],
        [lambda: run_hidden_back(0)],
    )
    slot([rows_far(0, 2), pair_grad_far(0, 0)], [lambda: run_attend_back(1)])
    slot(
        [rows_near(0, 2), pair_grad_near(0, 1)],
        [lambda: run_hidden_back(1), lambda: run_project_back(0, 0)],
    )
    last = micros - 1

    def run_branch_sums():
        run_sums(
            branch_sums,
            [[of("active", s), of("attended", s)] for s in both],
            [
                [of("upstream", 0, last) + [piece[0] for piece in a[last].row_pieces]],
                [of("upstream", 1)],
            ],
            False,
        )

    def run_expand_sums():
        run_sums(
            expand_sums,
            [[of("second", s)] for s in both],
            [[of("hidden", s)] for s in both],
            True,
        )

    def run_triple_sums():
        run_sums(
            triple_sums,
            [[of("first", s)] for s in both],
            [[of("stacked", s)] for s in both],
            True,
        )

    finals = SimpleNamespace()

    def run_final_branch():
        blocks = branch_out(
            order, flags[1], [(k.active, k.attended) for k in b], contract, packed
        )
        finals.keep = jnp.stack(blocks[0::2])
        finals.send = jnp.stack(blocks[1::2])

    def finals_near():
        return finals.send, lambda passed: fold_hops(finals, passed, "tp", 1, (1,))

    def finals_far():
        def go(passed):
            finals.came = hop(passed, "tp", lanes // 2, (1,))
            return finals.came

        return finals.send, go

    slot([pair_grad_far(0, 1), sum_near(0, a[0])], [run_branch_sums])
    slot(
        [wide_near(branch_sums)], [lambda: run_attend_back(2), lambda: run_project_back(0, 1)]
    )
    slot(
        [pair_grad_both(0, 2)], [lambda: run_fold(branch_sums), lambda: run_hidden_back(2)]
    )
    cut = [0, hidden // 2, hidden, hidden + across_units]
    slot(
        [wide_far(branch_sums, cut[0], cut[1]), sum_far(0, a[0]), sum_near(0, a[1])],
        [lambda: run_project_back(0, 2), run_triple_sums],
    )

    def side_of(mades):
        return sum(
            jnp.concatenate([k.side_first, k.side_second], axis=0) for k in mades
        )

    side = SimpleNamespace(all=jnp.where(first_section, side_of(a), side_of(b)))

    def side_ctx(passed):
        step = 1
        while step < spans:
            middle = passed.shape[1] // 2
            came = hop(passed[:, middle:], "ctx", step, both)
            passed = passed[:, :middle] + came
            step *= 2
        side.all = passed
        return came

    def side_near(passed):
        step = 1
        while 2 * step < lanes:
            came = hop(passed, "tp", step, both)
            passed = passed + came
            step *= 2
        side.all = passed
        return came

    def side_far(passed):
        came = hop(passed, "tp", lanes // 2, both)
        side.all = passed + came
        return came

    def held_back(w, j):
        def go(passed):
            w.parts[j] = passed
            return []

        return w.parts[j], go

    def wide_total(keep, parts):
        came = jnp.concatenate(parts, axis=0) if len(parts) > 1 else parts[0]
        return keep.astype(f32) + came.astype(f32)

    slot(
        [
            wide_near(triple_sums),
            wide_far(branch_sums, cut[1], cut[2]),
            (side.all, side_ctx),
            sum_far(0, a[1]),
        ],
        [run_expand_sums, run_final_branch],
    )
    slot([], [lambda: run_fold(triple_sums)])
    slot(
        [
            wide_near(expand_sums),
            wide_far(triple_sums, 0, half_depth),
            wide_far(branch_sums, cut[2], cut[3]),
            sum_near(0, a[2]),
            finals_near(),
        ]
    )
    slot([], [lambda: run_fold(expand_sums)])
    slot(
        [
            wide_far(triple_sums, half_depth, depth),
            wide_far(expand_sums, 0, depth // 4),
            sum_far(0, a[2]),
            (side.all, side_near),
            finals_far(),
        ]
    )
    slot(
        [
            wide_far(expand_sums, depth // 4, depth),
            (side.all, side_far),
            held_back(triple_sums, 1),
            held_back(branch_sums, 2),
        ]
    )
    triple_grads = wide_total(triple_sums.keep, triple_sums.parts)
    triple_grads = triple_grads.reshape(triple_weight.shape)
    branch_grads = wide_total(branch_sums.keep, branch_sums.parts)
    contract_grads, output_grads = branch_grads[:hidden], branch_grads[hidden:]
    expand_grads = wide_total(expand_sums.keep, expand_sums.parts)
    layer_outputs = jnp.stack(
        [
            jnp.where(
                first_section,
                kept[0][m].given,
                (
                    b[m].rows.astype(f32)
                    + finals.keep[m].astype(f32)
                    + finals.came[m].astype(f32)
                ).astype(bf16),
            )
            for m in range(micros)
        ]
    )
    entry_grads = jnp.stack(
        [
            jnp.where(
                first_section,
                norm_back(kept[0][m].rows, total_of(kept[0][m]), inputs[m]),
                kept[1][m].given,
            )
            for m in range(micros)
        ]
    )
    gain_grads = jnp.stack([side.all[0], side.all[2]])
    bias_grads = jnp.stack([side.all[1], side.all[3]])
    return (
        xor_blocks(layer_outputs, span, spans, inverse=True)[None],
        xor_blocks(entry_grads, span, spans, inverse=True)[None],
        triple_grads,
        output_grads.reshape(output_weight.shape),
        expand_grads[None],
        contract_grads[None],
        gain_grads[None],
        bias_grads[None],
    )


def solution(mesh):
    return jax.shard_map(
        shards,
        mesh=mesh,
        in_specs=(
            P(None, ("ctx", "tp"), None),
            P(None, ("ctx", "tp"), None),
            P("pipe", "ctx", "tp", None, None),
            P("pipe", "tp", None, "ctx"),
            P("pipe", "ctx", "tp"),
            P("pipe", "tp", "ctx"),
            P("pipe", None, "ctx"),
            P("pipe", None, "ctx"),
        ),
        out_specs=(
            P("pipe", None, ("ctx", "tp"), None),
            P("pipe", None, ("ctx", "tp"), None),
            P("pipe", "ctx", "tp", None, None),
            P("pipe", "tp", None, "ctx"),
            P("pipe", "ctx", "tp"),
            P("pipe", "tp", "ctx"),
            P("pipe", None, "ctx"),
            P("pipe", None, "ctx"),
        ),
        check_vma=False,
    )
```

profile of v0, /device:TPU:0, one launch (start us, length us, event | category | flops | bytes accessed | tf_op | source)
XLA Modules:
  0.0 797.9 jit_solution(6860961050823963073)
XLA Ops:
  24.0 6.3 collective-permute-done.refs_3_
  37.8 63.2 %collective-permute-done.5.refs_5_ = bf16[256,2048]{1,0:T(8,128)(2,1)S(1)} collective-permute-done((bf16[256,2048]{1,0:T(8,128)(2,1)S(1)}, bf16[256,2048]{1,0:T(8,128)(2,1)S(1)}, u32[]{:S(2)}, u32[]{:S(2)}) %collective-permute-start.5) | collective-permute-done | bytes 1048608 | tf_op jit(solution)/shard_map/ppermute | solution.py:868
  116.1 9.3 %collective-permute-done.10.refs_8_ = bf16[512,512]{1,0:T(8,128)(2,1)S(1)} collective-permute-done((bf16[512,512]{1,0:T(8,128)(2,1)S(1)}, bf16[512,512]{1,0:T(8,128)(2,1)S(1)}, u32[]{:S(2)}, u32[]{:S(2)}) %collective-permute-start.10) | collective-permute-done | bytes 524320 | tf_op jit(solution)/shard_map/ppermute | solution.py:868
  133.7 5.6 project.7
  156.4 5.6 expand.4
  168.5 6.4 collective-permute-done.13.refs_4_
  191.0 5.8 branch.4
  205.4 12.7 %collective-permute-done.18.refs_3_ = bf16[128,2048]{1,0:T(8,128)(2,1)S(1)} collective-permute-done((bf16[128,2048]{1,0:T(8,128)(2,1)S(1)}, bf16[128,2048]{1,0:T(8,128)(2,1)S(1)}, u32[]{:S(2)}, u32[]{:S(2)}) %collective-permute-start.18) | collective-permute-done | bytes 524320 | tf_op jit(solution)/shard_map/ppermute | solution.py:868
  231.1 5.8 branch.5
  245.1 6.2 collective-permute-done.22.refs_3_
  251.4 6.1 collective-permute-done.23.refs_4_
  265.8 6.6 branch.6
  298.1 9.1 %collective-permute-done.31.refs_5_ = bf16[64,2048]{1,0:T(8,128)(2,1)S(1)} collective-permute-done((bf16[64,2048]{1,0:T(8,128)(2,1)S(1)}, bf16[64,2048]{1,0:T(8,128)(2,1)S(1)}, u32[]{:S(2)}, u32[]{:S(2)}) %collective-permute-start.31) | collective-permute-done | bytes 262176 | tf_op jit(solution)/shard_map/ppermute | solution.py:868
  358.7 105.1 %collective-permute-done.50.refs_3_ = bf16[64,2048]{1,0:T(8,128)(2,1)S(1)} collective-permute-done((bf16[64,2048]{1,0:T(8,128)(2,1)S(1)}, bf16[64,2048]{1,0:T(8,128)(2,1)S(1)}, u32[]{:S(2)}, u32[]{:S(2)}) %collective-permute-start.50) | collective-permute-done | bytes 262176 | tf_op jit(solution)/shard_map/ppermute | solution.py:961
  469.8 10.4 %collective-permute-done.52.refs_5_ = bf16[64,2048]{1,0:T(8,128)(2,1)S(1)} collective-permute-done((bf16[64,2048]{1,0:T(8,128)(2,1)S(1)}, bf16[64,2048]{1,0:T(8,128)(2,1)S(1)}, u32[]{:S(2)}, u32[]{:S(2)}) %collective-permute-start.52) | collective-permute-done | bytes 262176 | tf_op jit(solution)/shard_map/ppermute | solution.py:868
  484.8 14.3 %collective-permute-done.56.refs_4_ = bf16[64,2048]{1,0:T(8,128)(2,1)S(1)} collective-permute-done((bf16[64,2048]{1,0:T(8,128)(2,1)S(1)}, bf16[64,2048]{1,0:T(8,128)(2,1)S(1)}, u32[]{:S(2)}, u32[]{:S(2)}) %collective-permute-start.56) | collective-permute-done | bytes 262176 | tf_op jit(solution)/shard_map/ppermute | solution.py:961
  520.3 8.5 %hidden_back.3 = (bf16[256,2048]{1,0:T(8,128)(2,1)S(1)}, f32[256,2048]{1,0:T(8,128)S(1)}, f32[2,2048]{1,0:T(2,128)S(1)}) custom-call(s32[3]{0:T(128)S(1)} %add_add_fusion.1.flag_ref, bf16[256,2048]{1,0:T(8,128)(2,1)S(1)} %get-tuple-element.344.refs_0_.refs_6_, bf16[2048,512]{1,0:T(8,128)(2,1)} %bitcast.27.refs_2_.refs_9_.refs_1_.refs_6_, ...), custom_call_target="tpu_custom_call" | custom-call | flops 14949999616 | tf_op jit(solution)/shard_map/hidden_back/pallas_call | solution.py:168
  542.1 7.4 collective-permute-done.62.refs_3_.refs_9_
  556.3 8.3 %hidden_back.4 = (bf16[256,2048]{1,0:T(8,128)(2,1)S(1)}, f32[256,2048]{1,0:T(8,128)S(1)}, f32[2,2048]{1,0:T(2,128)S(1)}) custom-call(s32[3]{0:T(128)S(1)} %add_add_fusion.1.flag_ref, bf16[256,2048]{1,0:T(8,128)(2,1)S(1)} %get-tuple-element.358.refs_0_.refs_7_, bf16[2048,512]{1,0:T(8,128)(2,1)} %bitcast.27.refs_2_.refs_9_.refs_1_.refs_6_, ...), custom_call_target="tpu_custom_call" | custom-call | flops 14949999616 | tf_op jit(solution)/shard_map/hidden_back/pallas_call | solution.py:168
  577.7 13.5 %weight_sums.3 = (bf16[2560,1024]{1,0:T(8,128)(2,1)S(1)}, bf16[2560,1024]{1,0:T(8,128)(2,1)S(1)}) custom-call(s32[3]{0:T(128)S(1)} %add_add_fusion.3.flag_ref, bf16[256,2048]{1,0:T(8,128)(2,1)S(1)} %copy-done.125, bf16[256,2048]{1,0:T(8,128)(2,1)S(1)} %copy-done.128, bf16[256,2048]{1,0:T(8,128)(2,1)S(1)} %copy-done.53, bf16[256,512]{1,0:T(8,128)(2,1)S(1)} %copy-done.197, ...), custom_call_target="tpu_custom_call" | custom-call | flops 18400000000 | tf_op jit(solution)/shard_map/weight_sums/pallas_call | solution.py:168
  598.6 5.7 project_back.10
  614.3 8.7 %hidden_back.5 = (bf16[256,2048]{1,0:T(8,128)(2,1)S(1)}, f32[256,2048]{1,0:T(8,128)S(1)}, f32[2,2048]{1,0:T(2,128)S(1)}) custom-call(s32[3]{0:T(128)S(1)} %add_add_fusion.1.flag_ref, bf16[256,2048]{1,0:T(8,128)(2,1)S(1)} %copy-done.122, bf16[2048,512]{1,0:T(8,128)(2,1)} %bitcast.27.refs_2_.refs_9_.refs_1_.refs_6_, ...), custom_call_target="tpu_custom_call" | custom-call | flops 14949999616 | tf_op jit(solution)/shard_map/hidden_back/pallas_call | solution.py:168
  639.1 10.1 %weight_sums.4 = (bf16[1024,1536]{1,0:T(8,128)(2,1)S(1)}, bf16[1024,1536]{1,0:T(8,128)(2,1)}) custom-call(s32[3]{0:T(128)S(1)} %add_add_fusion.3.flag_ref, bf16[256,2048]{1,0:T(8,128)(2,1)S(1)} %copy-done.132, bf16[256,2048]{1,0:T(8,128)(2,1)S(1)} %copy-done.140, bf16[256,2048]{1,0:T(8,128)(2,1)S(1)} %copy-done.142, bf16[256,1536]{1,0:T(8,128)(2,1)S(1)} %copy-done.191, ...), custom_call_target="tpu_custom_call" | custom-call | flops 18400000000 | tf_op jit(solution)/shard_map/weight_sums/pallas_call | solution.py:168
  661.4 10.0 %weight_sums.5 = (bf16[1024,2048]{1,0:T(8,128)(2,1)S(1)}, bf16[1024,2048]{1,0:T(8,128)(2,1)S(1)}) custom-call(s32[3]{0:T(128)S(1)} %add_add_fusion.3.flag_ref, bf16[256,2048]{1,0:T(8,128)(2,1)S(1)} %copy-done.130, bf16[256,2048]{1,0:T(8,128)(2,1)S(1)} %copy-done.136, bf16[256,2048]{1,0:T(8,128)(2,1)S(1)} %copy-done.138, bf16[256,2048]{1,0:T(8,128)(2,1)S(1)} %copy-done.218, ...), custom_call_target="tpu_custom_call" | custom-call | flops 18400000000 | tf_op jit(solution)/shard_map/weight_sums/pallas_call | solution.py:168
  675.3 7.5 collective-permute-done.77.refs_7_
  691.8 11.0 %collective-permute-done.83.refs_8_ = bf16[128,2048]{1,0:T(8,128)(2,1)S(1)} collective-permute-done((bf16[128,2048]{1,0:T(8,128)(2,1)S(1)}, bf16[128,2048]{1,0:T(8,128)(2,1)S(1)}, u32[]{:S(2)}, u32[]{:S(2)}) %collective-permute-start.83) | collective-permute-done | bytes 524320 | tf_op jit(solution)/shard_map/ppermute | solution.py:868
  703.6 16.5 %collective-permute-done.82.refs_7_.refs_3_ = bf16[512,512]{1,0:T(8,128)(2,1)S(1)} collective-permute-done((bf16[512,512]{1,0:T(8,128)(2,1)S(1)}, bf16[512,512]{1,0:T(8,128)(2,1)S(1)}, u32[]{:S(2)}, u32[]{:S(2)}) %collective-permute-start.82) | collective-permute-done | bytes 524320 | tf_op jit(solution)/shard_map/ppermute | solution.py:868
  732.3 6.3 collective-permute-done.85.refs_7_
  741.9 7.9 collective-permute-done.87.refs_5_
  749.9 8.3 %collective-permute-done.88.refs_6_ = bf16[128,2048]{1,0:T(8,128)(2,1)S(1)} collective-permute-done((bf16[128,2048]{1,0:T(8,128)(2,1)S(1)}, bf16[128,2048]{1,0:T(8,128)(2,1)S(1)}, u32[]{:S(2)}, u32[]{:S(2)}) %collective-permute-start.88) | collective-permute-done | bytes 524320 | tf_op jit(solution)/shard_map/ppermute | solution.py:868
  773.6 5.9 copy.119
  780.7 12.7 %collective-permute-done.89 = bf16[384,2048]{1,0:T(8,128)(2,1)} collective-permute-done((bf16[384,2048]{1,0:T(8,128)(2,1)}, bf16[384,2048]{1,0:T(8,128)(2,1)}, u32[]{:S(2)}, u32[]{:S(2)}) %collective-permute-start.89) | collective-permute-done | bytes 1572896 | tf_op jit(solution)/shard_map/ppermute | solution.py:868
  (904 shorter events, 365.2 us)
Async XLA Ops:
  3.9 26.4 %collective-permute-start = (bf16[256,2048]{1,0:T(8,128)(2,1)}, bf16[256,2048]{1,0:T(8,128)(2,1)}, u32[]{:S(2)}, u32[]{:S(2)}) collective-permute-start(bf16[256,2048]{1,0:T(8,128)(2,1)} %get-tuple-element.494), channel_id=1, source_target_pairs={{0,8},{4,12},{8,0},{12,4},{16,24},{20,28},{24,16},{28,20},{1,9},{5... | collective-permute-start | bytes 3145736 | tf_op jit(solution)/shard_map/ppermute | solution.py:868
  30.3 72.2 %collective-permute-start.4 = (bf16[528,2048]{1,0:T(8,128)(2,1)S(1)}, bf16[528,2048]{1,0:T(8,128)(2,1)S(1)}, u32[]{:S(2)}, u32[]{:S(2)}) collective-permute-start(bf16[528,2048]{1,0:T(8,128)(2,1)S(1)} %get-tuple-element.228), channel_id=1, source_target_pairs={{0,8},{4,12},{8,0},{12,4},{16,24},{20,28},{24,16},{28,20},{1,9},{5... | collective-permute-start | bytes 6488072 | tf_op jit(solution)/shard_map/ppermute | solution.py:868
  32.0 68.9 %collective-permute-start.5 = (bf16[256,2048]{1,0:T(8,128)(2,1)S(1)}, bf16[256,2048]{1,0:T(8,128)(2,1)S(1)}, u32[]{:S(2)}, u32[]{:S(2)}) collective-permute-start(bf16[256,2048]{1,0:T(8,128)(2,1)S(1)} %get-tuple-element.229), channel_id=1, source_target_pairs={{0,8},{4,12},{8,0},{12,4},{16,24},{20,28},{24,16},{28,20},{1,9},{5... | collective-permute-start | bytes 3145736 | tf_op jit(solution)/shard_map/ppermute | solution.py:868
  32.3 70.4 %collective-permute-start.1 = (bf16[3,64,2048]{2,1,0:T(8,128)(2,1)S(1)}, bf16[3,64,2048]{2,1,0:T(8,128)(2,1)S(1)}, u32[]{:S(2)}, u32[]{:S(2)}) collective-permute-start(bf16[3,64,2048]{2,1,0:T(8,128)(2,1)S(1)} %get-tuple-element.227.refs_3_.refs_0_.refs_1_), channel_id=1, source_target_pairs={{0,2},{1,3},{2,0},{3,1},{16,18},{17,19},{18,16},{19,17},{4,6},{5,7... | collective-permute-start | bytes 2359304 | tf_op jit(solution)/shard_map/ppermute | solution.py:868
  35.2 67.6 %collective-permute-start.2 = (bf16[3,64,2048]{2,1,0:T(8,128)(2,1)S(1)}, bf16[3,64,2048]{2,1,0:T(8,128)(2,1)S(1)}, u32[]{:S(2)}, u32[]{:S(2)}) collective-permute-start(bf16[3,64,2048]{2,1,0:T(8,128)(2,1)S(1)} %get-tuple-element.227.refs_3_.refs_0_.refs_1_), channel_id=1, source_target_pairs={{0,1},{1,0},{2,3},{3,2},{16,17},{17,16},{18,19},{19,18},{4,5},{5,4... | collective-permute-start | bytes 2359304 | tf_op jit(solution)/shard_map/ppermute | solution.py:868
  36.7 66.0 %collective-permute-start.3 = (bf16[3,64,2048]{2,1,0:T(8,128)(2,1)S(1)}, bf16[3,64,2048]{2,1,0:T(8,128)(2,1)S(1)}, u32[]{:S(2)}, u32[]{:S(2)}) collective-permute-start(bf16[3,64,2048]{2,1,0:T(8,128)(2,1)S(1)} %get-tuple-element.227.refs_3_.refs_0_.refs_1_), channel_id=1, source_target_pairs={{0,3},{1,2},{2,1},{3,0},{16,19},{17,18},{18,17},{19,16},{4,7},{5,6... | collective-permute-start | bytes 2359304 | tf_op jit(solution)/shard_map/ppermute | solution.py:868
  106.0 74.8 %collective-permute-start.15 = (bf16[2048,512]{1,0:T(8,128)(2,1)}, bf16[2048,512]{1,0:T(8,128)(2,1)}, u32[]{:S(2)}, u32[]{:S(2)}) collective-permute-start(bf16[2048,512]{1,0:T(8,128)(2,1)} %bitcast.27.refs_2_.refs_9_.refs_1_.refs_6_), channel_id=1, source_target_pairs={{0,4},{4,0},{8,12},{12,8},{16,20},{20,16},{24,28},{28,24},{1,5},{5... | collective-permute-start | bytes 6291464 | tf_op jit(solution)/shard_map/ppermute | solution.py:868
  106.8 18.6 %collective-permute-start.9 = (bf16[512,2048]{1,0:T(8,128)(2,1)}, bf16[512,2048]{1,0:T(8,128)(2,1)S(1)}, u32[]{:S(2)}, u32[]{:S(2)}) collective-permute-start(bf16[512,2048]{1,0:T(8,128)(2,1)} %copy-done), channel_id=1, source_target_pairs={{0,4},{4,0},{8,12},{12,8},{16,20},{20,16},{24,28},{28,24},{1,5},{5... | collective-permute-start | bytes 6291464 | tf_op jit(solution)/shard_map/ppermute | solution.py:868
  125.4 22.0 %collective-permute-start.11 = (bf16[896,512]{1,0:T(8,128)(2,1)S(1)}, bf16[896,512]{1,0:T(8,128)(2,1)S(1)}, u32[]{:S(2)}, u32[]{:S(2)}) collective-permute-start(bf16[896,512]{1,0:T(8,128)(2,1)S(1)} %fence.37.refs_11_), channel_id=1, source_target_pairs={{0,8},{4,12},{8,0},{12,4},{16,24},{20,28},{24,16},{28,20},{1,9},{5... | collective-permute-start | bytes 2752520 | tf_op jit(solution)/shard_map/ppermute | solution.py:868
  147.4 20.2 %collective-permute-start.12 = (bf16[1,2,2,256,256]{4,3,2,1,0:T(8,128)(2,1)S(1)}, bf16[1,2,2,256,256]{4,3,2,1,0:T(8,128)(2,1)S(1)}, u32[]{:S(2)}, u32[]{:S(2)}) collective-permute-start(bf16[1,2,2,256,256]{4,3,2,1,0:T(8,128)(2,1)S(1)} %get-tuple-element.238.refs_5_.refs_1_.refs_8_), channel_id=1, source_target_pairs={{0,8},{4,12},{1,9},{5,13},{2,10},{6,14},{3,11},{7,15}} | collective-permute-start | bytes 1572872 | tf_op jit(solution)/shard_map/ppermute | solution.py:989
  150.7 24.2 %collective-permute-start.13 = (bf16[640,512]{1,0:T(8,128)(2,1)S(1)}, bf16[640,512]{1,0:T(8,128)(2,1)S(1)}, u32[]{:S(2)}, u32[]{:S(2)}) collective-permute-start(bf16[640,512]{1,0:T(8,128)(2,1)S(1)} %get-tuple-element.240), channel_id=1, source_target_pairs={{0,8},{4,12},{8,0},{12,4},{16,24},{20,28},{24,16},{28,20},{1,9},{5... | collective-permute-start | bytes 1966088 | tf_op jit(solution)/shard_map/ppermute | solution.py:868
  218.4 20.8 %collective-permute-start.21 = (bf16[1,2,2,256,256]{4,3,2,1,0:T(8,128)(2,1)S(1)}, bf16[1,2,2,256,256]{4,3,2,1,0:T(8,128)(2,1)S(1)}, u32[]{:S(2)}, u32[]{:S(2)}) collective-permute-start(bf16[1,2,2,256,256]{4,3,2,1,0:T(8,128)(2,1)S(1)} %get-tuple-element.257.refs_1_.refs_8_), channel_id=1, source_target_pairs={{0,8},{4,12},{1,9},{5,13},{2,10},{6,14},{3,11},{7,15}} | collective-permute-start | bytes 1572872 | tf_op jit(solution)/shard_map/ppermute | solution.py:989
  355.6 108.3 %collective-permute-start.49 = (bf16[128,2048]{1,0:T(8,128)(2,1)S(1)}, bf16[128,2048]{1,0:T(8,128)(2,1)S(1)}, u32[]{:S(2)}, u32[]{:S(2)}) collective-permute-start(bf16[128,2048]{1,0:T(8,128)(2,1)S(1)} %get-tuple-element.329), channel_id=1, source_target_pairs={{16,17},{17,16},{18,19},{19,18},{20,21},{21,20},{22,23},{23,22},{2... | collective-permute-start | bytes 1572872 | tf_op jit(solution)/shard_map/ppermute | solution.py:868
  356.5 107.3 %collective-permute-start.50 = (bf16[64,2048]{1,0:T(8,128)(2,1)S(1)}, bf16[64,2048]{1,0:T(8,128)(2,1)S(1)}, u32[]{:S(2)}, u32[]{:S(2)}) collective-permute-start(bf16[64,2048]{1,0:T(8,128)(2,1)S(1)} %get-tuple-element.330.refs_2_), channel_id=1, source_target_pairs={{16,0},{17,1},{18,2},{19,3},{20,4},{21,5},{22,6},{23,7},{24,8},{25... | collective-permute-start | bytes 786440 | tf_op jit(solution)/shard_map/ppermute | solution.py:961
  357.8 106.2 %collective-permute-start.51 = (bf16[1,2,2,256,256]{4,3,2,1,0:T(8,128)(2,1)S(1)}, bf16[1,2,2,256,256]{4,3,2,1,0:T(8,128)(2,1)S(1)}, u32[]{:S(2)}, u32[]{:S(2)}) collective-permute-start(bf16[1,2,2,256,256]{4,3,2,1,0:T(8,128)(2,1)S(1)} %get-tuple-element.331), channel_id=1, source_target_pairs={{24,16},{28,20},{25,17},{29,21},{26,18},{30,22},{27,19},{31,23}} | collective-permute-start | bytes 1572872 | tf_op jit(solution)/shard_map/ppermute | solution.py:989
  480.6 18.5 %collective-permute-start.55 = (bf16[128,2048]{1,0:T(8,128)(2,1)S(1)}, bf16[128,2048]{1,0:T(8,128)(2,1)S(1)}, u32[]{:S(2)}, u32[]{:S(2)}) collective-permute-start(bf16[128,2048]{1,0:T(8,128)(2,1)S(1)} %get-tuple-element.341), channel_id=1, source_target_pairs={{16,17},{17,16},{18,19},{19,18},{20,21},{21,20},{22,23},{23,22},{2... | collective-permute-start | bytes 1572872 | tf_op jit(solution)/shard_map/ppermute | solution.py:868
  550.9 21.5 %collective-permute-start.65 = (bf16[2,2,2,256,256]{4,3,2,1,0:T(8,128)(2,1)S(1)}, bf16[2,2,2,256,256]{4,3,2,1,0:T(8,128)(2,1)S(1)}, u32[]{:S(2)}, u32[]{:S(2)}) collective-permute-start(bf16[2,2,2,256,256]{4,3,2,1,0:T(8,128)(2,1)S(1)} %get-tuple-element.368), channel_id=1, source_target_pairs={{0,4},{4,0},{8,12},{12,8},{1,5},{5,1},{9,13},{13,9},{2,6},{6,2},{1... | collective-permute-start | bytes 3145736 | tf_op jit(solution)/shard_map/ppermute | solution.py:868
  552.9 20.5 %collective-permute-start.64 = (bf16[128,2048]{1,0:T(8,128)(2,1)S(1)}, bf16[128,2048]{1,0:T(8,128)(2,1)S(1)}, u32[]{:S(2)}, u32[]{:S(2)}) collective-permute-start(bf16[128,2048]{1,0:T(8,128)(2,1)S(1)} %get-tuple-element.364.refs_12_), channel_id=1, source_target_pairs={{0,1},{1,0},{2,3},{3,2},{4,5},{5,4},{6,7},{7,6},{8,9},{9,8},{10,11... | collective-permute-start | bytes 1572872 | tf_op jit(solution)/shard_map/ppermute | solution.py:868
  627.0 22.4 %collective-permute-start.71 = (bf16[128,2048]{1,0:T(8,128)(2,1)}, bf16[128,2048]{1,0:T(8,128)(2,1)S(1)}, u32[]{:S(2)}, u32[]{:S(2)}) collective-permute-start(bf16[128,2048]{1,0:T(8,128)(2,1)} %get-tuple-element.411), channel_id=1, source_target_pairs={{0,1},{1,0},{2,3},{3,2},{4,5},{5,4},{6,7},{7,6},{8,9},{9,8},{10,11... | collective-permute-start | bytes 1572872 | tf_op jit(solution)/shard_map/ppermute | solution.py:868
  630.3 24.6 %collective-permute-start.72 = (bf16[1024,512]{1,0:T(8,128)(2,1)S(1)}, bf16[1024,512]{1,0:T(8,128)(2,1)S(1)}, u32[]{:S(2)}, u32[]{:S(2)}) collective-permute-start(bf16[1024,512]{1,0:T(8,128)(2,1)S(1)} %get-tuple-element.413), channel_id=1, source_target_pairs={{0,8},{4,12},{8,0},{12,4},{16,24},{20,28},{24,16},{28,20},{1,9},{5... | collective-permute-start | bytes 3145736 | tf_op jit(solution)/shard_map/ppermute | solution.py:868
  630.4 19.2 %collective-permute-start.73 = (bf16[64,2048]{1,0:T(8,128)(2,1)S(1)}, bf16[64,2048]{1,0:T(8,128)(2,1)S(1)}, u32[]{:S(2)}, u32[]{:S(2)}) collective-permute-start(bf16[64,2048]{1,0:T(8,128)(2,1)S(1)} %get-tuple-element.400.refs_11_), channel_id=1, source_target_pairs={{0,2},{1,3},{2,0},{3,1},{4,6},{5,7},{6,4},{7,5},{8,10},{9,11},{10,... | collective-permute-start | bytes 786440 | tf_op jit(solution)/shard_map/ppermute | solution.py:868
  655.0 27.8 %collective-permute-start.74 = (bf16[1024,1536]{1,0:T(8,128)(2,1)}, bf16[1024,1536]{1,0:T(8,128)(2,1)}, u32[]{:S(2)}, u32[]{:S(2)}) collective-permute-start(bf16[1024,1536]{1,0:T(8,128)(2,1)} %get-tuple-element.420), channel_id=1, source_target_pairs={{0,4},{4,0},{8,12},{12,8},{16,20},{20,16},{24,28},{28,24},{1,5},{5... | collective-permute-start | bytes 9437192 | tf_op jit(solution)/shard_map/ppermute | solution.py:868
  657.5 25.3 %collective-permute-start.75 = (bf16[1024,512]{1,0:T(8,128)(2,1)S(1)}, bf16[1024,512]{1,0:T(8,128)(2,1)S(1)}, u32[]{:S(2)}, u32[]{:S(2)}) collective-permute-start(bf16[1024,512]{1,0:T(8,128)(2,1)S(1)} %get-tuple-element.421), channel_id=1, source_target_pairs={{0,8},{4,12},{8,0},{12,4},{16,24},{20,28},{24,16},{28,20},{1,9},{5... | collective-permute-start | bytes 3145736 | tf_op jit(solution)/shard_map/ppermute | solution.py:868
  657.8 25.0 %collective-permute-start.78 = (bf16[64,2048]{1,0:T(8,128)(2,1)S(1)}, bf16[64,2048]{1,0:T(8,128)(2,1)S(1)}, u32[]{:S(2)}, u32[]{:S(2)}) collective-permute-start(bf16[64,2048]{1,0:T(8,128)(2,1)S(1)} %get-tuple-element.422), channel_id=1, source_target_pairs={{0,2},{1,3},{2,0},{3,1},{4,6},{5,7},{6,4},{7,5},{8,10},{9,11},{10,... | collective-permute-start | bytes 786440 | tf_op jit(solution)/shard_map/ppermute | solution.py:868
  685.3 34.9 %collective-permute-start.80 = (bf16[1024,2048]{1,0:T(8,128)(2,1)S(1)}, bf16[1024,2048]{1,0:T(8,128)(2,1)S(1)}, u32[]{:S(2)}, u32[]{:S(2)}) collective-permute-start(bf16[1024,2048]{1,0:T(8,128)(2,1)S(1)} %get-tuple-element.430), channel_id=1, source_target_pairs={{0,4},{4,0},{8,12},{12,8},{16,20},{20,16},{24,28},{28,24},{1,5},{5... | collective-permute-start | bytes 12582920 | tf_op jit(solution)/shard_map/ppermute | solution.py:868
  689.7 30.4 %collective-permute-start.81 = (bf16[256,1536]{1,0:T(8,128)(2,1)S(1)}, bf16[256,1536]{1,0:T(8,128)(2,1)S(1)}, u32[]{:S(2)}, u32[]{:S(2)}) collective-permute-start(bf16[256,1536]{1,0:T(8,128)(2,1)S(1)} %get-tuple-element.432), channel_id=1, source_target_pairs={{0,8},{4,12},{8,0},{12,4},{16,24},{20,28},{24,16},{28,20},{1,9},{5... | collective-permute-start | bytes 2359304 | tf_op jit(solution)/shard_map/ppermute | solution.py:868
  690.0 30.1 %collective-permute-start.82 = (bf16[512,512]{1,0:T(8,128)(2,1)S(1)}, bf16[512,512]{1,0:T(8,128)(2,1)S(1)}, u32[]{:S(2)}, u32[]{:S(2)}) collective-permute-start(bf16[512,512]{1,0:T(8,128)(2,1)S(1)} %get-tuple-element.431.refs_4_), channel_id=1, source_target_pairs={{0,8},{4,12},{8,0},{12,4},{16,24},{20,28},{24,16},{28,20},{1,9},{5... | collective-permute-start | bytes 1572872 | tf_op jit(solution)/shard_map/ppermute | solution.py:868
  729.3 20.5 %collective-permute-start.87 = (bf16[256,1536]{1,0:T(8,128)(2,1)S(1)}, bf16[256,1536]{1,0:T(8,128)(2,1)S(1)}, u32[]{:S(2)}, u32[]{:S(2)}) collective-permute-start(bf16[256,1536]{1,0:T(8,128)(2,1)S(1)} %get-tuple-element.440), channel_id=1, source_target_pairs={{0,8},{4,12},{8,0},{12,4},{16,24},{20,28},{24,16},{28,20},{1,9},{5... | collective-permute-start | bytes 2359304 | tf_op jit(solution)/shard_map/ppermute | solution.py:868
  729.6 28.6 %collective-permute-start.84 = (bf16[3,64,2048]{2,1,0:T(8,128)(2,1)S(1)}, bf16[3,64,2048]{2,1,0:T(8,128)(2,1)S(1)}, u32[]{:S(2)}, u32[]{:S(2)}) collective-permute-start(bf16[3,64,2048]{2,1,0:T(8,128)(2,1)S(1)} %get-tuple-element.437), channel_id=1, source_target_pairs={{16,18},{17,19},{18,16},{19,17},{20,22},{21,23},{22,20},{23,21},{2... | collective-permute-start | bytes 2359304 | tf_op jit(solution)/shard_map/ppermute | solution.py:868
  730.5 27.7 %collective-permute-start.88 = (bf16[128,2048]{1,0:T(8,128)(2,1)S(1)}, bf16[128,2048]{1,0:T(8,128)(2,1)S(1)}, u32[]{:S(2)}, u32[]{:S(2)}) collective-permute-start(bf16[128,2048]{1,0:T(8,128)(2,1)S(1)} %get-tuple-element.441), channel_id=1, source_target_pairs={{0,8},{4,12},{8,0},{12,4},{16,24},{20,28},{24,16},{28,20},{1,9},{5... | collective-permute-start | bytes 1572872 | tf_op jit(solution)/shard_map/ppermute | solution.py:868
  758.2 21.3 %collective-permute-start.90 = (f32[4,512]{1,0:T(4,128)S(1)}, f32[4,512]{1,0:T(4,128)S(1)}, u32[]{:S(2)}, u32[]{:S(2)}) collective-permute-start(f32[4,512]{1,0:T(4,128)S(1)} %get-tuple-element.445), channel_id=1, source_target_pairs={{0,2},{1,3},{2,0},{3,1},{16,18},{17,19},{18,16},{19,17},{4,6},{5,7... | collective-permute-start | bytes 24584 | tf_op jit(solution)/shard_map/ppermute | solution.py:868
  759.7 33.7 %collective-permute-start.89 = (bf16[384,2048]{1,0:T(8,128)(2,1)}, bf16[384,2048]{1,0:T(8,128)(2,1)}, u32[]{:S(2)}, u32[]{:S(2)}) collective-permute-start(bf16[384,2048]{1,0:T(8,128)(2,1)} %get-tuple-element.444), channel_id=1, source_target_pairs={{0,8},{4,12},{8,0},{12,4},{16,24},{20,28},{24,16},{28,20},{1,9},{5... | collective-permute-start | bytes 4718600 | tf_op jit(solution)/shard_map/ppermute | solution.py:868
  (307 other events, 3439.6 us)
where the time goes:
time: 809 us; the launch traced here: 798 us
  waiting for transfers between devices  368 us (45%)
  Pallas kernels  167 us (21%)
  starting transfers between devices  143 us (18%)
  local copies, waits for them, and re-layouts  77.6 us (10%)
  other arithmetic  36.3 us (4%)
    ppermute x73, waiting for transfers between devices, hop(): return lax.ppermute(array, ('pipe', axis), pairs)  225 us
    pallas_call x40, Pallas kernels, run(): pl.pallas_call(body, grid=grid, in_specs=[spec for spec, _ in in_specs],...  167 us
    ppermute x6, waiting for transfers between devices, across(): return lax.ppermute(array, ('pipe', 'tp'), pairs)  136 us
    ppermute x73, starting transfers between devices, hop(): return lax.ppermute(array, ('pipe', axis), pairs)  109 us
    unnamed x507, local copies, waits for them, and re-layouts  53 us
    ppermute x12, starting transfers between devices, one_way(): return lax.ppermute(array, ('pipe', 'ctx'), pairs)  21 us
  transfers between devices with their start and end apart: 91, of which 35 were waited for; matrix products, arithmetic and copies ran while one was open for 8% of the time, Pallas kernels for 20%

commit v1 on v0

--- a/solution.py
+++ b/solution.py
@@ -1343,27 +1343,32 @@
         finals.keep = jnp.stack(blocks[0::2])
         finals.send = jnp.stack(blocks[1::2])
 
-    def finals_near():
-        return finals.send, lambda passed: fold_hops(finals, passed, "tp", 1, (1,))
-
-    def finals_far():
+    def last_near(w, s):
+        return w.send, lambda passed: fold_hops(w, passed, "tp", 1, (s,))
+
+    def last_far(w, s):
         def go(passed):
-            finals.came = hop(passed, "tp", lanes // 2, (1,))
-            return finals.came
-
-        return finals.send, go
-
-    slot([pair_grad_far(0, 1), sum_near(0, a[0])], [run_branch_sums])
+            w.came = hop(passed, "tp", lanes // 2, (s,))
+            return w.came
+
+        return w.send, go
+
+    slot([pair_grad_far(0, 1)], [run_branch_sums])
     slot(
         [wide_near(branch_sums)], [lambda: run_attend_back(2), lambda: run_project_back(0, 1)]
     )
-    slot(
-        [pair_grad_both(0, 2)], [lambda: run_fold(branch_sums), lambda: run_hidden_back(2)]
-    )
+    slot([], [lambda: run_fold(branch_sums)])
     cut = [0, hidden // 2, hidden, hidden + across_units]
     slot(
-        [wide_far(branch_sums, cut[0], cut[1]), sum_far(0, a[0]), sum_near(0, a[1])],
+        [wide_far(branch_sums, cut[0], cut[1]), pair_grad_both(0, 2)],
+        [lambda: run_hidden_back(2)],
+    )
+    slot(
+        [wide_far(branch_sums, cut[1], cut[2])],
         [lambda: run_project_back(0, 2), run_triple_sums],
+    )
+    outs = SimpleNamespace(
+        keep=jnp.stack([k.blocks[0] for k in a]), send=jnp.stack([k.blocks[1] for k in a])
     )
 
     def side_of(mades):
@@ -1411,37 +1416,29 @@
     slot(
         [
             wide_near(triple_sums),
-            wide_far(branch_sums, cut[1], cut[2]),
+            wide_far(branch_sums, cut[2], cut[3]),
             (side.all, side_ctx),
-            sum_far(0, a[1]),
         ],
         [run_expand_sums, run_final_branch],
     )
     slot([], [lambda: run_fold(triple_sums)])
     slot(
         [
+            wide_far(triple_sums, 0, depth),
             wide_near(expand_sums),
-            wide_far(triple_sums, 0, half_depth),
-            wide_far(branch_sums, cut[2], cut[3]),
-            sum_near(0, a[2]),
-            finals_near(),
+            last_near(outs, 0),
+            last_near(finals, 1),
+            (side.all, side_near),
         ]
     )
     slot([], [lambda: run_fold(expand_sums)])
     slot(
         [
-            wide_far(triple_sums, half_depth, depth),
-            wide_far(expand_sums, 0, depth // 4),
-            sum_far(0, a[2]),
-            (side.all, side_near),
-            finals_far(),
-        ]
-    )
-    slot(
-        [
-            wide_far(expand_sums, depth // 4, depth),
+            wide_far(expand_sums, 0, depth),
+            last_far(outs, 0),
+            last_far(finals, 1),
             (side.all, side_far),
-            held_back(triple_sums, 1),
+            held_back(triple_sums, 0),
             held_back(branch_sums, 2),
         ]
     )
@@ -1464,15 +1461,11 @@
             for m in range(micros)
         ]
     )
-    entry_grads = jnp.stack(
-        [
-            jnp.where(
-                first_section,
-                norm_back(kept[0][m].rows, total_of(kept[0][m]), inputs[m]),
-                kept[1][m].given,
-            )
-            for m in range(micros)
-        ]
+    own_rows = jnp.stack(of("rows", 0))
+    entry_grads = jnp.where(
+        first_section,
+        norm_back(own_rows, outs.keep.astype(f32) + outs.came.astype(f32), inputs),
+        jnp.stack(of("given", 1)),
     )
     gain_grads = jnp.stack([side.all[0], side.all[2]])
     bias_grads = jnp.stack([side.all[1], side.all[3]])

time: 809 us -> 808 us (level)
  starting transfers between devices: 143 us -> 125 us
  waiting for transfers between devices: 368 us -> 378 us
    ppermute x73 -> x67, starting transfers between devices: 109 us -> 94 us  [hop(): return lax.ppermute(array, ('pipe', axis), pairs)]
    unnamed x507 -> x500, local copies, waits for them, and re-layouts: 53 us -> 56 us
    ppermute x73 -> x67, waiting for transfers between devices: 225 us -> 228 us  [hop(): return lax.ppermute(array, ('pipe', axis), pairs)]
  transfers between devices with their start and end apart: 91 -> 85, of which waited for: 35 -> 34; matrix products, arithmetic and copies ran while one was open for 8% -> 8% of each run, Pallas kernels for 20% -> 20%
where the time goes in v1:
time: 808 us; the launch traced here: 798 us
  waiting for transfers between devices  378 us (47%)
  Pallas kernels  170 us (21%)
  starting transfers between devices  125 us (15%)
  local copies, waits for them, and re-layouts  78.9 us (10%)
  other arithmetic  40.7 us (5%)
    ppermute x67, waiting for transfers between devices, hop(): return lax.ppermute(array, ('pipe', axis), pairs)  228 us
    pallas_call x40, Pallas kernels, run(): pl.pallas_call(body, grid=grid, in_specs=[spec for spec, _ in in_specs],...  170 us
    ppermute x6, waiting for transfers between devices, across(): return lax.ppermute(array, ('pipe', 'tp'), pairs)  136 us
    ppermute x67, starting transfers between devices, hop(): return lax.ppermute(array, ('pipe', axis), pairs)  94 us
    unnamed x500, local copies, waits for them, and re-layouts  56 us
    ppermute x12, starting transfers between devices, one_way(): return lax.ppermute(array, ('pipe', 'ctx'), pairs)  21.1 us
  transfers between devices with their start and end apart: 85, of which 34 were waited for; matrix products, arithmetic and copies ran while one was open for 8% of the time, Pallas kernels for 20%

profile of v1, /device:TPU:0, one launch (start us, length us, event | category | flops | bytes accessed | tf_op | source)
XLA Modules:
  0.0 797.6 jit_solution(15060131426230675594)
XLA Ops:
  37.8 63.2 %collective-permute-done.5.refs_5_ = bf16[256,2048]{1,0:T(8,128)(2,1)S(1)} collective-permute-done((bf16[256,2048]{1,0:T(8,128)(2,1)S(1)}, bf16[256,2048]{1,0:T(8,128)(2,1)S(1)}, u32[]{:S(2)}, u32[]{:S(2)}) %collective-permute-start.5) | collective-permute-done | bytes 1048608 | tf_op jit(solution)/shard_map/ppermute | solution.py:868
  116.0 9.3 %collective-permute-done.10.refs_8_ = bf16[512,512]{1,0:T(8,128)(2,1)S(1)} collective-permute-done((bf16[512,512]{1,0:T(8,128)(2,1)S(1)}, bf16[512,512]{1,0:T(8,128)(2,1)S(1)}, u32[]{:S(2)}, u32[]{:S(2)}) %collective-permute-start.10) | collective-permute-done | bytes 524320 | tf_op jit(solution)/shard_map/ppermute | solution.py:868
  133.6 5.6 project.7
  150.8 5.5 expand.3
  156.3 5.6 expand.4
  162.0 5.5 expand.5
  168.5 6.4 collective-permute-done.13.refs_4_
  190.9 5.8 branch.4
  205.4 12.7 %collective-permute-done.18.refs_3_ = bf16[128,2048]{1,0:T(8,128)(2,1)S(1)} collective-permute-done((bf16[128,2048]{1,0:T(8,128)(2,1)S(1)}, bf16[128,2048]{1,0:T(8,128)(2,1)S(1)}, u32[]{:S(2)}, u32[]{:S(2)}) %collective-permute-start.18) | collective-permute-done | bytes 524320 | tf_op jit(solution)/shard_map/ppermute | solution.py:868
  231.1 5.8 branch.5
  245.1 6.2 collective-permute-done.22.refs_3_
  251.4 6.1 collective-permute-done.23.refs_4_
  266.0 6.5 branch.6
  298.3 9.1 %collective-permute-done.31.refs_5_ = bf16[64,2048]{1,0:T(8,128)(2,1)S(1)} collective-permute-done((bf16[64,2048]{1,0:T(8,128)(2,1)S(1)}, bf16[64,2048]{1,0:T(8,128)(2,1)S(1)}, u32[]{:S(2)}, u32[]{:S(2)}) %collective-permute-start.31) | collective-permute-done | bytes 262176 | tf_op jit(solution)/shard_map/ppermute | solution.py:868
  357.6 105.2 %collective-permute-done.50.refs_3_ = bf16[64,2048]{1,0:T(8,128)(2,1)S(1)} collective-permute-done((bf16[64,2048]{1,0:T(8,128)(2,1)S(1)}, bf16[64,2048]{1,0:T(8,128)(2,1)S(1)}, u32[]{:S(2)}, u32[]{:S(2)}) %collective-permute-start.50) | collective-permute-done | bytes 262176 | tf_op jit(solution)/shard_map/ppermute | solution.py:961
  468.7 10.5 %collective-permute-done.52.refs_5_ = bf16[64,2048]{1,0:T(8,128)(2,1)S(1)} collective-permute-done((bf16[64,2048]{1,0:T(8,128)(2,1)S(1)}, bf16[64,2048]{1,0:T(8,128)(2,1)S(1)}, u32[]{:S(2)}, u32[]{:S(2)}) %collective-permute-start.52) | collective-permute-done | bytes 262176 | tf_op jit(solution)/shard_map/ppermute | solution.py:868
  483.8 14.3 %collective-permute-done.56.refs_4_ = bf16[64,2048]{1,0:T(8,128)(2,1)S(1)} collective-permute-done((bf16[64,2048]{1,0:T(8,128)(2,1)S(1)}, bf16[64,2048]{1,0:T(8,128)(2,1)S(1)}, u32[]{:S(2)}, u32[]{:S(2)}) %collective-permute-start.56) | collective-permute-done | bytes 262176 | tf_op jit(solution)/shard_map/ppermute | solution.py:961
  502.9 5.3 attend_back.3
  519.3 8.5 %hidden_back.3 = (bf16[256,2048]{1,0:T(8,128)(2,1)S(1)}, f32[256,2048]{1,0:T(8,128)S(1)}, f32[2,2048]{1,0:T(2,128)S(1)}) custom-call(s32[3]{0:T(128)S(1)} %add_add_fusion.1.flag_ref, bf16[256,2048]{1,0:T(8,128)(2,1)S(1)} %get-tuple-element.337.refs_0_.refs_6_, bf16[2048,512]{1,0:T(8,128)(2,1)} %bitcast.27.refs_2_.refs_9_.refs_1_.refs_6_, ...), custom_call_target="tpu_custom_call" | custom-call | flops 14949999616 | tf_op jit(solution)/shard_map/hidden_back/pallas_call | solution.py:168
  541.0 7.5 collective-permute-done.62.refs_3_.refs_9_
  555.3 8.3 %hidden_back.4 = (bf16[256,2048]{1,0:T(8,128)(2,1)S(1)}, f32[256,2048]{1,0:T(8,128)S(1)}, f32[2,2048]{1,0:T(2,128)S(1)}) custom-call(s32[3]{0:T(128)S(1)} %add_add_fusion.1.flag_ref, bf16[256,2048]{1,0:T(8,128)(2,1)S(1)} %get-tuple-element.351.refs_0_.refs_7_, bf16[2048,512]{1,0:T(8,128)(2,1)} %bitcast.27.refs_2_.refs_9_.refs_1_.refs_6_, ...), custom_call_target="tpu_custom_call" | custom-call | flops 14949999616 | tf_op jit(solution)/shard_map/hidden_back/pallas_call | solution.py:168
  563.7 6.1 project_back.9
  573.6 13.5 %weight_sums.3 = (bf16[2560,1024]{1,0:T(8,128)(2,1)S(1)}, bf16[2560,1024]{1,0:T(8,128)(2,1)S(1)}) custom-call(s32[3]{0:T(128)S(1)} %add_add_fusion.3.flag_ref, bf16[256,2048]{1,0:T(8,128)(2,1)S(1)} %copy-done.126, bf16[256,2048]{1,0:T(8,128)(2,1)S(1)} %copy-done.129, bf16[256,2048]{1,0:T(8,128)(2,1)S(1)} %copy-done.59, bf16[256,512]{1,0:T(8,128)(2,1)S(1)} %copy-done.197, ...), custom_call_target="tpu_custom_call" | custom-call | flops 18400000000 | tf_op jit(solution)/shard_map/weight_sums/pallas_call | solution.py:168
  610.6 8.7 %hidden_back.5 = (bf16[256,2048]{1,0:T(8,128)(2,1)S(1)}, f32[256,2048]{1,0:T(8,128)S(1)}, f32[2,2048]{1,0:T(2,128)S(1)}) custom-call(s32[3]{0:T(128)S(1)} %add_add_fusion.1.flag_ref, bf16[256,2048]{1,0:T(8,128)(2,1)S(1)} %copy-done.123, bf16[2048,512]{1,0:T(8,128)(2,1)} %bitcast.27.refs_2_.refs_9_.refs_1_.refs_6_, ...), custom_call_target="tpu_custom_call" | custom-call | flops 14949999616 | tf_op jit(solution)/shard_map/hidden_back/pallas_call | solution.py:168
  619.3 12.9 %collective-permute-done.70.refs_2_ = bf16[1024,512]{1,0:T(8,128)(2,1)S(1)} collective-permute-done((bf16[1024,512]{1,0:T(8,128)(2,1)S(1)}, bf16[1024,512]{1,0:T(8,128)(2,1)S(1)}, u32[]{:S(2)}, u32[]{:S(2)}) %collective-permute-start.70) | collective-permute-done | bytes 1048608 | tf_op jit(solution)/shard_map/ppermute | solution.py:868
  632.3 10.9 %collective-permute-done.69.refs_3_ = bf16[1,2,2,256,256]{4,3,2,1,0:T(8,128)(2,1)S(1)} collective-permute-done((bf16[1,2,2,256,256]{4,3,2,1,0:T(8,128)(2,1)S(1)}, bf16[1,2,2,256,256]{4,3,2,1,0:T(8,128)(2,1)S(1)}, u32[]{:S(2)}, u32[]{:S(2)}) %collective-permute-start.69) | collective-permute-done | bytes 524320 | tf_op jit(solution)/shard_map/ppermute | solution.py:989
  651.4 10.1 %weight_sums.4 = (bf16[1024,1536]{1,0:T(8,128)(2,1)S(1)}, bf16[1024,1536]{1,0:T(8,128)(2,1)}) custom-call(s32[3]{0:T(128)S(1)} %add_add_fusion.3.flag_ref, bf16[256,2048]{1,0:T(8,128)(2,1)S(1)} %copy-done.133, bf16[256,2048]{1,0:T(8,128)(2,1)S(1)} %copy-done.141, bf16[256,2048]{1,0:T(8,128)(2,1)S(1)} %copy-done.143, bf16[256,1536]{1,0:T(8,128)(2,1)S(1)} %copy-done.191, ...), custom_call_target="tpu_custom_call" | custom-call | flops 18400000000 | tf_op jit(solution)/shard_map/weight_sums/pallas_call | solution.py:168
  661.6 6.5 collective-permute-done.71.refs_4_
  671.2 10.0 %weight_sums.5 = (bf16[1024,2048]{1,0:T(8,128)(2,1)S(1)}, bf16[1024,2048]{1,0:T(8,128)(2,1)S(1)}) custom-call(s32[3]{0:T(128)S(1)} %add_add_fusion.3.flag_ref, bf16[256,2048]{1,0:T(8,128)(2,1)S(1)} %copy-done.131, bf16[256,2048]{1,0:T(8,128)(2,1)S(1)} %copy-done.137, bf16[256,2048]{1,0:T(8,128)(2,1)S(1)} %copy-done.139, bf16[256,2048]{1,0:T(8,128)(2,1)S(1)} %copy-done.218, ...), custom_call_target="tpu_custom_call" | custom-call | flops 18400000000 | tf_op jit(solution)/shard_map/weight_sums/pallas_call | solution.py:168
  694.9 34.0 %collective-permute-done.80.refs_9_ = f32[4,512]{1,0:T(4,128)S(1)} collective-permute-done((f32[4,512]{1,0:T(4,128)S(1)}, f32[4,512]{1,0:T(4,128)S(1)}, u32[]{:S(2)}, u32[]{:S(2)}) %collective-permute-start.80) | collective-permute-done | bytes 8224 | tf_op jit(solution)/shard_map/ppermute | solution.py:868
  753.5 5.8 copy.113
  761.6 21.1 %collective-permute-done.82 = bf16[3,64,2048]{2,1,0:T(8,128)(2,1)} collective-permute-done((bf16[3,64,2048]{2,1,0:T(8,128)(2,1)}, bf16[3,64,2048]{2,1,0:T(8,128)(2,1)}, u32[]{:S(2)}, u32[]{:S(2)}) %collective-permute-start.82) | collective-permute-done | bytes 786464 | tf_op jit(solution)/shard_map/ppermute | solution.py:868
  (868 shorter events, 339.8 us)
Async XLA Ops:
  3.8 26.4 %collective-permute-start = (bf16[256,2048]{1,0:T(8,128)(2,1)}, bf16[256,2048]{1,0:T(8,128)(2,1)}, u32[]{:S(2)}, u32[]{:S(2)}) collective-permute-start(bf16[256,2048]{1,0:T(8,128)(2,1)} %get-tuple-element.473), channel_id=1, source_target_pairs={{0,8},{4,12},{8,0},{12,4},{16,24},{20,28},{24,16},{28,20},{1,9},{5... | collective-permute-start | bytes 3145736 | tf_op jit(solution)/shard_map/ppermute | solution.py:868
  30.2 72.2 %collective-permute-start.4 = (bf16[528,2048]{1,0:T(8,128)(2,1)S(1)}, bf16[528,2048]{1,0:T(8,128)(2,1)S(1)}, u32[]{:S(2)}, u32[]{:S(2)}) collective-permute-start(bf16[528,2048]{1,0:T(8,128)(2,1)S(1)} %get-tuple-element.221), channel_id=1, source_target_pairs={{0,8},{4,12},{8,0},{12,4},{16,24},{20,28},{24,16},{28,20},{1,9},{5... | collective-permute-start | bytes 6488072 | tf_op jit(solution)/shard_map/ppermute | solution.py:868
  32.0 68.9 %collective-permute-start.5 = (bf16[256,2048]{1,0:T(8,128)(2,1)S(1)}, bf16[256,2048]{1,0:T(8,128)(2,1)S(1)}, u32[]{:S(2)}, u32[]{:S(2)}) collective-permute-start(bf16[256,2048]{1,0:T(8,128)(2,1)S(1)} %get-tuple-element.222), channel_id=1, source_target_pairs={{0,8},{4,12},{8,0},{12,4},{16,24},{20,28},{24,16},{28,20},{1,9},{5... | collective-permute-start | bytes 3145736 | tf_op jit(solution)/shard_map/ppermute | solution.py:868
  32.3 70.4 %collective-permute-start.1 = (bf16[3,64,2048]{2,1,0:T(8,128)(2,1)S(1)}, bf16[3,64,2048]{2,1,0:T(8,128)(2,1)S(1)}, u32[]{:S(2)}, u32[]{:S(2)}) collective-permute-start(bf16[3,64,2048]{2,1,0:T(8,128)(2,1)S(1)} %get-tuple-element.220.refs_3_.refs_0_.refs_1_), channel_id=1, source_target_pairs={{0,2},{1,3},{2,0},{3,1},{16,18},{17,19},{18,16},{19,17},{4,6},{5,7... | collective-permute-start | bytes 2359304 | tf_op jit(solution)/shard_map/ppermute | solution.py:868
  35.1 67.6 %collective-permute-start.2 = (bf16[3,64,2048]{2,1,0:T(8,128)(2,1)S(1)}, bf16[3,64,2048]{2,1,0:T(8,128)(2,1)S(1)}, u32[]{:S(2)}, u32[]{:S(2)}) collective-permute-start(bf16[3,64,2048]{2,1,0:T(8,128)(2,1)S(1)} %get-tuple-element.220.refs_3_.refs_0_.refs_1_), channel_id=1, source_target_pairs={{0,1},{1,0},{2,3},{3,2},{16,17},{17,16},{18,19},{19,18},{4,5},{5,4... | collective-permute-start | bytes 2359304 | tf_op jit(solution)/shard_map/ppermute | solution.py:868
  36.7 66.0 %collective-permute-start.3 = (bf16[3,64,2048]{2,1,0:T(8,128)(2,1)S(1)}, bf16[3,64,2048]{2,1,0:T(8,128)(2,1)S(1)}, u32[]{:S(2)}, u32[]{:S(2)}) collective-permute-start(bf16[3,64,2048]{2,1,0:T(8,128)(2,1)S(1)} %get-tuple-element.220.refs_3_.refs_0_.refs_1_), channel_id=1, source_target_pairs={{0,3},{1,2},{2,1},{3,0},{16,19},{17,18},{18,17},{19,16},{4,7},{5,6... | collective-permute-start | bytes 2359304 | tf_op jit(solution)/shard_map/ppermute | solution.py:868
  106.0 74.8 %collective-permute-start.15 = (bf16[2048,512]{1,0:T(8,128)(2,1)}, bf16[2048,512]{1,0:T(8,128)(2,1)}, u32[]{:S(2)}, u32[]{:S(2)}) collective-permute-start(bf16[2048,512]{1,0:T(8,128)(2,1)} %bitcast.27.refs_2_.refs_9_.refs_1_.refs_6_), channel_id=1, source_target_pairs={{0,4},{4,0},{8,12},{12,8},{16,20},{20,16},{24,28},{28,24},{1,5},{5... | collective-permute-start | bytes 6291464 | tf_op jit(solution)/shard_map/ppermute | solution.py:868
  106.7 18.6 %collective-permute-start.9 = (bf16[512,2048]{1,0:T(8,128)(2,1)}, bf16[512,2048]{1,0:T(8,128)(2,1)S(1)}, u32[]{:S(2)}, u32[]{:S(2)}) collective-permute-start(bf16[512,2048]{1,0:T(8,128)(2,1)} %copy-done), channel_id=1, source_target_pairs={{0,4},{4,0},{8,12},{12,8},{16,20},{20,16},{24,28},{28,24},{1,5},{5... | collective-permute-start | bytes 6291464 | tf_op jit(solution)/shard_map/ppermute | solution.py:868
  125.3 22.0 %collective-permute-start.11 = (bf16[896,512]{1,0:T(8,128)(2,1)S(1)}, bf16[896,512]{1,0:T(8,128)(2,1)S(1)}, u32[]{:S(2)}, u32[]{:S(2)}) collective-permute-start(bf16[896,512]{1,0:T(8,128)(2,1)S(1)} %fence.36.refs_11_), channel_id=1, source_target_pairs={{0,8},{4,12},{8,0},{12,4},{16,24},{20,28},{24,16},{28,20},{1,9},{5... | collective-permute-start | bytes 2752520 | tf_op jit(solution)/shard_map/ppermute | solution.py:868
  147.4 20.2 %collective-permute-start.12 = (bf16[1,2,2,256,256]{4,3,2,1,0:T(8,128)(2,1)S(1)}, bf16[1,2,2,256,256]{4,3,2,1,0:T(8,128)(2,1)S(1)}, u32[]{:S(2)}, u32[]{:S(2)}) collective-permute-start(bf16[1,2,2,256,256]{4,3,2,1,0:T(8,128)(2,1)S(1)} %get-tuple-element.231.refs_5_.refs_1_.refs_8_), channel_id=1, source_target_pairs={{0,8},{4,12},{1,9},{5,13},{2,10},{6,14},{3,11},{7,15}} | collective-permute-start | bytes 1572872 | tf_op jit(solution)/shard_map/ppermute | solution.py:989
  150.7 24.2 %collective-permute-start.13 = (bf16[640,512]{1,0:T(8,128)(2,1)S(1)}, bf16[640,512]{1,0:T(8,128)(2,1)S(1)}, u32[]{:S(2)}, u32[]{:S(2)}) collective-permute-start(bf16[640,512]{1,0:T(8,128)(2,1)S(1)} %get-tuple-element.233), channel_id=1, source_target_pairs={{0,8},{4,12},{8,0},{12,4},{16,24},{20,28},{24,16},{28,20},{1,9},{5... | collective-permute-start | bytes 1966088 | tf_op jit(solution)/shard_map/ppermute | solution.py:868
  199.9 18.5 %collective-permute-start.19 = (bf16[2,2,2,256,256]{4,3,2,1,0:T(8,128)(2,1)S(1)}, bf16[2,2,2,256,256]{4,3,2,1,0:T(8,128)(2,1)S(1)}, u32[]{:S(2)}, u32[]{:S(2)}) collective-permute-start(bf16[2,2,2,256,256]{4,3,2,1,0:T(8,128)(2,1)S(1)} %get-tuple-element.246), channel_id=1, source_target_pairs={{0,4},{4,0},{8,12},{12,8},{1,5},{5,1},{9,13},{13,9},{2,6},{6,2},{1... | collective-permute-start | bytes 3145736 | tf_op jit(solution)/shard_map/ppermute | solution.py:868
  218.4 20.8 %collective-permute-start.21 = (bf16[1,2,2,256,256]{4,3,2,1,0:T(8,128)(2,1)S(1)}, bf16[1,2,2,256,256]{4,3,2,1,0:T(8,128)(2,1)S(1)}, u32[]{:S(2)}, u32[]{:S(2)}) collective-permute-start(bf16[1,2,2,256,256]{4,3,2,1,0:T(8,128)(2,1)S(1)} %get-tuple-element.250.refs_1_.refs_8_), channel_id=1, source_target_pairs={{0,8},{4,12},{1,9},{5,13},{2,10},{6,14},{3,11},{7,15}} | collective-permute-start | bytes 1572872 | tf_op jit(solution)/shard_map/ppermute | solution.py:989
  239.3 18.3 %collective-permute-start.24 = (bf16[2,2,2,256,256]{4,3,2,1,0:T(8,128)(2,1)S(1)}, bf16[2,2,2,256,256]{4,3,2,1,0:T(8,128)(2,1)S(1)}, u32[]{:S(2)}, u32[]{:S(2)}) collective-permute-start(bf16[2,2,2,256,256]{4,3,2,1,0:T(8,128)(2,1)S(1)} %get-tuple-element.254), channel_id=1, source_target_pairs={{0,4},{4,0},{8,12},{12,8},{1,5},{5,1},{9,13},{13,9},{2,6},{6,2},{1... | collective-permute-start | bytes 3145736 | tf_op jit(solution)/shard_map/ppermute | solution.py:868
  354.5 108.3 %collective-permute-start.49 = (bf16[128,2048]{1,0:T(8,128)(2,1)S(1)}, bf16[128,2048]{1,0:T(8,128)(2,1)S(1)}, u32[]{:S(2)}, u32[]{:S(2)}) collective-permute-start(bf16[128,2048]{1,0:T(8,128)(2,1)S(1)} %get-tuple-element.322), channel_id=1, source_target_pairs={{16,17},{17,16},{18,19},{19,18},{20,21},{21,20},{22,23},{23,22},{2... | collective-permute-start | bytes 1572872 | tf_op jit(solution)/shard_map/ppermute | solution.py:868
  355.4 107.3 %collective-permute-start.50 = (bf16[64,2048]{1,0:T(8,128)(2,1)S(1)}, bf16[64,2048]{1,0:T(8,128)(2,1)S(1)}, u32[]{:S(2)}, u32[]{:S(2)}) collective-permute-start(bf16[64,2048]{1,0:T(8,128)(2,1)S(1)} %get-tuple-element.323.refs_2_), channel_id=1, source_target_pairs={{16,0},{17,1},{18,2},{19,3},{20,4},{21,5},{22,6},{23,7},{24,8},{25... | collective-permute-start | bytes 786440 | tf_op jit(solution)/shard_map/ppermute | solution.py:961
  356.7 106.2 %collective-permute-start.51 = (bf16[1,2,2,256,256]{4,3,2,1,0:T(8,128)(2,1)S(1)}, bf16[1,2,2,256,256]{4,3,2,1,0:T(8,128)(2,1)S(1)}, u32[]{:S(2)}, u32[]{:S(2)}) collective-permute-start(bf16[1,2,2,256,256]{4,3,2,1,0:T(8,128)(2,1)S(1)} %get-tuple-element.324), channel_id=1, source_target_pairs={{24,16},{28,20},{25,17},{29,21},{26,18},{30,22},{27,19},{31,23}} | collective-permute-start | bytes 1572872 | tf_op jit(solution)/shard_map/ppermute | solution.py:989
  479.6 18.5 %collective-permute-start.55 = (bf16[128,2048]{1,0:T(8,128)(2,1)S(1)}, bf16[128,2048]{1,0:T(8,128)(2,1)S(1)}, u32[]{:S(2)}, u32[]{:S(2)}) collective-permute-start(bf16[128,2048]{1,0:T(8,128)(2,1)S(1)} %get-tuple-element.334), channel_id=1, source_target_pairs={{16,17},{17,16},{18,19},{19,18},{20,21},{21,20},{22,23},{23,22},{2... | collective-permute-start | bytes 1572872 | tf_op jit(solution)/shard_map/ppermute | solution.py:868
  549.9 19.9 %collective-permute-start.65 = (bf16[2,2,2,256,256]{4,3,2,1,0:T(8,128)(2,1)S(1)}, bf16[2,2,2,256,256]{4,3,2,1,0:T(8,128)(2,1)S(1)}, u32[]{:S(2)}, u32[]{:S(2)}) collective-permute-start(bf16[2,2,2,256,256]{4,3,2,1,0:T(8,128)(2,1)S(1)} %get-tuple-element.361), channel_id=1, source_target_pairs={{0,4},{4,0},{8,12},{12,8},{1,5},{5,1},{9,13},{13,9},{2,6},{6,2},{1... | collective-permute-start | bytes 3145736 | tf_op jit(solution)/shard_map/ppermute | solution.py:868
  551.8 19.2 %collective-permute-start.64 = (bf16[128,2048]{1,0:T(8,128)(2,1)S(1)}, bf16[128,2048]{1,0:T(8,128)(2,1)S(1)}, u32[]{:S(2)}, u32[]{:S(2)}) collective-permute-start(bf16[128,2048]{1,0:T(8,128)(2,1)S(1)} %get-tuple-element.357.refs_12_), channel_id=1, source_target_pairs={{0,1},{1,0},{2,3},{3,2},{4,5},{5,4},{6,7},{7,6},{8,9},{9,8},{10,11... | collective-permute-start | bytes 1572872 | tf_op jit(solution)/shard_map/ppermute | solution.py:868
  606.3 26.0 %collective-permute-start.70 = (bf16[1024,512]{1,0:T(8,128)(2,1)S(1)}, bf16[1024,512]{1,0:T(8,128)(2,1)S(1)}, u32[]{:S(2)}, u32[]{:S(2)}) collective-permute-start(bf16[1024,512]{1,0:T(8,128)(2,1)S(1)} %get-tuple-element.376.refs_12_), channel_id=1, source_target_pairs={{0,8},{4,12},{8,0},{12,4},{16,24},{20,28},{24,16},{28,20},{1,9},{5... | collective-permute-start | bytes 3145736 | tf_op jit(solution)/shard_map/ppermute | solution.py:868
  609.1 34.1 %collective-permute-start.69 = (bf16[1,2,2,256,256]{4,3,2,1,0:T(8,128)(2,1)S(1)}, bf16[1,2,2,256,256]{4,3,2,1,0:T(8,128)(2,1)S(1)}, u32[]{:S(2)}, u32[]{:S(2)}) collective-permute-start(bf16[1,2,2,256,256]{4,3,2,1,0:T(8,128)(2,1)S(1)} %get-tuple-element.475), channel_id=1, source_target_pairs={{8,0},{12,4},{9,1},{13,5},{10,2},{14,6},{11,3},{15,7}} | collective-permute-start | bytes 1572872 | tf_op jit(solution)/shard_map/ppermute | solution.py:989
  643.2 24.9 %collective-permute-start.71 = (bf16[1024,512]{1,0:T(8,128)(2,1)S(1)}, bf16[1024,512]{1,0:T(8,128)(2,1)S(1)}, u32[]{:S(2)}, u32[]{:S(2)}) collective-permute-start(bf16[1024,512]{1,0:T(8,128)(2,1)S(1)} %fence.64.refs_11_), channel_id=1, source_target_pairs={{0,8},{4,12},{8,0},{12,4},{16,24},{20,28},{24,16},{28,20},{1,9},{5... | collective-permute-start | bytes 3145736 | tf_op jit(solution)/shard_map/ppermute | solution.py:868
  668.2 18.7 %collective-permute-start.72 = (bf16[1024,1536]{1,0:T(8,128)(2,1)}, bf16[1024,1536]{1,0:T(8,128)(2,1)}, u32[]{:S(2)}, u32[]{:S(2)}) collective-permute-start(bf16[1024,1536]{1,0:T(8,128)(2,1)} %get-tuple-element.405), channel_id=1, source_target_pairs={{0,4},{4,0},{8,12},{12,8},{16,20},{20,16},{24,28},{28,24},{1,5},{5... | collective-permute-start | bytes 9437192 | tf_op jit(solution)/shard_map/ppermute | solution.py:868
  689.3 43.9 %collective-permute-start.77 = (bf16[1024,2048]{1,0:T(8,128)(2,1)S(1)}, bf16[1024,2048]{1,0:T(8,128)(2,1)S(1)}, u32[]{:S(2)}, u32[]{:S(2)}) collective-permute-start(bf16[1024,2048]{1,0:T(8,128)(2,1)S(1)} %get-tuple-element.417), channel_id=1, source_target_pairs={{0,4},{4,0},{8,12},{12,8},{16,20},{20,16},{24,28},{28,24},{1,5},{5... | collective-permute-start | bytes 12582920 | tf_op jit(solution)/shard_map/ppermute | solution.py:868
  689.3 39.6 %collective-permute-start.76 = (bf16[3,128,2048]{2,1,0:T(8,128)(2,1)S(1)}, bf16[3,128,2048]{2,1,0:T(8,128)(2,1)S(1)}, u32[]{:S(2)}, u32[]{:S(2)}) collective-permute-start(bf16[3,128,2048]{2,1,0:T(8,128)(2,1)S(1)} %get-tuple-element.416), channel_id=1, source_target_pairs={{16,17},{17,16},{18,19},{19,18},{20,21},{21,20},{22,23},{23,22},{2... | collective-permute-start | bytes 4718600 | tf_op jit(solution)/shard_map/ppermute | solution.py:868
  690.3 39.4 %collective-permute-start.79 = (bf16[3,128,2048]{2,1,0:T(8,128)(2,1)S(1)}, bf16[3,128,2048]{2,1,0:T(8,128)(2,1)S(1)}, u32[]{:S(2)}, u32[]{:S(2)}) collective-permute-start(bf16[3,128,2048]{2,1,0:T(8,128)(2,1)S(1)} %get-tuple-element.420), channel_id=1, source_target_pairs={{0,1},{1,0},{2,3},{3,2},{4,5},{5,4},{6,7},{7,6},{8,9},{9,8},{10,11... | collective-permute-start | bytes 4718600 | tf_op jit(solution)/shard_map/ppermute | solution.py:868
  692.7 40.5 %collective-permute-start.78 = (bf16[512,1536]{1,0:T(8,128)(2,1)S(1)}, bf16[512,1536]{1,0:T(8,128)(2,1)S(1)}, u32[]{:S(2)}, u32[]{:S(2)}) collective-permute-start(bf16[512,1536]{1,0:T(8,128)(2,1)S(1)} %get-tuple-element.419), channel_id=1, source_target_pairs={{0,8},{4,12},{8,0},{12,4},{16,24},{20,28},{24,16},{28,20},{1,9},{5... | collective-permute-start | bytes 4718600 | tf_op jit(solution)/shard_map/ppermute | solution.py:868
  693.4 35.6 %collective-permute-start.80 = (f32[4,512]{1,0:T(4,128)S(1)}, f32[4,512]{1,0:T(4,128)S(1)}, u32[]{:S(2)}, u32[]{:S(2)}) collective-permute-start(f32[4,512]{1,0:T(4,128)S(1)} %get-tuple-element.418.refs_4_), channel_id=1, source_target_pairs={{0,1},{1,0},{2,3},{3,2},{16,17},{17,16},{18,19},{19,18},{4,5},{5,4... | collective-permute-start | bytes 24584 | tf_op jit(solution)/shard_map/ppermute | solution.py:868
  744.0 48.3 %collective-permute-start.83 = (bf16[512,2048]{1,0:T(8,128)(2,1)}, bf16[512,2048]{1,0:T(8,128)(2,1)}, u32[]{:S(2)}, u32[]{:S(2)}) collective-permute-start(bf16[512,2048]{1,0:T(8,128)(2,1)} %get-tuple-element.430), channel_id=1, source_target_pairs={{0,8},{4,12},{8,0},{12,4},{16,24},{20,28},{24,16},{28,20},{1,9},{5... | collective-permute-start | bytes 6291464 | tf_op jit(solution)/shard_map/ppermute | solution.py:868
  744.3 38.4 %collective-permute-start.82 = (bf16[3,64,2048]{2,1,0:T(8,128)(2,1)}, bf16[3,64,2048]{2,1,0:T(8,128)(2,1)}, u32[]{:S(2)}, u32[]{:S(2)}) collective-permute-start(bf16[3,64,2048]{2,1,0:T(8,128)(2,1)} %get-tuple-element.427), channel_id=1, source_target_pairs={{0,2},{1,3},{2,0},{3,1},{4,6},{5,7},{6,4},{7,5},{8,10},{9,11},{10,... | collective-permute-start | bytes 2359304 | tf_op jit(solution)/shard_map/ppermute | solution.py:868
  759.3 25.4 %collective-permute-start.81 = (bf16[3,64,2048]{2,1,0:T(8,128)(2,1)S(1)}, bf16[3,64,2048]{2,1,0:T(8,128)(2,1)S(1)}, u32[]{:S(2)}, u32[]{:S(2)}) collective-permute-start(bf16[3,64,2048]{2,1,0:T(8,128)(2,1)S(1)} %get-tuple-element.426), channel_id=1, source_target_pairs={{16,18},{17,19},{18,16},{19,17},{20,22},{21,23},{22,20},{23,21},{2... | collective-permute-start | bytes 2359304 | tf_op jit(solution)/shard_map/ppermute | solution.py:868
  (298 other events, 3593.8 us)

commit v2 on v1

--- a/solution.py
+++ b/solution.py
@@ -1358,18 +1358,22 @@
         [wide_near(branch_sums)], [lambda: run_attend_back(2), lambda: run_project_back(0, 1)]
     )
     slot([], [lambda: run_fold(branch_sums)])
-    cut = [0, hidden // 2, hidden, hidden + across_units]
+    cut = [0, 3 * hidden // 8, 7 * hidden // 8, hidden + across_units]
     slot(
         [wide_far(branch_sums, cut[0], cut[1]), pair_grad_both(0, 2)],
         [lambda: run_hidden_back(2)],
     )
+
+    def stacked(chosen):
+        keep, send = zip(*(k.blocks for k in chosen))
+        return SimpleNamespace(keep=jnp.stack(keep), send=jnp.stack(send))
+
+    outs = [stacked(a[:last])]
     slot(
-        [wide_far(branch_sums, cut[1], cut[2])],
+        [wide_far(branch_sums, cut[1], cut[2]), last_near(outs[0], 0)],
         [lambda: run_project_back(0, 2), run_triple_sums],
     )
-    outs = SimpleNamespace(
-        keep=jnp.stack([k.blocks[0] for k in a]), send=jnp.stack([k.blocks[1] for k in a])
-    )
+    outs.append(stacked(a[last:]))
 
     def side_of(mades):
         return sum(
@@ -1418,6 +1422,7 @@
             wide_near(triple_sums),
             wide_far(branch_sums, cut[2], cut[3]),
             (side.all, side_ctx),
+            last_near(outs[1], 0),
         ],
         [run_expand_sums, run_final_branch],
     )
@@ -1426,7 +1431,7 @@
         [
             wide_far(triple_sums, 0, depth),
             wide_near(expand_sums),
-            last_near(outs, 0),
+            last_far(outs[0], 0),
             last_near(finals, 1),
             (side.all, side_near),
         ]
@@ -1435,7 +1440,7 @@
     slot(
         [
             wide_far(expand_sums, 0, depth),
-            last_far(outs, 0),
+            last_far(outs[1], 0),
             last_far(finals, 1),
             (side.all, side_far),
             held_back(triple_sums, 0),
@@ -1461,11 +1466,16 @@
             for m in range(micros)
         ]
     )
-    own_rows = jnp.stack(of("rows", 0))
+    own_sums = [out.keep.astype(f32) + out.came.astype(f32) for out in outs]
+    own_entries = [
+        norm_back(jnp.stack([k.rows for k in chosen]), total, entering)
+        for chosen, total, entering in (
+            (a[:last], own_sums[0], inputs[:last]),
+            (a[last:], own_sums[1], inputs[last:]),
+        )
+    ]
     entry_grads = jnp.where(
-        first_section,
-        norm_back(own_rows, outs.keep.astype(f32) + outs.came.astype(f32), inputs),
-        jnp.stack(of("given", 1)),
+        first_section, jnp.concatenate(own_entries, axis=0), jnp.stack(of("given", 1))
     )
     gain_grads = jnp.stack([side.all[0], side.all[2]])
     bias_grads = jnp.stack([side.all[1], side.all[3]])

time: 808 us -> 818 us (1.012)
    ppermute x67 -> x69, starting transfers between devices: 94 us -> 101 us  [hop(): return lax.ppermute(array, ('pipe', axis), pairs)]
    unnamed x500 -> x496, local copies, waits for them, and re-layouts: 56 us -> 59.5 us
    ppermute x67 -> x69, waiting for transfers between devices: 228 us -> 227 us  [hop(): return lax.ppermute(array, ('pipe', axis), pairs)]
  transfers between devices with their start and end apart: 85 -> 87, of which waited for: 34 -> 38; matrix products, arithmetic and copies ran while one was open for 8% -> 7% of each run, Pallas kernels for 20% -> 20%
where the time goes in v2:
time: 818 us; the launch traced here: 807 us
  waiting for transfers between devices  378 us (46%)
  Pallas kernels  169 us (21%)
  starting transfers between devices  132 us (16%)
  local copies, waits for them, and re-layouts  81.4 us (10%)
  other arithmetic  40.9 us (5%)
    ppermute x69, waiting for transfers between devices, hop(): return lax.ppermute(array, ('pipe', axis), pairs)  227 us
    pallas_call x40, Pallas kernels, run(): pl.pallas_call(body, grid=grid, in_specs=[spec for spec, _ in in_specs],...  169 us
    ppermute x6, waiting for transfers between devices, across(): return lax.ppermute(array, ('pipe', 'tp'), pairs)  136 us
    ppermute x69, starting transfers between devices, hop(): return lax.ppermute(array, ('pipe', axis), pairs)  101 us
    unnamed x496, local copies, waits for them, and re-layouts  59.5 us
    ppermute x12, starting transfers between devices, one_way(): return lax.ppermute(array, ('pipe', 'ctx'), pairs)  21.4 us
  transfers between devices with their start and end apart: 87, of which 38 were waited for; matrix products, arithmetic and copies ran while one was open for 7% of the time, Pallas kernels for 20%

profile of v2, /device:TPU:0, one launch (start us, length us, event | category | flops | bytes accessed | tf_op | source)
XLA Modules:
  0.0 807.0 jit_solution(6161481146833845736)
XLA Ops:
  24.0 6.3 collective-permute-done.refs_3_
  37.8 63.2 %collective-permute-done.5.refs_5_ = bf16[256,2048]{1,0:T(8,128)(2,1)S(1)} collective-permute-done((bf16[256,2048]{1,0:T(8,128)(2,1)S(1)}, bf16[256,2048]{1,0:T(8,128)(2,1)S(1)}, u32[]{:S(2)}, u32[]{:S(2)}) %collective-permute-start.5) | collective-permute-done | bytes 1048608 | tf_op jit(solution)/shard_map/ppermute | solution.py:868
  116.1 9.3 %collective-permute-done.10.refs_8_ = bf16[512,512]{1,0:T(8,128)(2,1)S(1)} collective-permute-done((bf16[512,512]{1,0:T(8,128)(2,1)S(1)}, bf16[512,512]{1,0:T(8,128)(2,1)S(1)}, u32[]{:S(2)}, u32[]{:S(2)}) %collective-permute-start.10) | collective-permute-done | bytes 524320 | tf_op jit(solution)/shard_map/ppermute | solution.py:868
  168.6 6.4 collective-permute-done.13.refs_4_
  191.0 5.8 branch.4
  205.5 12.7 %collective-permute-done.18.refs_3_ = bf16[128,2048]{1,0:T(8,128)(2,1)S(1)} collective-permute-done((bf16[128,2048]{1,0:T(8,128)(2,1)S(1)}, bf16[128,2048]{1,0:T(8,128)(2,1)S(1)}, u32[]{:S(2)}, u32[]{:S(2)}) %collective-permute-start.18) | collective-permute-done | bytes 524320 | tf_op jit(solution)/shard_map/ppermute | solution.py:868
  231.1 5.8 branch.5
  245.2 6.2 collective-permute-done.22.refs_3_
  251.4 6.1 collective-permute-done.23.refs_4_
  265.9 6.5 branch.6
  298.1 9.2 %collective-permute-done.31.refs_5_ = bf16[64,2048]{1,0:T(8,128)(2,1)S(1)} collective-permute-done((bf16[64,2048]{1,0:T(8,128)(2,1)S(1)}, bf16[64,2048]{1,0:T(8,128)(2,1)S(1)}, u32[]{:S(2)}, u32[]{:S(2)}) %collective-permute-start.31) | collective-permute-done | bytes 262176 | tf_op jit(solution)/shard_map/ppermute | solution.py:868
  357.7 105.4 %collective-permute-done.50.refs_3_ = bf16[64,2048]{1,0:T(8,128)(2,1)S(1)} collective-permute-done((bf16[64,2048]{1,0:T(8,128)(2,1)S(1)}, bf16[64,2048]{1,0:T(8,128)(2,1)S(1)}, u32[]{:S(2)}, u32[]{:S(2)}) %collective-permute-start.50) | collective-permute-done | bytes 262176 | tf_op jit(solution)/shard_map/ppermute | solution.py:961
  469.0 10.4 %collective-permute-done.52.refs_5_ = bf16[64,2048]{1,0:T(8,128)(2,1)S(1)} collective-permute-done((bf16[64,2048]{1,0:T(8,128)(2,1)S(1)}, bf16[64,2048]{1,0:T(8,128)(2,1)S(1)}, u32[]{:S(2)}, u32[]{:S(2)}) %collective-permute-start.52) | collective-permute-done | bytes 262176 | tf_op jit(solution)/shard_map/ppermute | solution.py:868
  484.0 14.3 %collective-permute-done.56.refs_4_ = bf16[64,2048]{1,0:T(8,128)(2,1)S(1)} collective-permute-done((bf16[64,2048]{1,0:T(8,128)(2,1)S(1)}, bf16[64,2048]{1,0:T(8,128)(2,1)S(1)}, u32[]{:S(2)}, u32[]{:S(2)}) %collective-permute-start.56) | collective-permute-done | bytes 262176 | tf_op jit(solution)/shard_map/ppermute | solution.py:961
  519.5 8.5 %hidden_back.3 = (bf16[256,2048]{1,0:T(8,128)(2,1)S(1)}, f32[256,2048]{1,0:T(8,128)S(1)}, f32[2,2048]{1,0:T(2,128)S(1)}) custom-call(s32[3]{0:T(128)S(1)} %add_add_fusion.1.flag_ref, bf16[256,2048]{1,0:T(8,128)(2,1)S(1)} %get-tuple-element.340.refs_0_.refs_6_, bf16[2048,512]{1,0:T(8,128)(2,1)} %bitcast.27.refs_2_.refs_9_.refs_1_.refs_6_, ...), custom_call_target="tpu_custom_call" | custom-call | flops 14949999616 | tf_op jit(solution)/shard_map/hidden_back/pallas_call | solution.py:168
  541.3 7.5 collective-permute-done.62.refs_3_.refs_9_
  555.5 8.3 %hidden_back.4 = (bf16[256,2048]{1,0:T(8,128)(2,1)S(1)}, f32[256,2048]{1,0:T(8,128)S(1)}, f32[2,2048]{1,0:T(2,128)S(1)}) custom-call(s32[3]{0:T(128)S(1)} %add_add_fusion.1.flag_ref, bf16[256,2048]{1,0:T(8,128)(2,1)S(1)} %get-tuple-element.354.refs_0_.refs_7_, bf16[2048,512]{1,0:T(8,128)(2,1)} %bitcast.27.refs_2_.refs_9_.refs_1_.refs_6_, ...), custom_call_target="tpu_custom_call" | custom-call | flops 14949999616 | tf_op jit(solution)/shard_map/hidden_back/pallas_call | solution.py:168
  563.9 6.1 project_back.9
  574.4 13.5 %weight_sums.3 = (bf16[2560,1024]{1,0:T(8,128)(2,1)S(1)}, bf16[2560,1024]{1,0:T(8,128)(2,1)S(1)}) custom-call(s32[3]{0:T(128)S(1)} %add_add_fusion.3.flag_ref, bf16[256,2048]{1,0:T(8,128)(2,1)S(1)} %copy-done.126, bf16[256,2048]{1,0:T(8,128)(2,1)S(1)} %copy-done.129, bf16[256,2048]{1,0:T(8,128)(2,1)S(1)} %copy-done.60, bf16[256,512]{1,0:T(8,128)(2,1)S(1)} %copy-done.197, ...), custom_call_target="tpu_custom_call" | custom-call | flops 18400000000 | tf_op jit(solution)/shard_map/weight_sums/pallas_call | solution.py:168
  617.4 8.7 %hidden_back.5 = (bf16[256,2048]{1,0:T(8,128)(2,1)S(1)}, f32[256,2048]{1,0:T(8,128)S(1)}, f32[2,2048]{1,0:T(2,128)S(1)}) custom-call(s32[3]{0:T(128)S(1)} %add_add_fusion.1.flag_ref, bf16[256,2048]{1,0:T(8,128)(2,1)S(1)} %copy-done.123, bf16[2048,512]{1,0:T(8,128)(2,1)} %bitcast.27.refs_2_.refs_9_.refs_1_.refs_6_, ...), custom_call_target="tpu_custom_call" | custom-call | flops 14949999616 | tf_op jit(solution)/shard_map/hidden_back/pallas_call | solution.py:168
  632.9 10.9 %collective-permute-done.69.refs_4_ = bf16[1,2,2,256,256]{4,3,2,1,0:T(8,128)(2,1)S(1)} collective-permute-done((bf16[1,2,2,256,256]{4,3,2,1,0:T(8,128)(2,1)S(1)}, bf16[1,2,2,256,256]{4,3,2,1,0:T(8,128)(2,1)S(1)}, u32[]{:S(2)}, u32[]{:S(2)}) %collective-permute-start.69) | collective-permute-done | bytes 524320 | tf_op jit(solution)/shard_map/ppermute | solution.py:989
  644.0 5.8 project_back.11
  652.4 10.1 %weight_sums.4 = (bf16[1024,1536]{1,0:T(8,128)(2,1)S(1)}, bf16[1024,1536]{1,0:T(8,128)(2,1)}) custom-call(s32[3]{0:T(128)S(1)} %add_add_fusion.3.flag_ref, bf16[256,2048]{1,0:T(8,128)(2,1)S(1)} %copy-done.133, bf16[256,2048]{1,0:T(8,128)(2,1)S(1)} %copy-done.141, bf16[256,2048]{1,0:T(8,128)(2,1)S(1)} %copy-done.143, bf16[256,1536]{1,0:T(8,128)(2,1)S(1)} %copy-done.191, ...), custom_call_target="tpu_custom_call" | custom-call | flops 18400000000 | tf_op jit(solution)/shard_map/weight_sums/pallas_call | solution.py:168
  662.6 6.0 collective-permute-done.71.refs_5_
  668.6 8.0 collective-permute-done.72.refs_6_
  681.7 10.0 %weight_sums.5 = (bf16[1024,2048]{1,0:T(8,128)(2,1)S(1)}, bf16[1024,2048]{1,0:T(8,128)(2,1)S(1)}) custom-call(s32[3]{0:T(128)S(1)} %add_add_fusion.3.flag_ref, bf16[256,2048]{1,0:T(8,128)(2,1)S(1)} %copy-done.131, bf16[256,2048]{1,0:T(8,128)(2,1)S(1)} %copy-done.137, bf16[256,2048]{1,0:T(8,128)(2,1)S(1)} %copy-done.139, bf16[256,2048]{1,0:T(8,128)(2,1)S(1)} %copy-done.218, ...), custom_call_target="tpu_custom_call" | custom-call | flops 18400000000 | tf_op jit(solution)/shard_map/weight_sums/pallas_call | solution.py:168
  710.1 8.8 %collective-permute-done.82.refs_9_ = f32[4,512]{1,0:T(4,128)S(1)} collective-permute-done((f32[4,512]{1,0:T(4,128)S(1)}, f32[4,512]{1,0:T(4,128)S(1)}, u32[]{:S(2)}, u32[]{:S(2)}) %collective-permute-start.82) | collective-permute-done | bytes 8224 | tf_op jit(solution)/shard_map/ppermute | solution.py:868
  718.8 12.0 %collective-permute-done.81.refs_7_ = bf16[2,64,2048]{2,1,0:T(8,128)(2,1)S(1)} collective-permute-done((bf16[2,64,2048]{2,1,0:T(8,128)(2,1)S(1)}, bf16[2,64,2048]{2,1,0:T(8,128)(2,1)S(1)}, u32[]{:S(2)}, u32[]{:S(2)}) %collective-permute-start.81) | collective-permute-done | bytes 524320 | tf_op jit(solution)/shard_map/ppermute | solution.py:868
  733.5 11.4 %collective-permute-done.80.refs_5_.refs_4_ = bf16[512,1536]{1,0:T(8,128)(2,1)S(1)} collective-permute-done((bf16[512,1536]{1,0:T(8,128)(2,1)S(1)}, bf16[512,1536]{1,0:T(8,128)(2,1)S(1)}, u32[]{:S(2)}, u32[]{:S(2)}) %collective-permute-start.80) | collective-permute-done | bytes 1572896 | tf_op jit(solution)/shard_map/ppermute | solution.py:868
  762.8 5.9 copy.115
  774.1 8.8 %collective-permute-done.84 = bf16[1,64,2048]{2,1,0:T(8,128)(2,1)S(1)} collective-permute-done((bf16[1,64,2048]{2,1,0:T(8,128)(2,1)S(1)}, bf16[1,64,2048]{2,1,0:T(8,128)(2,1)S(1)}, u32[]{:S(2)}, u32[]{:S(2)}) %collective-permute-start.84) | collective-permute-done | bytes 262176 | tf_op jit(solution)/shard_map/ppermute | solution.py:868
  790.2 12.1 %collective-permute-done.85 = bf16[512,2048]{1,0:T(8,128)(2,1)} collective-permute-done((bf16[512,2048]{1,0:T(8,128)(2,1)}, bf16[512,2048]{1,0:T(8,128)(2,1)}, u32[]{:S(2)}, u32[]{:S(2)}) %collective-permute-start.85) | collective-permute-done | bytes 2097184 | tf_op jit(solution)/shard_map/ppermute | solution.py:868
  (879 shorter events, 371.6 us)
Async XLA Ops:
  3.9 26.4 %collective-permute-start = (bf16[256,2048]{1,0:T(8,128)(2,1)}, bf16[256,2048]{1,0:T(8,128)(2,1)}, u32[]{:S(2)}, u32[]{:S(2)}) collective-permute-start(bf16[256,2048]{1,0:T(8,128)(2,1)} %get-tuple-element.479), channel_id=1, source_target_pairs={{0,8},{4,12},{8,0},{12,4},{16,24},{20,28},{24,16},{28,20},{1,9},{5... | collective-permute-start | bytes 3145736 | tf_op jit(solution)/shard_map/ppermute | solution.py:868
  30.3 72.2 %collective-permute-start.4 = (bf16[528,2048]{1,0:T(8,128)(2,1)S(1)}, bf16[528,2048]{1,0:T(8,128)(2,1)S(1)}, u32[]{:S(2)}, u32[]{:S(2)}) collective-permute-start(bf16[528,2048]{1,0:T(8,128)(2,1)S(1)} %get-tuple-element.224), channel_id=1, source_target_pairs={{0,8},{4,12},{8,0},{12,4},{16,24},{20,28},{24,16},{28,20},{1,9},{5... | collective-permute-start | bytes 6488072 | tf_op jit(solution)/shard_map/ppermute | solution.py:868
  32.0 68.9 %collective-permute-start.5 = (bf16[256,2048]{1,0:T(8,128)(2,1)S(1)}, bf16[256,2048]{1,0:T(8,128)(2,1)S(1)}, u32[]{:S(2)}, u32[]{:S(2)}) collective-permute-start(bf16[256,2048]{1,0:T(8,128)(2,1)S(1)} %get-tuple-element.225), channel_id=1, source_target_pairs={{0,8},{4,12},{8,0},{12,4},{16,24},{20,28},{24,16},{28,20},{1,9},{5... | collective-permute-start | bytes 3145736 | tf_op jit(solution)/shard_map/ppermute | solution.py:868
  32.3 70.4 %collective-permute-start.1 = (bf16[3,64,2048]{2,1,0:T(8,128)(2,1)S(1)}, bf16[3,64,2048]{2,1,0:T(8,128)(2,1)S(1)}, u32[]{:S(2)}, u32[]{:S(2)}) collective-permute-start(bf16[3,64,2048]{2,1,0:T(8,128)(2,1)S(1)} %get-tuple-element.223.refs_3_.refs_0_.refs_1_), channel_id=1, source_target_pairs={{0,2},{1,3},{2,0},{3,1},{16,18},{17,19},{18,16},{19,17},{4,6},{5,7... | collective-permute-start | bytes 2359304 | tf_op jit(solution)/shard_map/ppermute | solution.py:868
  35.2 67.6 %collective-permute-start.2 = (bf16[3,64,2048]{2,1,0:T(8,128)(2,1)S(1)}, bf16[3,64,2048]{2,1,0:T(8,128)(2,1)S(1)}, u32[]{:S(2)}, u32[]{:S(2)}) collective-permute-start(bf16[3,64,2048]{2,1,0:T(8,128)(2,1)S(1)} %get-tuple-element.223.refs_3_.refs_0_.refs_1_), channel_id=1, source_target_pairs={{0,1},{1,0},{2,3},{3,2},{16,17},{17,16},{18,19},{19,18},{4,5},{5,4... | collective-permute-start | bytes 2359304 | tf_op jit(solution)/shard_map/ppermute | solution.py:868
  36.7 66.0 %collective-permute-start.3 = (bf16[3,64,2048]{2,1,0:T(8,128)(2,1)S(1)}, bf16[3,64,2048]{2,1,0:T(8,128)(2,1)S(1)}, u32[]{:S(2)}, u32[]{:S(2)}) collective-permute-start(bf16[3,64,2048]{2,1,0:T(8,128)(2,1)S(1)} %get-tuple-element.223.refs_3_.refs_0_.refs_1_), channel_id=1, source_target_pairs={{0,3},{1,2},{2,1},{3,0},{16,19},{17,18},{18,17},{19,16},{4,7},{5,6... | collective-permute-start | bytes 2359304 | tf_op jit(solution)/shard_map/ppermute | solution.py:868
  106.0 74.8 %collective-permute-start.15 = (bf16[2048,512]{1,0:T(8,128)(2,1)}, bf16[2048,512]{1,0:T(8,128)(2,1)}, u32[]{:S(2)}, u32[]{:S(2)}) collective-permute-start(bf16[2048,512]{1,0:T(8,128)(2,1)} %bitcast.27.refs_2_.refs_9_.refs_1_.refs_6_), channel_id=1, source_target_pairs={{0,4},{4,0},{8,12},{12,8},{16,20},{20,16},{24,28},{28,24},{1,5},{5... | collective-permute-start | bytes 6291464 | tf_op jit(solution)/shard_map/ppermute | solution.py:868
  106.8 18.6 %collective-permute-start.9 = (bf16[512,2048]{1,0:T(8,128)(2,1)}, bf16[512,2048]{1,0:T(8,128)(2,1)S(1)}, u32[]{:S(2)}, u32[]{:S(2)}) collective-permute-start(bf16[512,2048]{1,0:T(8,128)(2,1)} %copy-done), channel_id=1, source_target_pairs={{0,4},{4,0},{8,12},{12,8},{16,20},{20,16},{24,28},{28,24},{1,5},{5... | collective-permute-start | bytes 6291464 | tf_op jit(solution)/shard_map/ppermute | solution.py:868
  125.4 22.0 %collective-permute-start.11 = (bf16[896,512]{1,0:T(8,128)(2,1)S(1)}, bf16[896,512]{1,0:T(8,128)(2,1)S(1)}, u32[]{:S(2)}, u32[]{:S(2)}) collective-permute-start(bf16[896,512]{1,0:T(8,128)(2,1)S(1)} %fence.36.refs_11_), channel_id=1, source_target_pairs={{0,8},{4,12},{8,0},{12,4},{16,24},{20,28},{24,16},{28,20},{1,9},{5... | collective-permute-start | bytes 2752520 | tf_op jit(solution)/shard_map/ppermute | solution.py:868
  147.4 20.2 %collective-permute-start.12 = (bf16[1,2,2,256,256]{4,3,2,1,0:T(8,128)(2,1)S(1)}, bf16[1,2,2,256,256]{4,3,2,1,0:T(8,128)(2,1)S(1)}, u32[]{:S(2)}, u32[]{:S(2)}) collective-permute-start(bf16[1,2,2,256,256]{4,3,2,1,0:T(8,128)(2,1)S(1)} %get-tuple-element.234.refs_5_.refs_1_.refs_8_), channel_id=1, source_target_pairs={{0,8},{4,12},{1,9},{5,13},{2,10},{6,14},{3,11},{7,15}} | collective-permute-start | bytes 1572872 | tf_op jit(solution)/shard_map/ppermute | solution.py:989
  150.8 24.2 %collective-permute-start.13 = (bf16[640,512]{1,0:T(8,128)(2,1)S(1)}, bf16[640,512]{1,0:T(8,128)(2,1)S(1)}, u32[]{:S(2)}, u32[]{:S(2)}) collective-permute-start(bf16[640,512]{1,0:T(8,128)(2,1)S(1)} %get-tuple-element.236), channel_id=1, source_target_pairs={{0,8},{4,12},{8,0},{12,4},{16,24},{20,28},{24,16},{28,20},{1,9},{5... | collective-permute-start | bytes 1966088 | tf_op jit(solution)/shard_map/ppermute | solution.py:868
  199.9 18.5 %collective-permute-start.19 = (bf16[2,2,2,256,256]{4,3,2,1,0:T(8,128)(2,1)S(1)}, bf16[2,2,2,256,256]{4,3,2,1,0:T(8,128)(2,1)S(1)}, u32[]{:S(2)}, u32[]{:S(2)}) collective-permute-start(bf16[2,2,2,256,256]{4,3,2,1,0:T(8,128)(2,1)S(1)} %get-tuple-element.249), channel_id=1, source_target_pairs={{0,4},{4,0},{8,12},{12,8},{1,5},{5,1},{9,13},{13,9},{2,6},{6,2},{1... | collective-permute-start | bytes 3145736 | tf_op jit(solution)/shard_map/ppermute | solution.py:868
  218.5 20.8 %collective-permute-start.21 = (bf16[1,2,2,256,256]{4,3,2,1,0:T(8,128)(2,1)S(1)}, bf16[1,2,2,256,256]{4,3,2,1,0:T(8,128)(2,1)S(1)}, u32[]{:S(2)}, u32[]{:S(2)}) collective-permute-start(bf16[1,2,2,256,256]{4,3,2,1,0:T(8,128)(2,1)S(1)} %get-tuple-element.253.refs_1_.refs_8_), channel_id=1, source_target_pairs={{0,8},{4,12},{1,9},{5,13},{2,10},{6,14},{3,11},{7,15}} | collective-permute-start | bytes 1572872 | tf_op jit(solution)/shard_map/ppermute | solution.py:989
  354.6 108.5 %collective-permute-start.49 = (bf16[128,2048]{1,0:T(8,128)(2,1)S(1)}, bf16[128,2048]{1,0:T(8,128)(2,1)S(1)}, u32[]{:S(2)}, u32[]{:S(2)}) collective-permute-start(bf16[128,2048]{1,0:T(8,128)(2,1)S(1)} %get-tuple-element.325), channel_id=1, source_target_pairs={{16,17},{17,16},{18,19},{19,18},{20,21},{21,20},{22,23},{23,22},{2... | collective-permute-start | bytes 1572872 | tf_op jit(solution)/shard_map/ppermute | solution.py:868
  355.5 107.5 %collective-permute-start.50 = (bf16[64,2048]{1,0:T(8,128)(2,1)S(1)}, bf16[64,2048]{1,0:T(8,128)(2,1)S(1)}, u32[]{:S(2)}, u32[]{:S(2)}) collective-permute-start(bf16[64,2048]{1,0:T(8,128)(2,1)S(1)} %get-tuple-element.326.refs_2_), channel_id=1, source_target_pairs={{16,0},{17,1},{18,2},{19,3},{20,4},{21,5},{22,6},{23,7},{24,8},{25... | collective-permute-start | bytes 786440 | tf_op jit(solution)/shard_map/ppermute | solution.py:961
  356.8 106.4 %collective-permute-start.51 = (bf16[1,2,2,256,256]{4,3,2,1,0:T(8,128)(2,1)S(1)}, bf16[1,2,2,256,256]{4,3,2,1,0:T(8,128)(2,1)S(1)}, u32[]{:S(2)}, u32[]{:S(2)}) collective-permute-start(bf16[1,2,2,256,256]{4,3,2,1,0:T(8,128)(2,1)S(1)} %get-tuple-element.327), channel_id=1, source_target_pairs={{24,16},{28,20},{25,17},{29,21},{26,18},{30,22},{27,19},{31,23}} | collective-permute-start | bytes 1572872 | tf_op jit(solution)/shard_map/ppermute | solution.py:989
  479.8 18.5 %collective-permute-start.55 = (bf16[128,2048]{1,0:T(8,128)(2,1)S(1)}, bf16[128,2048]{1,0:T(8,128)(2,1)S(1)}, u32[]{:S(2)}, u32[]{:S(2)}) collective-permute-start(bf16[128,2048]{1,0:T(8,128)(2,1)S(1)} %get-tuple-element.337), channel_id=1, source_target_pairs={{16,17},{17,16},{18,19},{19,18},{20,21},{21,20},{22,23},{23,22},{2... | collective-permute-start | bytes 1572872 | tf_op jit(solution)/shard_map/ppermute | solution.py:868
  550.1 20.8 %collective-permute-start.65 = (bf16[2,2,2,256,256]{4,3,2,1,0:T(8,128)(2,1)S(1)}, bf16[2,2,2,256,256]{4,3,2,1,0:T(8,128)(2,1)S(1)}, u32[]{:S(2)}, u32[]{:S(2)}) collective-permute-start(bf16[2,2,2,256,256]{4,3,2,1,0:T(8,128)(2,1)S(1)} %get-tuple-element.364), channel_id=1, source_target_pairs={{0,4},{4,0},{8,12},{12,8},{1,5},{5,1},{9,13},{13,9},{2,6},{6,2},{1... | collective-permute-start | bytes 3145736 | tf_op jit(solution)/shard_map/ppermute | solution.py:868
  552.1 19.7 %collective-permute-start.64 = (bf16[128,2048]{1,0:T(8,128)(2,1)S(1)}, bf16[128,2048]{1,0:T(8,128)(2,1)S(1)}, u32[]{:S(2)}, u32[]{:S(2)}) collective-permute-start(bf16[128,2048]{1,0:T(8,128)(2,1)S(1)} %get-tuple-element.360.refs_12_), channel_id=1, source_target_pairs={{0,1},{1,0},{2,3},{3,2},{4,5},{5,4},{6,7},{7,6},{8,9},{9,8},{10,11... | collective-permute-start | bytes 1572872 | tf_op jit(solution)/shard_map/ppermute | solution.py:868
  612.5 20.4 %collective-permute-start.70 = (bf16[768,512]{1,0:T(8,128)(2,1)S(1)}, bf16[768,512]{1,0:T(8,128)(2,1)S(1)}, u32[]{:S(2)}, u32[]{:S(2)}) collective-permute-start(bf16[768,512]{1,0:T(8,128)(2,1)S(1)} %get-tuple-element.379.refs_12_), channel_id=1, source_target_pairs={{0,8},{4,12},{8,0},{12,4},{16,24},{20,28},{24,16},{28,20},{1,9},{5... | collective-permute-start | bytes 2359304 | tf_op jit(solution)/shard_map/ppermute | solution.py:868
  615.2 28.6 %collective-permute-start.69 = (bf16[1,2,2,256,256]{4,3,2,1,0:T(8,128)(2,1)S(1)}, bf16[1,2,2,256,256]{4,3,2,1,0:T(8,128)(2,1)S(1)}, u32[]{:S(2)}, u32[]{:S(2)}) collective-permute-start(bf16[1,2,2,256,256]{4,3,2,1,0:T(8,128)(2,1)S(1)} %get-tuple-element.481), channel_id=1, source_target_pairs={{8,0},{12,4},{9,1},{13,5},{10,2},{14,6},{11,3},{15,7}} | collective-permute-start | bytes 1572872 | tf_op jit(solution)/shard_map/ppermute | solution.py:989
  643.8 24.8 %collective-permute-start.71 = (bf16[1024,512]{1,0:T(8,128)(2,1)S(1)}, bf16[1024,512]{1,0:T(8,128)(2,1)S(1)}, u32[]{:S(2)}, u32[]{:S(2)}) collective-permute-start(bf16[1024,512]{1,0:T(8,128)(2,1)S(1)} %get-tuple-element.395.refs_11_), channel_id=1, source_target_pairs={{0,8},{4,12},{8,0},{12,4},{16,24},{20,28},{24,16},{28,20},{1,9},{5... | collective-permute-start | bytes 3145736 | tf_op jit(solution)/shard_map/ppermute | solution.py:868
  649.9 26.7 %collective-permute-start.72 = (bf16[2,128,2048]{2,1,0:T(8,128)(2,1)S(1)}, bf16[2,128,2048]{2,1,0:T(8,128)(2,1)S(1)}, u32[]{:S(2)}, u32[]{:S(2)}) collective-permute-start(bf16[2,128,2048]{2,1,0:T(8,128)(2,1)S(1)} %get-tuple-element.407), channel_id=1, source_target_pairs={{0,1},{1,0},{2,3},{3,2},{4,5},{5,4},{6,7},{7,6},{8,9},{9,8},{10,11... | collective-permute-start | bytes 3145736 | tf_op jit(solution)/shard_map/ppermute | solution.py:868
  676.7 18.6 %collective-permute-start.75 = (f32[4,1024]{1,0:T(4,128)S(1)}, f32[4,1024]{1,0:T(4,128)S(1)}, u32[]{:S(2)}, u32[]{:S(2)}) collective-permute-start(f32[4,1024]{1,0:T(4,128)S(1)} %slice.427), channel_id=1, source_target_pairs={{0,4},{4,0},{8,12},{12,8},{16,20},{20,16},{24,28},{28,24},{1,5},{5... | collective-permute-start | bytes 49160 | tf_op jit(solution)/shard_map/ppermute | solution.py:868
  676.8 22.3 %collective-permute-start.73 = (bf16[1024,1536]{1,0:T(8,128)(2,1)}, bf16[1024,1536]{1,0:T(8,128)(2,1)}, u32[]{:S(2)}, u32[]{:S(2)}) collective-permute-start(bf16[1024,1536]{1,0:T(8,128)(2,1)} %get-tuple-element.413), channel_id=1, source_target_pairs={{0,4},{4,0},{8,12},{12,8},{16,20},{20,16},{24,28},{28,24},{1,5},{5... | collective-permute-start | bytes 9437192 | tf_op jit(solution)/shard_map/ppermute | solution.py:868
  677.3 21.8 %collective-permute-start.74 = (bf16[768,512]{1,0:T(8,128)(2,1)S(1)}, bf16[768,512]{1,0:T(8,128)(2,1)S(1)}, u32[]{:S(2)}, u32[]{:S(2)}) collective-permute-start(bf16[768,512]{1,0:T(8,128)(2,1)S(1)} %get-tuple-element.414), channel_id=1, source_target_pairs={{0,8},{4,12},{8,0},{12,4},{16,24},{20,28},{24,16},{28,20},{1,9},{5... | collective-permute-start | bytes 2359304 | tf_op jit(solution)/shard_map/ppermute | solution.py:868
  679.0 20.0 %collective-permute-start.77 = (bf16[1,128,2048]{2,1,0:T(8,128)(2,1)}, bf16[1,128,2048]{2,1,0:T(8,128)(2,1)S(1)}, u32[]{:S(2)}, u32[]{:S(2)}) collective-permute-start(bf16[1,128,2048]{2,1,0:T(8,128)(2,1)} %get-tuple-element.415), channel_id=1, source_target_pairs={{0,1},{1,0},{2,3},{3,2},{4,5},{5,4},{6,7},{7,6},{8,9},{9,8},{10,11... | collective-permute-start | bytes 1572872 | tf_op jit(solution)/shard_map/ppermute | solution.py:868
  701.6 43.2 %collective-permute-start.79 = (bf16[1024,2048]{1,0:T(8,128)(2,1)S(1)}, bf16[1024,2048]{1,0:T(8,128)(2,1)S(1)}, u32[]{:S(2)}, u32[]{:S(2)}) collective-permute-start(bf16[1024,2048]{1,0:T(8,128)(2,1)S(1)} %get-tuple-element.425), channel_id=1, source_target_pairs={{0,4},{4,0},{8,12},{12,8},{16,20},{20,16},{24,28},{28,24},{1,5},{5... | collective-permute-start | bytes 12582920 | tf_op jit(solution)/shard_map/ppermute | solution.py:868
  703.5 27.3 %collective-permute-start.81 = (bf16[2,64,2048]{2,1,0:T(8,128)(2,1)S(1)}, bf16[2,64,2048]{2,1,0:T(8,128)(2,1)S(1)}, u32[]{:S(2)}, u32[]{:S(2)}) collective-permute-start(bf16[2,64,2048]{2,1,0:T(8,128)(2,1)S(1)} %get-tuple-element.428), channel_id=1, source_target_pairs={{0,2},{1,3},{2,0},{3,1},{4,6},{5,7},{6,4},{7,5},{8,10},{9,11},{10,... | collective-permute-start | bytes 1572872 | tf_op jit(solution)/shard_map/ppermute | solution.py:868
  708.4 24.3 %collective-permute-start.78 = (bf16[3,128,2048]{2,1,0:T(8,128)(2,1)S(1)}, bf16[3,128,2048]{2,1,0:T(8,128)(2,1)S(1)}, u32[]{:S(2)}, u32[]{:S(2)}) collective-permute-start(bf16[3,128,2048]{2,1,0:T(8,128)(2,1)S(1)} %get-tuple-element.424), channel_id=1, source_target_pairs={{16,17},{17,16},{18,19},{19,18},{20,21},{21,20},{22,23},{23,22},{2... | collective-permute-start | bytes 4718600 | tf_op jit(solution)/shard_map/ppermute | solution.py:868
  709.5 35.3 %collective-permute-start.80 = (bf16[512,1536]{1,0:T(8,128)(2,1)S(1)}, bf16[512,1536]{1,0:T(8,128)(2,1)S(1)}, u32[]{:S(2)}, u32[]{:S(2)}) collective-permute-start(bf16[512,1536]{1,0:T(8,128)(2,1)S(1)} %get-tuple-element.427), channel_id=1, source_target_pairs={{0,8},{4,12},{8,0},{12,4},{16,24},{20,28},{24,16},{28,20},{1,9},{5... | collective-permute-start | bytes 4718600 | tf_op jit(solution)/shard_map/ppermute | solution.py:868
  756.7 45.6 %collective-permute-start.85 = (bf16[512,2048]{1,0:T(8,128)(2,1)}, bf16[512,2048]{1,0:T(8,128)(2,1)}, u32[]{:S(2)}, u32[]{:S(2)}) collective-permute-start(bf16[512,2048]{1,0:T(8,128)(2,1)} %get-tuple-element.436), channel_id=1, source_target_pairs={{0,8},{4,12},{8,0},{12,4},{16,24},{20,28},{24,16},{28,20},{1,9},{5... | collective-permute-start | bytes 6291464 | tf_op jit(solution)/shard_map/ppermute | solution.py:868
  (298 other events, 3565.6 us)

commit v3 on v1

--- a/solution.py
+++ b/solution.py
@@ -173,7 +173,7 @@
         out_shape=[struct for struct, _ in outs],
         scratch_shapes=scratch,
         compiler_params=pltpu.CompilerParams(
-            vmem_limit_bytes=int(held + (work + 4) * mebibyte)
+            vmem_limit_bytes=int(held + (work + 2) * mebibyte)
         ),
         cost_estimate=pl.CostEstimate(
             flops=int(took[name] * peak), bytes_accessed=0, transcendentals=0
@@ -1358,7 +1358,7 @@
         [wide_near(branch_sums)], [lambda: run_attend_back(2), lambda: run_project_back(0, 1)]
     )
     slot([], [lambda: run_fold(branch_sums)])
-    cut = [0, hidden // 2, hidden, hidden + across_units]
+    cut = [0, 3 * hidden // 8, 7 * hidden // 8, hidden + across_units]
     slot(
         [wide_far(branch_sums, cut[0], cut[1]), pair_grad_both(0, 2)],
         [lambda: run_hidden_back(2)],

time: 808 us -> 800 us (0.990)
    unnamed x500 -> x488, local copies, waits for them, and re-layouts: 56 us -> 55.5 us
where the time goes in v3:
time: 800 us; the launch traced here: 790 us
  waiting for transfers between devices  373 us (47%)
  Pallas kernels  167 us (21%)
  starting transfers between devices  125 us (16%)
  local copies, waits for them, and re-layouts  78.4 us (10%)
  other arithmetic  40.8 us (5%)
    ppermute x67, waiting for transfers between devices, hop(): return lax.ppermute(array, ('pipe', axis), pairs)  223 us
    pallas_call x40, Pallas kernels, run(): pl.pallas_call(body, grid=grid, in_specs=[spec for spec, _ in in_specs],...  167 us
    ppermute x6, waiting for transfers between devices, across(): return lax.ppermute(array, ('pipe', 'tp'), pairs)  136 us
    ppermute x67, starting transfers between devices, hop(): return lax.ppermute(array, ('pipe', axis), pairs)  93.8 us
    unnamed x488, local copies, waits for them, and re-layouts  55.5 us
    ppermute x12, starting transfers between devices, one_way(): return lax.ppermute(array, ('pipe', 'ctx'), pairs)  21.1 us
  transfers between devices with their start and end apart: 85, of which 34 were waited for; matrix products, arithmetic and copies ran while one was open for 8% of the time, Pallas kernels for 20%

profile of v3, /device:TPU:0, one launch (start us, length us, event | category | flops | bytes accessed | tf_op | source)
XLA Modules:
  0.0 789.6 jit_solution(494434030101602126)
XLA Ops:
  37.8 63.2 %collective-permute-done.5.refs_5_ = bf16[256,2048]{1,0:T(8,128)(2,1)S(1)} collective-permute-done((bf16[256,2048]{1,0:T(8,128)(2,1)S(1)}, bf16[256,2048]{1,0:T(8,128)(2,1)S(1)}, u32[]{:S(2)}, u32[]{:S(2)}) %collective-permute-start.5) | collective-permute-done | bytes 1048608 | tf_op jit(solution)/shard_map/ppermute | solution.py:868
  116.0 9.3 %collective-permute-done.10.refs_8_ = bf16[512,512]{1,0:T(8,128)(2,1)S(1)} collective-permute-done((bf16[512,512]{1,0:T(8,128)(2,1)S(1)}, bf16[512,512]{1,0:T(8,128)(2,1)S(1)}, u32[]{:S(2)}, u32[]{:S(2)}) %collective-permute-start.10) | collective-permute-done | bytes 524320 | tf_op jit(solution)/shard_map/ppermute | solution.py:868
  133.6 5.6 project.7
  150.7 5.5 expand.3
  156.3 5.6 expand.4
  161.9 5.5 expand.5
  168.5 6.3 collective-permute-done.13.refs_4_
  190.9 5.8 branch.4
  205.3 12.7 %collective-permute-done.18.refs_3_ = bf16[128,2048]{1,0:T(8,128)(2,1)S(1)} collective-permute-done((bf16[128,2048]{1,0:T(8,128)(2,1)S(1)}, bf16[128,2048]{1,0:T(8,128)(2,1)S(1)}, u32[]{:S(2)}, u32[]{:S(2)}) %collective-permute-start.18) | collective-permute-done | bytes 524320 | tf_op jit(solution)/shard_map/ppermute | solution.py:868
  231.0 5.8 branch.5
  245.1 6.2 collective-permute-done.22.refs_3_
  251.3 6.1 collective-permute-done.23.refs_4_
  264.9 6.6 branch.6
  298.2 9.2 %collective-permute-done.31.refs_5_ = bf16[64,2048]{1,0:T(8,128)(2,1)S(1)} collective-permute-done((bf16[64,2048]{1,0:T(8,128)(2,1)S(1)}, bf16[64,2048]{1,0:T(8,128)(2,1)S(1)}, u32[]{:S(2)}, u32[]{:S(2)}) %collective-permute-start.31) | collective-permute-done | bytes 262176 | tf_op jit(solution)/shard_map/ppermute | solution.py:868
  357.6 105.1 %collective-permute-done.50.refs_3_ = bf16[64,2048]{1,0:T(8,128)(2,1)S(1)} collective-permute-done((bf16[64,2048]{1,0:T(8,128)(2,1)S(1)}, bf16[64,2048]{1,0:T(8,128)(2,1)S(1)}, u32[]{:S(2)}, u32[]{:S(2)}) %collective-permute-start.50) | collective-permute-done | bytes 262176 | tf_op jit(solution)/shard_map/ppermute | solution.py:961
  468.6 10.5 %collective-permute-done.52.refs_5_ = bf16[64,2048]{1,0:T(8,128)(2,1)S(1)} collective-permute-done((bf16[64,2048]{1,0:T(8,128)(2,1)S(1)}, bf16[64,2048]{1,0:T(8,128)(2,1)S(1)}, u32[]{:S(2)}, u32[]{:S(2)}) %collective-permute-start.52) | collective-permute-done | bytes 262176 | tf_op jit(solution)/shard_map/ppermute | solution.py:868
  483.7 14.3 %collective-permute-done.56.refs_4_ = bf16[64,2048]{1,0:T(8,128)(2,1)S(1)} collective-permute-done((bf16[64,2048]{1,0:T(8,128)(2,1)S(1)}, bf16[64,2048]{1,0:T(8,128)(2,1)S(1)}, u32[]{:S(2)}, u32[]{:S(2)}) %collective-permute-start.56) | collective-permute-done | bytes 262176 | tf_op jit(solution)/shard_map/ppermute | solution.py:961
  502.9 5.3 attend_back.3
  519.2 8.5 %hidden_back.3 = (bf16[256,2048]{1,0:T(8,128)(2,1)S(1)}, f32[256,2048]{1,0:T(8,128)S(1)}, f32[2,2048]{1,0:T(2,128)S(1)}) custom-call(s32[3]{0:T(128)S(1)} %add_add_fusion.1.flag_ref, bf16[256,2048]{1,0:T(8,128)(2,1)S(1)} %get-tuple-element.337.refs_0_.refs_6_, bf16[2048,512]{1,0:T(8,128)(2,1)} %bitcast.27.refs_2_.refs_9_.refs_1_.refs_6_, ...), custom_call_target="tpu_custom_call" | custom-call | flops 14949999616 | tf_op jit(solution)/shard_map/hidden_back/pallas_call | solution.py:168
  540.9 7.5 collective-permute-done.62.refs_3_.refs_9_
  555.2 8.3 %hidden_back.4 = (bf16[256,2048]{1,0:T(8,128)(2,1)S(1)}, f32[256,2048]{1,0:T(8,128)S(1)}, f32[2,2048]{1,0:T(2,128)S(1)}) custom-call(s32[3]{0:T(128)S(1)} %add_add_fusion.1.flag_ref, bf16[256,2048]{1,0:T(8,128)(2,1)S(1)} %get-tuple-element.351.refs_0_.refs_7_, bf16[2048,512]{1,0:T(8,128)(2,1)} %bitcast.27.refs_2_.refs_9_.refs_1_.refs_6_, ...), custom_call_target="tpu_custom_call" | custom-call | flops 14949999616 | tf_op jit(solution)/shard_map/hidden_back/pallas_call | solution.py:168
  563.6 5.3 project_back.9
  572.8 13.5 %weight_sums.3 = (bf16[2560,1024]{1,0:T(8,128)(2,1)S(1)}, bf16[2560,1024]{1,0:T(8,128)(2,1)S(1)}) custom-call(s32[3]{0:T(128)S(1)} %add_add_fusion.3.flag_ref, bf16[256,2048]{1,0:T(8,128)(2,1)S(1)} %copy-done.119, bf16[256,2048]{1,0:T(8,128)(2,1)S(1)} %copy-done.122, bf16[256,2048]{1,0:T(8,128)(2,1)S(1)} %copy-done.58, bf16[256,512]{1,0:T(8,128)(2,1)S(1)} %copy-done.191, ...), custom_call_target="tpu_custom_call" | custom-call | flops 18400000000 | tf_op jit(solution)/shard_map/weight_sums/pallas_call | solution.py:168
  606.9 8.7 %hidden_back.5 = (bf16[256,2048]{1,0:T(8,128)(2,1)S(1)}, f32[256,2048]{1,0:T(8,128)S(1)}, f32[2,2048]{1,0:T(2,128)S(1)}) custom-call(s32[3]{0:T(128)S(1)} %add_add_fusion.1.flag_ref, bf16[256,2048]{1,0:T(8,128)(2,1)S(1)} %copy-done.116, bf16[2048,512]{1,0:T(8,128)(2,1)} %bitcast.27.refs_2_.refs_9_.refs_1_.refs_6_, ...), custom_call_target="tpu_custom_call" | custom-call | flops 14949999616 | tf_op jit(solution)/shard_map/hidden_back/pallas_call | solution.py:168
  616.6 6.2 collective-permute-done.70.refs_2_
  622.8 10.9 %collective-permute-done.69.refs_3_ = bf16[1,2,2,256,256]{4,3,2,1,0:T(8,128)(2,1)S(1)} collective-permute-done((bf16[1,2,2,256,256]{4,3,2,1,0:T(8,128)(2,1)S(1)}, bf16[1,2,2,256,256]{4,3,2,1,0:T(8,128)(2,1)S(1)}, u32[]{:S(2)}, u32[]{:S(2)}) %collective-permute-start.69) | collective-permute-done | bytes 524320 | tf_op jit(solution)/shard_map/ppermute | solution.py:989
  641.8 10.1 %weight_sums.4 = (bf16[1024,1536]{1,0:T(8,128)(2,1)S(1)}, bf16[1024,1536]{1,0:T(8,128)(2,1)}) custom-call(s32[3]{0:T(128)S(1)} %add_add_fusion.3.flag_ref, bf16[256,2048]{1,0:T(8,128)(2,1)S(1)} %copy-done.126, bf16[256,2048]{1,0:T(8,128)(2,1)S(1)} %copy-done.134, bf16[256,2048]{1,0:T(8,128)(2,1)S(1)} %copy-done.136, bf16[256,1536]{1,0:T(8,128)(2,1)S(1)} %copy-done.185, ...), custom_call_target="tpu_custom_call" | custom-call | flops 18400000000 | tf_op jit(solution)/shard_map/weight_sums/pallas_call | solution.py:168
  652.0 6.5 collective-permute-done.71.refs_4_
  661.6 10.0 %weight_sums.5 = (bf16[1024,2048]{1,0:T(8,128)(2,1)S(1)}, bf16[1024,2048]{1,0:T(8,128)(2,1)S(1)}) custom-call(s32[3]{0:T(128)S(1)} %add_add_fusion.3.flag_ref, bf16[256,2048]{1,0:T(8,128)(2,1)S(1)} %copy-done.124, bf16[256,2048]{1,0:T(8,128)(2,1)S(1)} %copy-done.130, bf16[256,2048]{1,0:T(8,128)(2,1)S(1)} %copy-done.132, bf16[256,2048]{1,0:T(8,128)(2,1)S(1)} %copy-done.212, ...), custom_call_target="tpu_custom_call" | custom-call | flops 18400000000 | tf_op jit(solution)/shard_map/weight_sums/pallas_call | solution.py:168
  686.9 34.0 %collective-permute-done.80.refs_9_ = f32[4,512]{1,0:T(4,128)S(1)} collective-permute-done((f32[4,512]{1,0:T(4,128)S(1)}, f32[4,512]{1,0:T(4,128)S(1)}, u32[]{:S(2)}, u32[]{:S(2)}) %collective-permute-start.80) | collective-permute-done | bytes 8224 | tf_op jit(solution)/shard_map/ppermute | solution.py:868
  745.5 5.8 copy.113
  753.6 21.1 %collective-permute-done.82 = bf16[3,64,2048]{2,1,0:T(8,128)(2,1)} collective-permute-done((bf16[3,64,2048]{2,1,0:T(8,128)(2,1)}, bf16[3,64,2048]{2,1,0:T(8,128)(2,1)}, u32[]{:S(2)}, u32[]{:S(2)}) %collective-permute-start.82) | collective-permute-done | bytes 786464 | tf_op jit(solution)/shard_map/ppermute | solution.py:868
  (856 shorter events, 339.4 us)
Async XLA Ops:
  3.8 26.4 %collective-permute-start = (bf16[256,2048]{1,0:T(8,128)(2,1)}, bf16[256,2048]{1,0:T(8,128)(2,1)}, u32[]{:S(2)}, u32[]{:S(2)}) collective-permute-start(bf16[256,2048]{1,0:T(8,128)(2,1)} %get-tuple-element.473), channel_id=1, source_target_pairs={{0,8},{4,12},{8,0},{12,4},{16,24},{20,28},{24,16},{28,20},{1,9},{5... | collective-permute-start | bytes 3145736 | tf_op jit(solution)/shard_map/ppermute | solution.py:868
  30.2 72.2 %collective-permute-start.4 = (bf16[528,2048]{1,0:T(8,128)(2,1)S(1)}, bf16[528,2048]{1,0:T(8,128)(2,1)S(1)}, u32[]{:S(2)}, u32[]{:S(2)}) collective-permute-start(bf16[528,2048]{1,0:T(8,128)(2,1)S(1)} %get-tuple-element.221), channel_id=1, source_target_pairs={{0,8},{4,12},{8,0},{12,4},{16,24},{20,28},{24,16},{28,20},{1,9},{5... | collective-permute-start | bytes 6488072 | tf_op jit(solution)/shard_map/ppermute | solution.py:868
  32.0 68.9 %collective-permute-start.5 = (bf16[256,2048]{1,0:T(8,128)(2,1)S(1)}, bf16[256,2048]{1,0:T(8,128)(2,1)S(1)}, u32[]{:S(2)}, u32[]{:S(2)}) collective-permute-start(bf16[256,2048]{1,0:T(8,128)(2,1)S(1)} %get-tuple-element.222), channel_id=1, source_target_pairs={{0,8},{4,12},{8,0},{12,4},{16,24},{20,28},{24,16},{28,20},{1,9},{5... | collective-permute-start | bytes 3145736 | tf_op jit(solution)/shard_map/ppermute | solution.py:868
  32.3 70.4 %collective-permute-start.1 = (bf16[3,64,2048]{2,1,0:T(8,128)(2,1)S(1)}, bf16[3,64,2048]{2,1,0:T(8,128)(2,1)S(1)}, u32[]{:S(2)}, u32[]{:S(2)}) collective-permute-start(bf16[3,64,2048]{2,1,0:T(8,128)(2,1)S(1)} %get-tuple-element.220.refs_3_.refs_0_.refs_1_), channel_id=1, source_target_pairs={{0,2},{1,3},{2,0},{3,1},{16,18},{17,19},{18,16},{19,17},{4,6},{5,7... | collective-permute-start | bytes 2359304 | tf_op jit(solution)/shard_map/ppermute | solution.py:868
  35.1 67.6 %collective-permute-start.2 = (bf16[3,64,2048]{2,1,0:T(8,128)(2,1)S(1)}, bf16[3,64,2048]{2,1,0:T(8,128)(2,1)S(1)}, u32[]{:S(2)}, u32[]{:S(2)}) collective-permute-start(bf16[3,64,2048]{2,1,0:T(8,128)(2,1)S(1)} %get-tuple-element.220.refs_3_.refs_0_.refs_1_), channel_id=1, source_target_pairs={{0,1},{1,0},{2,3},{3,2},{16,17},{17,16},{18,19},{19,18},{4,5},{5,4... | collective-permute-start | bytes 2359304 | tf_op jit(solution)/shard_map/ppermute | solution.py:868
  36.7 66.0 %collective-permute-start.3 = (bf16[3,64,2048]{2,1,0:T(8,128)(2,1)S(1)}, bf16[3,64,2048]{2,1,0:T(8,128)(2,1)S(1)}, u32[]{:S(2)}, u32[]{:S(2)}) collective-permute-start(bf16[3,64,2048]{2,1,0:T(8,128)(2,1)S(1)} %get-tuple-element.220.refs_3_.refs_0_.refs_1_), channel_id=1, source_target_pairs={{0,3},{1,2},{2,1},{3,0},{16,19},{17,18},{18,17},{19,16},{4,7},{5,6... | collective-permute-start | bytes 2359304 | tf_op jit(solution)/shard_map/ppermute | solution.py:868
  105.9 74.8 %collective-permute-start.15 = (bf16[2048,512]{1,0:T(8,128)(2,1)}, bf16[2048,512]{1,0:T(8,128)(2,1)}, u32[]{:S(2)}, u32[]{:S(2)}) collective-permute-start(bf16[2048,512]{1,0:T(8,128)(2,1)} %bitcast.27.refs_2_.refs_9_.refs_1_.refs_6_), channel_id=1, source_target_pairs={{0,4},{4,0},{8,12},{12,8},{16,20},{20,16},{24,28},{28,24},{1,5},{5... | collective-permute-start | bytes 6291464 | tf_op jit(solution)/shard_map/ppermute | solution.py:868
  106.7 18.6 %collective-permute-start.9 = (bf16[512,2048]{1,0:T(8,128)(2,1)}, bf16[512,2048]{1,0:T(8,128)(2,1)S(1)}, u32[]{:S(2)}, u32[]{:S(2)}) collective-permute-start(bf16[512,2048]{1,0:T(8,128)(2,1)} %copy-done), channel_id=1, source_target_pairs={{0,4},{4,0},{8,12},{12,8},{16,20},{20,16},{24,28},{28,24},{1,5},{5... | collective-permute-start | bytes 6291464 | tf_op jit(solution)/shard_map/ppermute | solution.py:868
  125.3 22.0 %collective-permute-start.11 = (bf16[896,512]{1,0:T(8,128)(2,1)S(1)}, bf16[896,512]{1,0:T(8,128)(2,1)S(1)}, u32[]{:S(2)}, u32[]{:S(2)}) collective-permute-start(bf16[896,512]{1,0:T(8,128)(2,1)S(1)} %fence.36.refs_11_), channel_id=1, source_target_pairs={{0,8},{4,12},{8,0},{12,4},{16,24},{20,28},{24,16},{28,20},{1,9},{5... | collective-permute-start | bytes 2752520 | tf_op jit(solution)/shard_map/ppermute | solution.py:868
  147.3 20.2 %collective-permute-start.12 = (bf16[1,2,2,256,256]{4,3,2,1,0:T(8,128)(2,1)S(1)}, bf16[1,2,2,256,256]{4,3,2,1,0:T(8,128)(2,1)S(1)}, u32[]{:S(2)}, u32[]{:S(2)}) collective-permute-start(bf16[1,2,2,256,256]{4,3,2,1,0:T(8,128)(2,1)S(1)} %get-tuple-element.231.refs_5_.refs_1_.refs_8_), channel_id=1, source_target_pairs={{0,8},{4,12},{1,9},{5,13},{2,10},{6,14},{3,11},{7,15}} | collective-permute-start | bytes 1572872 | tf_op jit(solution)/shard_map/ppermute | solution.py:989
  150.7 24.2 %collective-permute-start.13 = (bf16[640,512]{1,0:T(8,128)(2,1)S(1)}, bf16[640,512]{1,0:T(8,128)(2,1)S(1)}, u32[]{:S(2)}, u32[]{:S(2)}) collective-permute-start(bf16[640,512]{1,0:T(8,128)(2,1)S(1)} %get-tuple-element.233), channel_id=1, source_target_pairs={{0,8},{4,12},{8,0},{12,4},{16,24},{20,28},{24,16},{28,20},{1,9},{5... | collective-permute-start | bytes 1966088 | tf_op jit(solution)/shard_map/ppermute | solution.py:868
  199.8 18.5 %collective-permute-start.19 = (bf16[2,2,2,256,256]{4,3,2,1,0:T(8,128)(2,1)S(1)}, bf16[2,2,2,256,256]{4,3,2,1,0:T(8,128)(2,1)S(1)}, u32[]{:S(2)}, u32[]{:S(2)}) collective-permute-start(bf16[2,2,2,256,256]{4,3,2,1,0:T(8,128)(2,1)S(1)} %get-tuple-element.246), channel_id=1, source_target_pairs={{0,4},{4,0},{8,12},{12,8},{1,5},{5,1},{9,13},{13,9},{2,6},{6,2},{1... | collective-permute-start | bytes 3145736 | tf_op jit(solution)/shard_map/ppermute | solution.py:868
  218.3 20.8 %collective-permute-start.21 = (bf16[1,2,2,256,256]{4,3,2,1,0:T(8,128)(2,1)S(1)}, bf16[1,2,2,256,256]{4,3,2,1,0:T(8,128)(2,1)S(1)}, u32[]{:S(2)}, u32[]{:S(2)}) collective-permute-start(bf16[1,2,2,256,256]{4,3,2,1,0:T(8,128)(2,1)S(1)} %get-tuple-element.250.refs_1_.refs_8_), channel_id=1, source_target_pairs={{0,8},{4,12},{1,9},{5,13},{2,10},{6,14},{3,11},{7,15}} | collective-permute-start | bytes 1572872 | tf_op jit(solution)/shard_map/ppermute | solution.py:989
  354.5 108.2 %collective-permute-start.49 = (bf16[128,2048]{1,0:T(8,128)(2,1)S(1)}, bf16[128,2048]{1,0:T(8,128)(2,1)S(1)}, u32[]{:S(2)}, u32[]{:S(2)}) collective-permute-start(bf16[128,2048]{1,0:T(8,128)(2,1)S(1)} %get-tuple-element.322), channel_id=1, source_target_pairs={{16,17},{17,16},{18,19},{19,18},{20,21},{21,20},{22,23},{23,22},{2... | collective-permute-start | bytes 1572872 | tf_op jit(solution)/shard_map/ppermute | solution.py:868
  355.4 107.3 %collective-permute-start.50 = (bf16[64,2048]{1,0:T(8,128)(2,1)S(1)}, bf16[64,2048]{1,0:T(8,128)(2,1)S(1)}, u32[]{:S(2)}, u32[]{:S(2)}) collective-permute-start(bf16[64,2048]{1,0:T(8,128)(2,1)S(1)} %get-tuple-element.323.refs_2_), channel_id=1, source_target_pairs={{16,0},{17,1},{18,2},{19,3},{20,4},{21,5},{22,6},{23,7},{24,8},{25... | collective-permute-start | bytes 786440 | tf_op jit(solution)/shard_map/ppermute | solution.py:961
  356.7 106.2 %collective-permute-start.51 = (bf16[1,2,2,256,256]{4,3,2,1,0:T(8,128)(2,1)S(1)}, bf16[1,2,2,256,256]{4,3,2,1,0:T(8,128)(2,1)S(1)}, u32[]{:S(2)}, u32[]{:S(2)}) collective-permute-start(bf16[1,2,2,256,256]{4,3,2,1,0:T(8,128)(2,1)S(1)} %get-tuple-element.324), channel_id=1, source_target_pairs={{24,16},{28,20},{25,17},{29,21},{26,18},{30,22},{27,19},{31,23}} | collective-permute-start | bytes 1572872 | tf_op jit(solution)/shard_map/ppermute | solution.py:989
  479.5 18.5 %collective-permute-start.55 = (bf16[128,2048]{1,0:T(8,128)(2,1)S(1)}, bf16[128,2048]{1,0:T(8,128)(2,1)S(1)}, u32[]{:S(2)}, u32[]{:S(2)}) collective-permute-start(bf16[128,2048]{1,0:T(8,128)(2,1)S(1)} %get-tuple-element.334), channel_id=1, source_target_pairs={{16,17},{17,16},{18,19},{19,18},{20,21},{21,20},{22,23},{23,22},{2... | collective-permute-start | bytes 1572872 | tf_op jit(solution)/shard_map/ppermute | solution.py:868
  549.8 19.1 %collective-permute-start.65 = (bf16[2,2,2,256,256]{4,3,2,1,0:T(8,128)(2,1)S(1)}, bf16[2,2,2,256,256]{4,3,2,1,0:T(8,128)(2,1)S(1)}, u32[]{:S(2)}, u32[]{:S(2)}) collective-permute-start(bf16[2,2,2,256,256]{4,3,2,1,0:T(8,128)(2,1)S(1)} %get-tuple-element.361), channel_id=1, source_target_pairs={{0,4},{4,0},{8,12},{12,8},{1,5},{5,1},{9,13},{13,9},{2,6},{6,2},{1... | collective-permute-start | bytes 3145736 | tf_op jit(solution)/shard_map/ppermute | solution.py:868
  551.7 18.4 %collective-permute-start.64 = (bf16[128,2048]{1,0:T(8,128)(2,1)S(1)}, bf16[128,2048]{1,0:T(8,128)(2,1)S(1)}, u32[]{:S(2)}, u32[]{:S(2)}) collective-permute-start(bf16[128,2048]{1,0:T(8,128)(2,1)S(1)} %get-tuple-element.357.refs_12_), channel_id=1, source_target_pairs={{0,1},{1,0},{2,3},{3,2},{4,5},{5,4},{6,7},{7,6},{8,9},{9,8},{10,11... | collective-permute-start | bytes 1572872 | tf_op jit(solution)/shard_map/ppermute | solution.py:868
  602.4 20.4 %collective-permute-start.70 = (bf16[768,512]{1,0:T(8,128)(2,1)S(1)}, bf16[768,512]{1,0:T(8,128)(2,1)S(1)}, u32[]{:S(2)}, u32[]{:S(2)}) collective-permute-start(bf16[768,512]{1,0:T(8,128)(2,1)S(1)} %get-tuple-element.376.refs_12_), channel_id=1, source_target_pairs={{0,8},{4,12},{8,0},{12,4},{16,24},{20,28},{24,16},{28,20},{1,9},{5... | collective-permute-start | bytes 2359304 | tf_op jit(solution)/shard_map/ppermute | solution.py:868
  605.2 28.4 %collective-permute-start.69 = (bf16[1,2,2,256,256]{4,3,2,1,0:T(8,128)(2,1)S(1)}, bf16[1,2,2,256,256]{4,3,2,1,0:T(8,128)(2,1)S(1)}, u32[]{:S(2)}, u32[]{:S(2)}) collective-permute-start(bf16[1,2,2,256,256]{4,3,2,1,0:T(8,128)(2,1)S(1)} %get-tuple-element.475), channel_id=1, source_target_pairs={{8,0},{12,4},{9,1},{13,5},{10,2},{14,6},{11,3},{15,7}} | collective-permute-start | bytes 1572872 | tf_op jit(solution)/shard_map/ppermute | solution.py:989
  633.7 24.8 %collective-permute-start.71 = (bf16[1024,512]{1,0:T(8,128)(2,1)S(1)}, bf16[1024,512]{1,0:T(8,128)(2,1)S(1)}, u32[]{:S(2)}, u32[]{:S(2)}) collective-permute-start(bf16[1024,512]{1,0:T(8,128)(2,1)S(1)} %fence.64.refs_11_), channel_id=1, source_target_pairs={{0,8},{4,12},{8,0},{12,4},{16,24},{20,28},{24,16},{28,20},{1,9},{5... | collective-permute-start | bytes 3145736 | tf_op jit(solution)/shard_map/ppermute | solution.py:868
  658.6 20.2 %collective-permute-start.72 = (bf16[1024,1536]{1,0:T(8,128)(2,1)}, bf16[1024,1536]{1,0:T(8,128)(2,1)}, u32[]{:S(2)}, u32[]{:S(2)}) collective-permute-start(bf16[1024,1536]{1,0:T(8,128)(2,1)} %get-tuple-element.405), channel_id=1, source_target_pairs={{0,4},{4,0},{8,12},{12,8},{16,20},{20,16},{24,28},{28,24},{1,5},{5... | collective-permute-start | bytes 9437192 | tf_op jit(solution)/shard_map/ppermute | solution.py:868
  659.1 19.7 %collective-permute-start.73 = (bf16[768,512]{1,0:T(8,128)(2,1)S(1)}, bf16[768,512]{1,0:T(8,128)(2,1)S(1)}, u32[]{:S(2)}, u32[]{:S(2)}) collective-permute-start(bf16[768,512]{1,0:T(8,128)(2,1)S(1)} %get-tuple-element.406), channel_id=1, source_target_pairs={{0,8},{4,12},{8,0},{12,4},{16,24},{20,28},{24,16},{28,20},{1,9},{5... | collective-permute-start | bytes 2359304 | tf_op jit(solution)/shard_map/ppermute | solution.py:868
  681.2 44.5 %collective-permute-start.77 = (bf16[1024,2048]{1,0:T(8,128)(2,1)S(1)}, bf16[1024,2048]{1,0:T(8,128)(2,1)S(1)}, u32[]{:S(2)}, u32[]{:S(2)}) collective-permute-start(bf16[1024,2048]{1,0:T(8,128)(2,1)S(1)} %get-tuple-element.417), channel_id=1, source_target_pairs={{0,4},{4,0},{8,12},{12,8},{16,20},{20,16},{24,28},{28,24},{1,5},{5... | collective-permute-start | bytes 12582920 | tf_op jit(solution)/shard_map/ppermute | solution.py:868
  681.3 39.6 %collective-permute-start.76 = (bf16[3,128,2048]{2,1,0:T(8,128)(2,1)S(1)}, bf16[3,128,2048]{2,1,0:T(8,128)(2,1)S(1)}, u32[]{:S(2)}, u32[]{:S(2)}) collective-permute-start(bf16[3,128,2048]{2,1,0:T(8,128)(2,1)S(1)} %get-tuple-element.416), channel_id=1, source_target_pairs={{16,17},{17,16},{18,19},{19,18},{20,21},{21,20},{22,23},{23,22},{2... | collective-permute-start | bytes 4718600 | tf_op jit(solution)/shard_map/ppermute | solution.py:868
  682.2 39.5 %collective-permute-start.79 = (bf16[3,128,2048]{2,1,0:T(8,128)(2,1)S(1)}, bf16[3,128,2048]{2,1,0:T(8,128)(2,1)S(1)}, u32[]{:S(2)}, u32[]{:S(2)}) collective-permute-start(bf16[3,128,2048]{2,1,0:T(8,128)(2,1)S(1)} %get-tuple-element.420), channel_id=1, source_target_pairs={{0,1},{1,0},{2,3},{3,2},{4,5},{5,4},{6,7},{7,6},{8,9},{9,8},{10,11... | collective-permute-start | bytes 4718600 | tf_op jit(solution)/shard_map/ppermute | solution.py:868
  684.6 40.5 %collective-permute-start.78 = (bf16[512,1536]{1,0:T(8,128)(2,1)S(1)}, bf16[512,1536]{1,0:T(8,128)(2,1)S(1)}, u32[]{:S(2)}, u32[]{:S(2)}) collective-permute-start(bf16[512,1536]{1,0:T(8,128)(2,1)S(1)} %get-tuple-element.419), channel_id=1, source_target_pairs={{0,8},{4,12},{8,0},{12,4},{16,24},{20,28},{24,16},{28,20},{1,9},{5... | collective-permute-start | bytes 4718600 | tf_op jit(solution)/shard_map/ppermute | solution.py:868
  685.3 35.6 %collective-permute-start.80 = (f32[4,512]{1,0:T(4,128)S(1)}, f32[4,512]{1,0:T(4,128)S(1)}, u32[]{:S(2)}, u32[]{:S(2)}) collective-permute-start(f32[4,512]{1,0:T(4,128)S(1)} %get-tuple-element.418.refs_4_), channel_id=1, source_target_pairs={{0,1},{1,0},{2,3},{3,2},{16,17},{17,16},{18,19},{19,18},{4,5},{5,4... | collective-permute-start | bytes 24584 | tf_op jit(solution)/shard_map/ppermute | solution.py:868
  736.0 48.2 %collective-permute-start.83 = (bf16[512,2048]{1,0:T(8,128)(2,1)}, bf16[512,2048]{1,0:T(8,128)(2,1)}, u32[]{:S(2)}, u32[]{:S(2)}) collective-permute-start(bf16[512,2048]{1,0:T(8,128)(2,1)} %get-tuple-element.430), channel_id=1, source_target_pairs={{0,8},{4,12},{8,0},{12,4},{16,24},{20,28},{24,16},{28,20},{1,9},{5... | collective-permute-start | bytes 6291464 | tf_op jit(solution)/shard_map/ppermute | solution.py:868
  736.3 38.4 %collective-permute-start.82 = (bf16[3,64,2048]{2,1,0:T(8,128)(2,1)}, bf16[3,64,2048]{2,1,0:T(8,128)(2,1)}, u32[]{:S(2)}, u32[]{:S(2)}) collective-permute-start(bf16[3,64,2048]{2,1,0:T(8,128)(2,1)} %get-tuple-element.427), channel_id=1, source_target_pairs={{0,2},{1,3},{2,0},{3,1},{4,6},{5,7},{6,4},{7,5},{8,10},{9,11},{10,... | collective-permute-start | bytes 2359304 | tf_op jit(solution)/shard_map/ppermute | solution.py:868
  751.3 25.4 %collective-permute-start.81 = (bf16[3,64,2048]{2,1,0:T(8,128)(2,1)S(1)}, bf16[3,64,2048]{2,1,0:T(8,128)(2,1)S(1)}, u32[]{:S(2)}, u32[]{:S(2)}) collective-permute-start(bf16[3,64,2048]{2,1,0:T(8,128)(2,1)S(1)} %get-tuple-element.426), channel_id=1, source_target_pairs={{16,18},{17,19},{18,16},{19,17},{20,22},{21,23},{22,20},{23,21},{2... | collective-permute-start | bytes 2359304 | tf_op jit(solution)/shard_map/ppermute | solution.py:868
  (292 other events, 3310.2 us)

commit v4 on v3

--- a/solution.py
+++ b/solution.py
@@ -173,7 +173,7 @@
         out_shape=[struct for struct, _ in outs],
         scratch_shapes=scratch,
         compiler_params=pltpu.CompilerParams(
-            vmem_limit_bytes=int(held + (work + 2) * mebibyte)
+            vmem_limit_bytes=int(held + (work + 1) * mebibyte)
         ),
         cost_estimate=pl.CostEstimate(
             flops=int(took[name] * peak), bytes_accessed=0, transcendentals=0
@@ -1439,7 +1439,6 @@
             last_far(finals, 1),
             (side.all, side_far),
             held_back(triple_sums, 0),
-            held_back(branch_sums, 2),
         ]
     )
     triple_grads = wide_total(triple_sums.keep, triple_sums.parts)

time: 800 us -> 798 us (level)
  waiting for transfers between devices: 373 us -> 362 us
    ppermute x67, waiting for transfers between devices: 223 us -> 213 us  [hop(): return lax.ppermute(array, ('pipe', axis), pairs)]
    unnamed x488 -> x480, local copies, waits for them, and re-layouts: 55.5 us -> 54.6 us
  transfers between devices with their start and end apart: 85 -> 85, of which waited for: 34 -> 35; matrix products, arithmetic and copies ran while one was open for 8% -> 9% of each run, Pallas kernels for 20% -> 20%
where the time goes in v4:
time: 798 us; the launch traced here: 787 us
  waiting for transfers between devices  362 us (45%)
  Pallas kernels  169 us (21%)
  starting transfers between devices  124 us (16%)
  local copies, waits for them, and re-layouts  80.9 us (10%)
  other arithmetic  44.3 us (6%)
    ppermute x67, waiting for transfers between devices, hop(): return lax.ppermute(array, ('pipe', axis), pairs)  213 us
    pallas_call x40, Pallas kernels, run(): pl.pallas_call(body, grid=grid, in_specs=[spec for spec, _ in in_specs],...  169 us
    ppermute x6, waiting for transfers between devices, across(): return lax.ppermute(array, ('pipe', 'tp'), pairs)  135 us
    ppermute x67, starting transfers between devices, hop(): return lax.ppermute(array, ('pipe', axis), pairs)  93.6 us
    unnamed x480, local copies, waits for them, and re-layouts  54.6 us
    ppermute x12, starting transfers between devices, one_way(): return lax.ppermute(array, ('pipe', 'ctx'), pairs)  21.2 us
  transfers between devices with their start and end apart: 85, of which 35 were waited for; matrix products, arithmetic and copies ran while one was open for 9% of the time, Pallas kernels for 20%

profile of v4, /device:TPU:0, one launch (start us, length us, event | category | flops | bytes accessed | tf_op | source)
XLA Modules:
  0.0 786.8 jit_solution(2118644967077439838)
XLA Ops:
  37.8 63.2 %collective-permute-done.5.refs_5_ = bf16[256,2048]{1,0:T(8,128)(2,1)S(1)} collective-permute-done((bf16[256,2048]{1,0:T(8,128)(2,1)S(1)}, bf16[256,2048]{1,0:T(8,128)(2,1)S(1)}, u32[]{:S(2)}, u32[]{:S(2)}) %collective-permute-start.5) | collective-permute-done | bytes 1048608 | tf_op jit(solution)/shard_map/ppermute | solution.py:868
  116.0 9.3 %collective-permute-done.10.refs_8_ = bf16[512,512]{1,0:T(8,128)(2,1)S(1)} collective-permute-done((bf16[512,512]{1,0:T(8,128)(2,1)S(1)}, bf16[512,512]{1,0:T(8,128)(2,1)S(1)}, u32[]{:S(2)}, u32[]{:S(2)}) %collective-permute-start.10) | collective-permute-done | bytes 524320 | tf_op jit(solution)/shard_map/ppermute | solution.py:868
  133.6 5.6 project.7
  150.8 5.5 expand.3
  156.3 5.6 expand.4
  162.9 5.4 expand.5
  169.3 5.6 collective-permute-done.13.refs_4_
  190.9 5.8 branch.4
  205.4 12.7 %collective-permute-done.18.refs_3_ = bf16[128,2048]{1,0:T(8,128)(2,1)S(1)} collective-permute-done((bf16[128,2048]{1,0:T(8,128)(2,1)S(1)}, bf16[128,2048]{1,0:T(8,128)(2,1)S(1)}, u32[]{:S(2)}, u32[]{:S(2)}) %collective-permute-start.18) | collective-permute-done | bytes 524320 | tf_op jit(solution)/shard_map/ppermute | solution.py:868
  231.0 5.8 branch.5
  245.1 6.2 collective-permute-done.22.refs_3_
  251.3 6.1 collective-permute-done.23.refs_4_
  264.9 6.6 branch.6
  290.7 5.2 collective-permute-start.31
  297.3 10.2 %collective-permute-done.31.refs_5_ = bf16[64,2048]{1,0:T(8,128)(2,1)S(1)} collective-permute-done((bf16[64,2048]{1,0:T(8,128)(2,1)S(1)}, bf16[64,2048]{1,0:T(8,128)(2,1)S(1)}, u32[]{:S(2)}, u32[]{:S(2)}) %collective-permute-start.31) | collective-permute-done | bytes 262176 | tf_op jit(solution)/shard_map/ppermute | solution.py:868
  357.8 103.6 %collective-permute-done.50.refs_3_ = bf16[64,2048]{1,0:T(8,128)(2,1)S(1)} collective-permute-done((bf16[64,2048]{1,0:T(8,128)(2,1)S(1)}, bf16[64,2048]{1,0:T(8,128)(2,1)S(1)}, u32[]{:S(2)}, u32[]{:S(2)}) %collective-permute-start.50) | collective-permute-done | bytes 262176 | tf_op jit(solution)/shard_map/ppermute | solution.py:961
  467.4 10.4 %collective-permute-done.52.refs_5_ = bf16[64,2048]{1,0:T(8,128)(2,1)S(1)} collective-permute-done((bf16[64,2048]{1,0:T(8,128)(2,1)S(1)}, bf16[64,2048]{1,0:T(8,128)(2,1)S(1)}, u32[]{:S(2)}, u32[]{:S(2)}) %collective-permute-start.52) | collective-permute-done | bytes 262176 | tf_op jit(solution)/shard_map/ppermute | solution.py:868
  482.4 14.3 %collective-permute-done.56.refs_4_ = bf16[64,2048]{1,0:T(8,128)(2,1)S(1)} collective-permute-done((bf16[64,2048]{1,0:T(8,128)(2,1)S(1)}, bf16[64,2048]{1,0:T(8,128)(2,1)S(1)}, u32[]{:S(2)}, u32[]{:S(2)}) %collective-permute-start.56) | collective-permute-done | bytes 262176 | tf_op jit(solution)/shard_map/ppermute | solution.py:961
  501.6 5.3 attend_back.3
  517.9 8.5 %hidden_back.3 = (bf16[256,2048]{1,0:T(8,128)(2,1)S(1)}, f32[256,2048]{1,0:T(8,128)S(1)}, f32[2,2048]{1,0:T(2,128)S(1)}) custom-call(s32[3]{0:T(128)S(1)} %add_add_fusion.1.flag_ref, bf16[256,2048]{1,0:T(8,128)(2,1)S(1)} %get-tuple-element.336.refs_0_.refs_6_, bf16[2048,512]{1,0:T(8,128)(2,1)} %bitcast.27.refs_2_.refs_9_.refs_1_.refs_6_, ...), custom_call_target="tpu_custom_call" | custom-call | flops 14949999616 | tf_op jit(solution)/shard_map/hidden_back/pallas_call | solution.py:168
  539.7 7.5 collective-permute-done.62.refs_3_.refs_9_
  553.9 8.3 %hidden_back.4 = (bf16[256,2048]{1,0:T(8,128)(2,1)S(1)}, f32[256,2048]{1,0:T(8,128)S(1)}, f32[2,2048]{1,0:T(2,128)S(1)}) custom-call(s32[3]{0:T(128)S(1)} %add_add_fusion.1.flag_ref, bf16[256,2048]{1,0:T(8,128)(2,1)S(1)} %get-tuple-element.350.refs_0_.refs_7_, bf16[2048,512]{1,0:T(8,128)(2,1)} %bitcast.27.refs_2_.refs_9_.refs_1_.refs_6_, ...), custom_call_target="tpu_custom_call" | custom-call | flops 14949999616 | tf_op jit(solution)/shard_map/hidden_back/pallas_call | solution.py:168
  572.1 13.5 %weight_sums.3 = (bf16[2560,1024]{1,0:T(8,128)(2,1)S(1)}, bf16[2560,1024]{1,0:T(8,128)(2,1)S(1)}) custom-call(s32[3]{0:T(128)S(1)} %add_add_fusion.3.flag_ref, bf16[256,2048]{1,0:T(8,128)(2,1)S(1)} %copy-done.117, bf16[256,2048]{1,0:T(8,128)(2,1)S(1)} %copy-done.120, bf16[256,2048]{1,0:T(8,128)(2,1)S(1)} %copy-done.53, bf16[256,512]{1,0:T(8,128)(2,1)S(1)} %copy-done.187, ...), custom_call_target="tpu_custom_call" | custom-call | flops 18400000000 | tf_op jit(solution)/shard_map/weight_sums/pallas_call | solution.py:168
  607.7 8.8 %hidden_back.5 = (bf16[256,2048]{1,0:T(8,128)(2,1)S(1)}, f32[256,2048]{1,0:T(8,128)S(1)}, f32[2,2048]{1,0:T(2,128)S(1)}) custom-call(s32[3]{0:T(128)S(1)} %add_add_fusion.1.flag_ref, bf16[256,2048]{1,0:T(8,128)(2,1)S(1)} %get-tuple-element.366.refs_0_, bf16[2048,512]{1,0:T(8,128)(2,1)} %bitcast.27.refs_2_.refs_9_.refs_1_.refs_6_, ...), custom_call_target="tpu_custom_call" | custom-call | flops 14949999616 | tf_op jit(solution)/shard_map/hidden_back/pallas_call | solution.py:168
  617.5 6.3 collective-permute-done.70.refs_2_
  623.8 10.9 %collective-permute-done.69.refs_3_ = bf16[1,2,2,256,256]{4,3,2,1,0:T(8,128)(2,1)S(1)} collective-permute-done((bf16[1,2,2,256,256]{4,3,2,1,0:T(8,128)(2,1)S(1)}, bf16[1,2,2,256,256]{4,3,2,1,0:T(8,128)(2,1)S(1)}, u32[]{:S(2)}, u32[]{:S(2)}) %collective-permute-start.69) | collective-permute-done | bytes 524320 | tf_op jit(solution)/shard_map/ppermute | solution.py:989
  642.9 8.9 %weight_sums.4 = (bf16[1024,1536]{1,0:T(8,128)(2,1)S(1)}, bf16[1024,1536]{1,0:T(8,128)(2,1)S(1)}) custom-call(s32[3]{0:T(128)S(1)} %add_add_fusion.3.flag_ref, bf16[256,2048]{1,0:T(8,128)(2,1)S(1)} %copy-done.124, bf16[256,2048]{1,0:T(8,128)(2,1)S(1)} %copy-done.132, bf16[256,2048]{1,0:T(8,128)(2,1)S(1)} %copy-done.134, bf16[256,1536]{1,0:T(8,128)(2,1)S(1)} %copy-done.183, ...), custom_call_target="tpu_custom_call" | custom-call | flops 18400000000 | tf_op jit(solution)/shard_map/weight_sums/pallas_call | solution.py:168
  651.9 7.7 collective-permute-done.71.refs_4_
  662.7 10.0 %weight_sums.5 = (bf16[1024,2048]{1,0:T(8,128)(2,1)S(1)}, bf16[1024,2048]{1,0:T(8,128)(2,1)S(1)}) custom-call(s32[3]{0:T(128)S(1)} %add_add_fusion.3.flag_ref, bf16[256,2048]{1,0:T(8,128)(2,1)S(1)} %copy-done.122, bf16[256,2048]{1,0:T(8,128)(2,1)S(1)} %copy-done.128, bf16[256,2048]{1,0:T(8,128)(2,1)S(1)} %copy-done.130, bf16[256,2048]{1,0:T(8,128)(2,1)S(1)} %copy-done.208, ...), custom_call_target="tpu_custom_call" | custom-call | flops 18400000000 | tf_op jit(solution)/shard_map/weight_sums/pallas_call | solution.py:168
  700.0 22.3 %collective-permute-done.80.refs_9_ = f32[4,512]{1,0:T(4,128)S(1)} collective-permute-done((f32[4,512]{1,0:T(4,128)S(1)}, f32[4,512]{1,0:T(4,128)S(1)}, u32[]{:S(2)}, u32[]{:S(2)}) %collective-permute-start.80) | collective-permute-done | bytes 8224 | tf_op jit(solution)/shard_map/ppermute | solution.py:868
  743.8 5.8 copy.112
  751.9 19.9 %collective-permute-done.82 = bf16[3,64,2048]{2,1,0:T(8,128)(2,1)} collective-permute-done((bf16[3,64,2048]{2,1,0:T(8,128)(2,1)}, bf16[3,64,2048]{2,1,0:T(8,128)(2,1)}, u32[]{:S(2)}, u32[]{:S(2)}) %collective-permute-start.82) | collective-permute-done | bytes 786464 | tf_op jit(solution)/shard_map/ppermute | solution.py:868
  (848 shorter events, 350.9 us)
Async XLA Ops:
  3.8 26.4 %collective-permute-start = (bf16[256,2048]{1,0:T(8,128)(2,1)}, bf16[256,2048]{1,0:T(8,128)(2,1)}, u32[]{:S(2)}, u32[]{:S(2)}) collective-permute-start(bf16[256,2048]{1,0:T(8,128)(2,1)} %get-tuple-element.471), channel_id=1, source_target_pairs={{0,8},{4,12},{8,0},{12,4},{16,24},{20,28},{24,16},{28,20},{1,9},{5... | collective-permute-start | bytes 3145736 | tf_op jit(solution)/shard_map/ppermute | solution.py:868
  30.2 72.2 %collective-permute-start.4 = (bf16[528,2048]{1,0:T(8,128)(2,1)S(1)}, bf16[528,2048]{1,0:T(8,128)(2,1)S(1)}, u32[]{:S(2)}, u32[]{:S(2)}) collective-permute-start(bf16[528,2048]{1,0:T(8,128)(2,1)S(1)} %get-tuple-element.220), channel_id=1, source_target_pairs={{0,8},{4,12},{8,0},{12,4},{16,24},{20,28},{24,16},{28,20},{1,9},{5... | collective-permute-start | bytes 6488072 | tf_op jit(solution)/shard_map/ppermute | solution.py:868
  32.0 68.9 %collective-permute-start.5 = (bf16[256,2048]{1,0:T(8,128)(2,1)S(1)}, bf16[256,2048]{1,0:T(8,128)(2,1)S(1)}, u32[]{:S(2)}, u32[]{:S(2)}) collective-permute-start(bf16[256,2048]{1,0:T(8,128)(2,1)S(1)} %get-tuple-element.221), channel_id=1, source_target_pairs={{0,8},{4,12},{8,0},{12,4},{16,24},{20,28},{24,16},{28,20},{1,9},{5... | collective-permute-start | bytes 3145736 | tf_op jit(solution)/shard_map/ppermute | solution.py:868
  32.3 70.4 %collective-permute-start.1 = (bf16[3,64,2048]{2,1,0:T(8,128)(2,1)S(1)}, bf16[3,64,2048]{2,1,0:T(8,128)(2,1)S(1)}, u32[]{:S(2)}, u32[]{:S(2)}) collective-permute-start(bf16[3,64,2048]{2,1,0:T(8,128)(2,1)S(1)} %get-tuple-element.219.refs_3_.refs_0_.refs_1_), channel_id=1, source_target_pairs={{0,2},{1,3},{2,0},{3,1},{16,18},{17,19},{18,16},{19,17},{4,6},{5,7... | collective-permute-start | bytes 2359304 | tf_op jit(solution)/shard_map/ppermute | solution.py:868
  35.1 67.6 %collective-permute-start.2 = (bf16[3,64,2048]{2,1,0:T(8,128)(2,1)S(1)}, bf16[3,64,2048]{2,1,0:T(8,128)(2,1)S(1)}, u32[]{:S(2)}, u32[]{:S(2)}) collective-permute-start(bf16[3,64,2048]{2,1,0:T(8,128)(2,1)S(1)} %get-tuple-element.219.refs_3_.refs_0_.refs_1_), channel_id=1, source_target_pairs={{0,1},{1,0},{2,3},{3,2},{16,17},{17,16},{18,19},{19,18},{4,5},{5,4... | collective-permute-start | bytes 2359304 | tf_op jit(solution)/shard_map/ppermute | solution.py:868
  36.7 66.0 %collective-permute-start.3 = (bf16[3,64,2048]{2,1,0:T(8,128)(2,1)S(1)}, bf16[3,64,2048]{2,1,0:T(8,128)(2,1)S(1)}, u32[]{:S(2)}, u32[]{:S(2)}) collective-permute-start(bf16[3,64,2048]{2,1,0:T(8,128)(2,1)S(1)} %get-tuple-element.219.refs_3_.refs_0_.refs_1_), channel_id=1, source_target_pairs={{0,3},{1,2},{2,1},{3,0},{16,19},{17,18},{18,17},{19,16},{4,7},{5,6... | collective-permute-start | bytes 2359304 | tf_op jit(solution)/shard_map/ppermute | solution.py:868
  105.9 74.8 %collective-permute-start.15 = (bf16[2048,512]{1,0:T(8,128)(2,1)}, bf16[2048,512]{1,0:T(8,128)(2,1)}, u32[]{:S(2)}, u32[]{:S(2)}) collective-permute-start(bf16[2048,512]{1,0:T(8,128)(2,1)} %bitcast.27.refs_2_.refs_9_.refs_1_.refs_6_), channel_id=1, source_target_pairs={{0,4},{4,0},{8,12},{12,8},{16,20},{20,16},{24,28},{28,24},{1,5},{5... | collective-permute-start | bytes 6291464 | tf_op jit(solution)/shard_map/ppermute | solution.py:868
  106.7 18.6 %collective-permute-start.9 = (bf16[512,2048]{1,0:T(8,128)(2,1)}, bf16[512,2048]{1,0:T(8,128)(2,1)S(1)}, u32[]{:S(2)}, u32[]{:S(2)}) collective-permute-start(bf16[512,2048]{1,0:T(8,128)(2,1)} %copy-done), channel_id=1, source_target_pairs={{0,4},{4,0},{8,12},{12,8},{16,20},{20,16},{24,28},{28,24},{1,5},{5... | collective-permute-start | bytes 6291464 | tf_op jit(solution)/shard_map/ppermute | solution.py:868
  125.3 22.0 %collective-permute-start.11 = (bf16[896,512]{1,0:T(8,128)(2,1)S(1)}, bf16[896,512]{1,0:T(8,128)(2,1)S(1)}, u32[]{:S(2)}, u32[]{:S(2)}) collective-permute-start(bf16[896,512]{1,0:T(8,128)(2,1)S(1)} %fence.36.refs_11_), channel_id=1, source_target_pairs={{0,8},{4,12},{8,0},{12,4},{16,24},{20,28},{24,16},{28,20},{1,9},{5... | collective-permute-start | bytes 2752520 | tf_op jit(solution)/shard_map/ppermute | solution.py:868
  147.3 21.0 %collective-permute-start.12 = (bf16[1,2,2,256,256]{4,3,2,1,0:T(8,128)(2,1)S(1)}, bf16[1,2,2,256,256]{4,3,2,1,0:T(8,128)(2,1)S(1)}, u32[]{:S(2)}, u32[]{:S(2)}) collective-permute-start(bf16[1,2,2,256,256]{4,3,2,1,0:T(8,128)(2,1)S(1)} %get-tuple-element.230.refs_5_.refs_1_.refs_8_), channel_id=1, source_target_pairs={{0,8},{4,12},{1,9},{5,13},{2,10},{6,14},{3,11},{7,15}} | collective-permute-start | bytes 1572872 | tf_op jit(solution)/shard_map/ppermute | solution.py:989
  150.7 24.2 %collective-permute-start.13 = (bf16[640,512]{1,0:T(8,128)(2,1)S(1)}, bf16[640,512]{1,0:T(8,128)(2,1)S(1)}, u32[]{:S(2)}, u32[]{:S(2)}) collective-permute-start(bf16[640,512]{1,0:T(8,128)(2,1)S(1)} %get-tuple-element.232), channel_id=1, source_target_pairs={{0,8},{4,12},{8,0},{12,4},{16,24},{20,28},{24,16},{28,20},{1,9},{5... | collective-permute-start | bytes 1966088 | tf_op jit(solution)/shard_map/ppermute | solution.py:868
  199.8 18.5 %collective-permute-start.19 = (bf16[2,2,2,256,256]{4,3,2,1,0:T(8,128)(2,1)S(1)}, bf16[2,2,2,256,256]{4,3,2,1,0:T(8,128)(2,1)S(1)}, u32[]{:S(2)}, u32[]{:S(2)}) collective-permute-start(bf16[2,2,2,256,256]{4,3,2,1,0:T(8,128)(2,1)S(1)} %get-tuple-element.245), channel_id=1, source_target_pairs={{0,4},{4,0},{8,12},{12,8},{1,5},{5,1},{9,13},{13,9},{2,6},{6,2},{1... | collective-permute-start | bytes 3145736 | tf_op jit(solution)/shard_map/ppermute | solution.py:868
  218.3 20.8 %collective-permute-start.21 = (bf16[1,2,2,256,256]{4,3,2,1,0:T(8,128)(2,1)S(1)}, bf16[1,2,2,256,256]{4,3,2,1,0:T(8,128)(2,1)S(1)}, u32[]{:S(2)}, u32[]{:S(2)}) collective-permute-start(bf16[1,2,2,256,256]{4,3,2,1,0:T(8,128)(2,1)S(1)} %get-tuple-element.249.refs_1_.refs_8_), channel_id=1, source_target_pairs={{0,8},{4,12},{1,9},{5,13},{2,10},{6,14},{3,11},{7,15}} | collective-permute-start | bytes 1572872 | tf_op jit(solution)/shard_map/ppermute | solution.py:989
  354.7 106.7 %collective-permute-start.49 = (bf16[128,2048]{1,0:T(8,128)(2,1)S(1)}, bf16[128,2048]{1,0:T(8,128)(2,1)S(1)}, u32[]{:S(2)}, u32[]{:S(2)}) collective-permute-start(bf16[128,2048]{1,0:T(8,128)(2,1)S(1)} %get-tuple-element.321), channel_id=1, source_target_pairs={{16,17},{17,16},{18,19},{19,18},{20,21},{21,20},{22,23},{23,22},{2... | collective-permute-start | bytes 1572872 | tf_op jit(solution)/shard_map/ppermute | solution.py:868
  355.6 105.7 %collective-permute-start.50 = (bf16[64,2048]{1,0:T(8,128)(2,1)S(1)}, bf16[64,2048]{1,0:T(8,128)(2,1)S(1)}, u32[]{:S(2)}, u32[]{:S(2)}) collective-permute-start(bf16[64,2048]{1,0:T(8,128)(2,1)S(1)} %get-tuple-element.322.refs_2_), channel_id=1, source_target_pairs={{16,0},{17,1},{18,2},{19,3},{20,4},{21,5},{22,6},{23,7},{24,8},{25... | collective-permute-start | bytes 786440 | tf_op jit(solution)/shard_map/ppermute | solution.py:961
  356.9 104.6 %collective-permute-start.51 = (bf16[1,2,2,256,256]{4,3,2,1,0:T(8,128)(2,1)S(1)}, bf16[1,2,2,256,256]{4,3,2,1,0:T(8,128)(2,1)S(1)}, u32[]{:S(2)}, u32[]{:S(2)}) collective-permute-start(bf16[1,2,2,256,256]{4,3,2,1,0:T(8,128)(2,1)S(1)} %get-tuple-element.323), channel_id=1, source_target_pairs={{24,16},{28,20},{25,17},{29,21},{26,18},{30,22},{27,19},{31,23}} | collective-permute-start | bytes 1572872 | tf_op jit(solution)/shard_map/ppermute | solution.py:989
  478.2 18.5 %collective-permute-start.55 = (bf16[128,2048]{1,0:T(8,128)(2,1)S(1)}, bf16[128,2048]{1,0:T(8,128)(2,1)S(1)}, u32[]{:S(2)}, u32[]{:S(2)}) collective-permute-start(bf16[128,2048]{1,0:T(8,128)(2,1)S(1)} %get-tuple-element.333), channel_id=1, source_target_pairs={{16,17},{17,16},{18,19},{19,18},{20,21},{21,20},{22,23},{23,22},{2... | collective-permute-start | bytes 1572872 | tf_op jit(solution)/shard_map/ppermute | solution.py:868
  548.5 19.7 %collective-permute-start.65 = (bf16[2,2,2,256,256]{4,3,2,1,0:T(8,128)(2,1)S(1)}, bf16[2,2,2,256,256]{4,3,2,1,0:T(8,128)(2,1)S(1)}, u32[]{:S(2)}, u32[]{:S(2)}) collective-permute-start(bf16[2,2,2,256,256]{4,3,2,1,0:T(8,128)(2,1)S(1)} %get-tuple-element.360), channel_id=1, source_target_pairs={{0,4},{4,0},{8,12},{12,8},{1,5},{5,1},{9,13},{13,9},{2,6},{6,2},{1... | collective-permute-start | bytes 3145736 | tf_op jit(solution)/shard_map/ppermute | solution.py:868
  550.5 18.9 %collective-permute-start.64 = (bf16[128,2048]{1,0:T(8,128)(2,1)S(1)}, bf16[128,2048]{1,0:T(8,128)(2,1)S(1)}, u32[]{:S(2)}, u32[]{:S(2)}) collective-permute-start(bf16[128,2048]{1,0:T(8,128)(2,1)S(1)} %get-tuple-element.356.refs_12_), channel_id=1, source_target_pairs={{0,1},{1,0},{2,3},{3,2},{4,5},{5,4},{6,7},{7,6},{8,9},{9,8},{10,11... | collective-permute-start | bytes 1572872 | tf_op jit(solution)/shard_map/ppermute | solution.py:868
  603.4 20.4 %collective-permute-start.70 = (bf16[768,512]{1,0:T(8,128)(2,1)S(1)}, bf16[768,512]{1,0:T(8,128)(2,1)S(1)}, u32[]{:S(2)}, u32[]{:S(2)}) collective-permute-start(bf16[768,512]{1,0:T(8,128)(2,1)S(1)} %get-tuple-element.375.refs_12_), channel_id=1, source_target_pairs={{0,8},{4,12},{8,0},{12,4},{16,24},{20,28},{24,16},{28,20},{1,9},{5... | collective-permute-start | bytes 2359304 | tf_op jit(solution)/shard_map/ppermute | solution.py:868
  606.3 28.4 %collective-permute-start.69 = (bf16[1,2,2,256,256]{4,3,2,1,0:T(8,128)(2,1)S(1)}, bf16[1,2,2,256,256]{4,3,2,1,0:T(8,128)(2,1)S(1)}, u32[]{:S(2)}, u32[]{:S(2)}) collective-permute-start(bf16[1,2,2,256,256]{4,3,2,1,0:T(8,128)(2,1)S(1)} %get-tuple-element.473), channel_id=1, source_target_pairs={{8,0},{12,4},{9,1},{13,5},{10,2},{14,6},{11,3},{15,7}} | collective-permute-start | bytes 1572872 | tf_op jit(solution)/shard_map/ppermute | solution.py:989
  634.7 24.8 %collective-permute-start.71 = (bf16[1024,512]{1,0:T(8,128)(2,1)S(1)}, bf16[1024,512]{1,0:T(8,128)(2,1)S(1)}, u32[]{:S(2)}, u32[]{:S(2)}) collective-permute-start(bf16[1024,512]{1,0:T(8,128)(2,1)S(1)} %fence.64.refs_11_), channel_id=1, source_target_pairs={{0,8},{4,12},{8,0},{12,4},{16,24},{20,28},{24,16},{28,20},{1,9},{5... | collective-permute-start | bytes 3145736 | tf_op jit(solution)/shard_map/ppermute | solution.py:868
  659.7 20.2 %collective-permute-start.72 = (bf16[1024,1536]{1,0:T(8,128)(2,1)S(1)}, bf16[1024,1536]{1,0:T(8,128)(2,1)}, u32[]{:S(2)}, u32[]{:S(2)}) collective-permute-start(bf16[1024,1536]{1,0:T(8,128)(2,1)S(1)} %get-tuple-element.404), channel_id=1, source_target_pairs={{0,4},{4,0},{8,12},{12,8},{16,20},{20,16},{24,28},{28,24},{1,5},{5... | collective-permute-start | bytes 9437192 | tf_op jit(solution)/shard_map/ppermute | solution.py:868
  660.2 19.7 %collective-permute-start.73 = (bf16[768,512]{1,0:T(8,128)(2,1)S(1)}, bf16[768,512]{1,0:T(8,128)(2,1)}, u32[]{:S(2)}, u32[]{:S(2)}) collective-permute-start(bf16[768,512]{1,0:T(8,128)(2,1)S(1)} %get-tuple-element.405), channel_id=1, source_target_pairs={{0,8},{4,12},{8,0},{12,4},{16,24},{20,28},{24,16},{28,20},{1,9},{5... | collective-permute-start | bytes 2359304 | tf_op jit(solution)/shard_map/ppermute | solution.py:868
  682.2 45.7 %collective-permute-start.77 = (bf16[1024,2048]{1,0:T(8,128)(2,1)S(1)}, bf16[1024,2048]{1,0:T(8,128)(2,1)}, u32[]{:S(2)}, u32[]{:S(2)}) collective-permute-start(bf16[1024,2048]{1,0:T(8,128)(2,1)S(1)} %get-tuple-element.416), channel_id=1, source_target_pairs={{0,4},{4,0},{8,12},{12,8},{16,20},{20,16},{24,28},{28,24},{1,5},{5... | collective-permute-start | bytes 12582920 | tf_op jit(solution)/shard_map/ppermute | solution.py:868
  683.7 38.6 %collective-permute-start.76 = (bf16[3,128,2048]{2,1,0:T(8,128)(2,1)S(1)}, bf16[3,128,2048]{2,1,0:T(8,128)(2,1)S(1)}, u32[]{:S(2)}, u32[]{:S(2)}) collective-permute-start(bf16[3,128,2048]{2,1,0:T(8,128)(2,1)S(1)} %get-tuple-element.415), channel_id=1, source_target_pairs={{16,17},{17,16},{18,19},{19,18},{20,21},{21,20},{22,23},{23,22},{2... | collective-permute-start | bytes 4718600 | tf_op jit(solution)/shard_map/ppermute | solution.py:868
  684.5 38.6 %collective-permute-start.79 = (bf16[3,128,2048]{2,1,0:T(8,128)(2,1)S(1)}, bf16[3,128,2048]{2,1,0:T(8,128)(2,1)S(1)}, u32[]{:S(2)}, u32[]{:S(2)}) collective-permute-start(bf16[3,128,2048]{2,1,0:T(8,128)(2,1)S(1)} %get-tuple-element.419), channel_id=1, source_target_pairs={{0,1},{1,0},{2,3},{3,2},{4,5},{5,4},{6,7},{7,6},{8,9},{9,8},{10,11... | collective-permute-start | bytes 4718600 | tf_op jit(solution)/shard_map/ppermute | solution.py:868
  691.2 31.1 %collective-permute-start.80 = (f32[4,512]{1,0:T(4,128)S(1)}, f32[4,512]{1,0:T(4,128)S(1)}, u32[]{:S(2)}, u32[]{:S(2)}) collective-permute-start(f32[4,512]{1,0:T(4,128)S(1)} %get-tuple-element.417.refs_4_), channel_id=1, source_target_pairs={{0,1},{1,0},{2,3},{3,2},{16,17},{17,16},{18,19},{19,18},{4,5},{5,4... | collective-permute-start | bytes 24584 | tf_op jit(solution)/shard_map/ppermute | solution.py:868
  692.8 35.2 %collective-permute-start.78 = (bf16[512,1536]{1,0:T(8,128)(2,1)S(1)}, bf16[512,1536]{1,0:T(8,128)(2,1)S(1)}, u32[]{:S(2)}, u32[]{:S(2)}) collective-permute-start(bf16[512,1536]{1,0:T(8,128)(2,1)S(1)} %get-tuple-element.418), channel_id=1, source_target_pairs={{0,8},{4,12},{8,0},{12,4},{16,24},{20,28},{24,16},{28,20},{1,9},{5... | collective-permute-start | bytes 4718600 | tf_op jit(solution)/shard_map/ppermute | solution.py:868
  734.3 47.1 %collective-permute-start.83 = (bf16[512,2048]{1,0:T(8,128)(2,1)}, bf16[512,2048]{1,0:T(8,128)(2,1)}, u32[]{:S(2)}, u32[]{:S(2)}) collective-permute-start(bf16[512,2048]{1,0:T(8,128)(2,1)} %get-tuple-element.428), channel_id=1, source_target_pairs={{0,8},{4,12},{8,0},{12,4},{16,24},{20,28},{24,16},{28,20},{1,9},{5... | collective-permute-start | bytes 6291464 | tf_op jit(solution)/shard_map/ppermute | solution.py:868
  734.6 37.3 %collective-permute-start.82 = (bf16[3,64,2048]{2,1,0:T(8,128)(2,1)}, bf16[3,64,2048]{2,1,0:T(8,128)(2,1)}, u32[]{:S(2)}, u32[]{:S(2)}) collective-permute-start(bf16[3,64,2048]{2,1,0:T(8,128)(2,1)} %get-tuple-element.426), channel_id=1, source_target_pairs={{0,2},{1,3},{2,0},{3,1},{4,6},{5,7},{6,4},{7,5},{8,10},{9,11},{10,... | collective-permute-start | bytes 2359304 | tf_op jit(solution)/shard_map/ppermute | solution.py:868
  749.6 24.2 %collective-permute-start.81 = (bf16[3,64,2048]{2,1,0:T(8,128)(2,1)S(1)}, bf16[3,64,2048]{2,1,0:T(8,128)(2,1)S(1)}, u32[]{:S(2)}, u32[]{:S(2)}) collective-permute-start(bf16[3,64,2048]{2,1,0:T(8,128)(2,1)S(1)} %get-tuple-element.425), channel_id=1, source_target_pairs={{16,18},{17,19},{18,16},{19,17},{20,22},{21,23},{22,20},{23,21},{2... | collective-permute-start | bytes 2359304 | tf_op jit(solution)/shard_map/ppermute | solution.py:868
  (288 other events, 3284.1 us)
